TPU v7x, 512 devices: a whole 4x8x8 slice. The times are simulated.
512 devices in a mesh: rep: 4 (over x), shard: 128 (over y, z, core).
Axes of the slice: x: 4, y: 8, z: 8, core: 2. Of those that a mesh axis runs over, the one named last changes fastest.
Arguments:
- partials: bfloat16 [4, 224, 512, 512], P('rep', None, 'shard'), may hold values from -0.41992188 to 0.41992188
- owners: int32 [224], replicated, may hold values from 0 to 127, as said below
- left_stat: bfloat16 [128, 4, 512, 512], P('shard', None, 'rep'), may hold values from -6 to 6
- right_stat: bfloat16 [128, 4, 512, 512], P('shard', None, 'rep'), may hold values from -6 to 6
- left_factor: bfloat16 [128, 4, 512, 512], P('shard', None, 'rep'), may hold values from -0.2 to 3.2
- right_factor: bfloat16 [128, 4, 512, 512], P('shard', None, None, 'rep'), may hold values from -0.2 to 3.2
Outputs:
- left_stat_new: bfloat16 [128, 4, 512, 512], P('shard', None, 'rep')
- right_stat_new: bfloat16 [128, 4, 512, 512], P('shard', None, 'rep')
- update: bfloat16 [224, 512, 512], P(None, 'shard', 'rep')
Inputs may be any that keep to these rules, and one draw needn't show every extreme that they name: `owners`: each owner holds at most 4 blocks, and some owner holds exactly 4.
All inputs are finite; a program needn't handle non-finite values.
Results may differ from a plain program's by a relative error of at most 0.017.
Values may be sent and summed in bfloat16 or wider, within the bound.
No kernel may reach another device: no remote copies, remote signals or barrier semaphores. Data moves between devices by JAX's collectives and lax.ppermute only.
A program may use at most 64 MiB of HBM per device.

v0:
```python
import jax
import jax.numpy as jnp
from jax import lax
from jax.sharding import PartitionSpec as P


def slot_numbers(owners, shard_count):
    count = owners.shape[0]
    same_owner = owners[:, None] == owners[None, :]
    before = lax.broadcasted_iota(jnp.int32, (count, count), 1) < lax.broadcasted_iota(
        jnp.int32, (count, count), 0
    )
    slot = jnp.sum(jnp.where(same_owner & before, 1, 0), axis=1).astype(jnp.int32)
    return slot * shard_count + owners


def per_device(partials, owners, left_stat, right_stat, left_factor, right_factor):
    shard_count = lax.axis_size("shard")
    replica_count = lax.axis_size("rep")
    replica = lax.axis_index("rep")
    local_part = partials[0]
    block_count, block_rows, width = local_part.shape
    capacity = left_stat.shape[1]
    quarter = width // replica_count
    flat_slot = slot_numbers(owners, shard_count)
    summed = lax.psum(local_part.astype(jnp.float32).astype(jnp.bfloat16), "rep")
    outgoing = (
        jnp.zeros((capacity * shard_count, block_rows, width), jnp.bfloat16)
        .at[flat_slot]
        .set(summed)
    )
    incoming = lax.all_to_all(
        outgoing.reshape(capacity, shard_count, block_rows, width),
        "shard",
        split_axis=1,
        concat_axis=1,
        tiled=True,
    )
    whole_grad = incoming.reshape(capacity, shard_count * block_rows, width)
    start = replica * quarter
    own_rows = lax.dynamic_slice_in_dim(whole_grad, start, quarter, 1)
    own_cols = lax.dynamic_slice_in_dim(whole_grad, start, quarter, 2)
    left_upd = jnp.einsum("kij,klj->kil", own_rows, whole_grad, preferred_element_type=jnp.float32)
    right_upd = jnp.einsum("kji,kjl->kil", own_cols, whole_grad, preferred_element_type=jnp.float32)
    left_new = (0.9 * left_stat[0].astype(jnp.float32) + 0.1 * left_upd).astype(jnp.bfloat16)
    right_new = (0.9 * right_stat[0].astype(jnp.float32) + 0.1 * right_upd).astype(jnp.bfloat16)
    own_product = jnp.einsum(
        "kij,kjl->kil", left_factor[0], whole_grad, preferred_element_type=jnp.float32
    ).astype(jnp.bfloat16)
    left_product = lax.all_gather(own_product, "rep", axis=1, tiled=True)
    update_cols = jnp.einsum(
        "kij,kjl->kil", left_product, right_factor[0], preferred_element_type=jnp.float32
    ).astype(jnp.bfloat16)
    returned = lax.all_to_all(
        update_cols.reshape(capacity, shard_count, block_rows, quarter),
        "shard",
        split_axis=1,
        concat_axis=1,
        tiled=True,
    )
    update = returned.reshape(capacity * shard_count, block_rows, quarter)[flat_slot]
    return (left_new[None], right_new[None], update)


def solution(mesh):
    return jax.shard_map(
        per_device,
        mesh=mesh,
        in_specs=(
            P("rep", None, "shard", None),
            P(),
            P("shard", None, "rep", None),
            P("shard", None, "rep", None),
            P("shard", None, "rep", None),
            P("shard", None, None, "rep"),
        ),
        out_specs=(
            P("shard", None, "rep", None),
            P("shard", None, "rep", None),
            P(None, "shard", "rep"),
        ),
        check_vma=False,
    )
```

profile of v0, /device:TPU:1, one launch (start us, length us, event | category | flops | bytes accessed | tf_op | source)
XLA Modules:
  0.0 234.2 jit_solution(5947192470959106725)
XLA Ops:
  7.2 0.0 copy-start
  7.2 0.0 all-reduce.2.cloned.1.call-start
  7.2 0.7 all-reduce.2.cloned.1.call-update
  7.9 0.0 all-gather.2.cloned.1.call-start
  8.0 0.9 select_reduce_fusion
  8.9 0.7 compare_select_fusion
  9.6 60.5 %all-reduce.2.cloned.1.call-done = bf16[224,4,512]{2,1,0:T(4,128)(2,1)} async-done(((bf16[224,4,512]{2,1,0:T(4,128)(2,1)}), bf16[224,4,512]{2,1,0:T(4,128)(2,1)}) %all-reduce.2.cloned.1.call-update) | async-done | bytes 917520 | tf_op jit(solution)/shard_map/psum | solution.py:26
  70.1 0.0 copy-start.1
  70.1 0.5 broadcast_in_dim.23
  70.6 0.6 copy-done.1
  71.3 7.1 %scatter_fusion = bf16[512,4,512]{2,1,0:T(4,128)(2,1)S(1)} fusion(bf16[512,4,512]{2,1,0:T(4,128)(2,1)S(1)} %broadcast_in_dim.23, s32[224]{0:T(256)S(1)} %compare_select_fusion, bf16[224,4,512]{2,1,0:T(4,128)(2,1)S(1)} %copy-done.1), kind=kCustom, calls=%fused_computation.1 | custom fusion | bytes 2753408 | tf_op jit(solution)/shard_map/scatter | solution.py:30
  78.4 1.2 copy.34
  79.6 67.9 %all_to_all.10 = bf16[4,128,4,512]{3,2,0,1:T(4,128)(2,1)S(1)} all-to-all(bf16[4,128,4,512]{3,2,0,1:T(4,128)(2,1)S(1)} %copy.34), channel_id=1, replica_groups=mesh['rep'=4,'shard'=128] {'shard'}, dimensions={1} | all-to-all | bytes 4194304 | tf_op jit(solution)/shard_map/all_to_all | solution.py:32
  147.5 2.0 copy.35
  149.5 2.5 %reshape.27 = bf16[4,512,512]{2,1,0:T(8,128)(2,1)S(1)} reshape(bf16[4,128,4,512]{3,2,1,0:T(4,128)(2,1)} %copy.35) | data formatting | bytes 4194304 | tf_op jit(solution)/shard_map/reshape | solution.py:39
  152.1 0.0 copy-done
  152.1 0.0 copy-start.2
  152.1 1.7 fusion.4
  153.9 0.0 all-gather.2.cloned.1.call-update
  153.9 33.6 %all-gather.2.cloned.1.call-done = bf16[4,512,512]{1,2,0:T(8,128)(2,1)} async-done(((bf16[4,128,512]{1,2,0:T(8,128)(2,1)}), bf16[4,512,512]{1,2,0:T(8,128)(2,1)}) %all-gather.2.cloned.1.call-update) | async-done | bytes 2097168 | tf_op jit(solution)/shard_map/all_gather | solution.py:50
  187.5 0.0 copy-done.2
  187.5 2.5 %convolution_convert_fusion = bf16[4,512,128]{2,1,0:T(8,128)(2,1)S(1)} fusion(bf16[4,512,512]{1,2,0:T(8,128)(2,1)} %all-gather.2.cloned.1.call-done, bf16[1,4,512,128]{3,2,1,0:T(8,128)(2,1)S(1)} %copy-done.2), kind=kOutput, calls=%fused_computation.8 | convolution fusion | flops 268697600 | bytes 3145728 | tf_op jit(solution)/shard_map/kij,kjl->kil/dot_general | solution.py:51
  190.0 1.0 copy.39
  190.9 15.2 %all-to-all-start.1 = ((bf16[4,128,4,128]{3,2,0,1:T(4,128)(2,1)}), bf16[4,128,4,128]{3,2,0,1:T(4,128)(2,1)S(1)}, u32[]{:S(2)}, u32[]{:S(2)}) async-start(bf16[4,128,4,128]{3,2,0,1:T(4,128)(2,1)} %copy.39), calls=%async_computation.1 | async-start | bytes 1048576 | tf_op jit(solution)/shard_map/all_to_all | solution.py:54
  206.1 0.0 copy-start.3
  206.1 2.4 %fusion.5 = bf16[1,4,128,512]{3,2,1,0:T(8,128)(2,1)} fusion(bf16[4,512,512]{2,1,0:T(8,128)(2,1)S(1)} %reshape.27, bf16[1,4,128,512]{3,2,1,0:T(8,128)(2,1)} %param.9, s32[]{:T(128)S(6)} %select_n.14), kind=kOutput, calls=%fused_computation.11 | convolution fusion | flops 269746176 | bytes 3670020 | tf_op jit(solution)/shard_map/kji,kjl->kil/dot_general | solution.py:44
  208.5 0.0 copy-done.3
  208.5 1.6 fusion.6
  210.1 15.4 %all-to-all-done.1 = bf16[4,128,4,128]{3,2,0,1:T(4,128)(2,1)S(1)} async-done(((bf16[4,128,4,128]{3,2,0,1:T(4,128)(2,1)}), bf16[4,128,4,128]{3,2,0,1:T(4,128)(2,1)S(1)}, u32[]{:S(2)}, u32[]{:S(2)}) %all-to-all-start.1) | async-done | bytes 524320 | tf_op jit(solution)/shard_map/all_to_all | solution.py:54
  225.6 0.2 copy.40
  225.7 1.6 gather_fusion
  (1 shorter events, 0.0 us)
Async XLA Ops:
  7.2 144.9 %copy-start = (bf16[1,4,128,512]{3,2,1,0:T(8,128)(2,1)S(1)}, bf16[1,4,128,512]{3,2,1,0:T(8,128)(2,1)}, u32[]{:S(2)}) copy-start(bf16[1,4,128,512]{3,2,1,0:T(8,128)(2,1)} %param.10) | copy-start | bytes 1572868
  7.2 62.9 %all-reduce.2.cloned.1.call-start = ((), (), s32[]{:S(2)}) async-start(), calls=%async_computation.2 | async-start | bytes 1835008 | tf_op jit(solution)/shard_map/psum | solution.py:26
  7.9 179.5 %all-gather.2.cloned.1.call-start = ((), (), s32[]{:S(2)}) async-start(), calls=%async_computation.3 | async-start | bytes 2621440 | tf_op jit(solution)/shard_map/all_gather | solution.py:50
  70.1 1.2 copy-start.1
  152.1 35.4 %copy-start.2 = (bf16[1,4,512,128]{3,2,1,0:T(8,128)(2,1)S(1)}, bf16[1,4,512,128]{3,2,1,0:T(8,128)(2,1)}, u32[]{:S(2)}) copy-start(bf16[1,4,512,128]{3,2,1,0:T(8,128)(2,1)} %param.11) | copy-start | bytes 1572868
  190.9 34.6 %all-to-all-start.1 = ((bf16[4,128,4,128]{3,2,0,1:T(4,128)(2,1)}), bf16[4,128,4,128]{3,2,0,1:T(4,128)(2,1)S(1)}, u32[]{:S(2)}, u32[]{:S(2)}) async-start(bf16[4,128,4,128]{3,2,0,1:T(4,128)(2,1)} %copy.39), calls=%async_computation.1 | async-start | bytes 1048576 | tf_op jit(solution)/shard_map/all_to_all | solution.py:54
  206.1 2.4 %copy-start.3 = (bf16[1,4,128,512]{3,2,1,0:T(8,128)(2,1)S(1)}, bf16[1,4,128,512]{3,2,1,0:T(8,128)(2,1)}, u32[]{:S(2)}) copy-start(bf16[1,4,128,512]{3,2,1,0:T(8,128)(2,1)} %param.8) | copy-start | bytes 1572868
Sparse Core Ops, SparseCore 0:
  10.4 59.6 all-reduce.1
  154.0 33.4 all-gather.1
where the time goes:
time: 235 us; the launch traced here: 234 us
  waiting for transfers between devices  110 us (47%)
  blocking collectives  67.9 us (29%)
  local copies, waits for them, and re-layouts  16.9 us (7%)
  starting transfers between devices  15.2 us (6%)
  between operations  14.1 us (6%)
  matrix products  8.24 us (4%)
    all_to_all x1, blocking collectives, per_device(): lax.all_to_all(outgoing.reshape(capacity, shard_count, block_rows, width)...  67.9 us
    psum x1, waiting for transfers between devices, per_device(): lax.psum(local_part.astype(jnp.float32).astype(jnp.bfloat16), 'rep')  60.5 us
    all_gather x1, waiting for transfers between devices, per_device(): left_product = lax.all_gather(own_product, 'rep', axis=1, tiled=True)  33.6 us
    all_to_all x1, waiting for transfers between devices, per_device(): lax.all_to_all(update_cols.reshape(capacity, shard_count, block_rows, qua...  15.4 us
    all_to_all x1, starting transfers between devices, per_device(): lax.all_to_all(update_cols.reshape(capacity, shard_count, block_rows, qua...  15.2 us
    scatter x1, local copies, waits for them, and re-layouts, per_device(): outgoing = jnp.zeros((capacity * shard_count, block_rows, width), jnp.bfl...  7.12 us
  transfers between devices with their start and end apart: 3, of which 3 were waited for; matrix products, arithmetic and copies ran while one was open for 2% of the time, Pallas kernels for 0%

commit v1 on v0

v1 whole, which is shorter than its diff:
```python
import functools

import jax
import jax.numpy as jnp
from jax import lax
from jax.experimental import pallas as pl
from jax.experimental.pallas import tpu as pltpu
from jax.sharding import PartitionSpec as P

VMEM = pltpu.VMEM
LIMIT = 48 * 1024 * 1024
F32 = jnp.float32
BF16 = jnp.bfloat16


def params(**kw):
    return pltpu.CompilerParams(vmem_limit_bytes=LIMIT, **kw)


def whole():
    return pl.BlockSpec(memory_space=VMEM)


def smem():
    return pl.BlockSpec(memory_space=pltpu.SMEM)


def pack_kernel(order_ref, slot_ref, part_ref, factor_ref, out_ref):
    classes, size = out_ref.shape[0], out_ref.shape[1]
    panel = factor_ref.shape[1]
    count = size - panel
    for c in range(classes):

        def move(j, _):
            out_ref[c, j] = part_ref[order_ref[c * count + j]]
            return 0

        lax.fori_loop(0, count, move, 0, unroll=8)
        out_ref[c, pl.ds(count, panel)] = factor_ref[slot_ref[c]]


def spread_kernel(owner_ref, in_ref, out_ref):
    out_ref[...] = jnp.zeros_like(out_ref)
    count = owner_ref.shape[0]

    def add(j, _):
        total = in_ref[0, j].astype(F32)
        for r in range(1, in_ref.shape[0]):
            total = total + in_ref[r, j].astype(F32)
        out_ref[owner_ref[j]] = total.astype(out_ref.dtype)
        return 0

    lax.fori_loop(0, count, add, 0, unroll=4)


def update_kernel(slot_ref, left_ref, grad_ref, right_ref, out_ref):
    del slot_ref
    panels = grad_ref.shape[0]
    grad = jnp.concatenate([grad_ref[c] for c in range(panels)], axis=1)
    right = jnp.concatenate([right_ref[c] for c in range(panels)], axis=1)
    rows = left_ref.shape[2]
    for r in range(left_ref.shape[0]):
        product = jnp.dot(left_ref[r, 0], grad, preferred_element_type=F32).astype(BF16)
        result = jnp.dot(product, right, preferred_element_type=F32).astype(BF16)
        for c in range(panels):
            out_ref[c, pl.ds(r * rows, rows), :] = result[:, c * 128 : (c + 1) * 128]


def stats_kernel(meta_ref, grad_ref, left_ref, right_ref, left_out, right_out):
    replica = meta_ref[4]
    panels = grad_ref.shape[1]
    rows = left_ref.shape[2]
    start = pl.multiple_of(replica * rows, rows)
    grad = jnp.concatenate([grad_ref[0, c] for c in range(panels)], axis=1)
    own_rows = jnp.concatenate([grad_ref[0, c, pl.ds(start, rows), :] for c in range(panels)], axis=1)
    own_cols = grad_ref[0, replica]
    left = lax.dot_general(own_rows, grad, (((1,), (1,)), ((), ())), preferred_element_type=F32)
    right = lax.dot_general(own_cols, grad, (((0,), (0,)), ((), ())), preferred_element_type=F32)
    left_out[0, 0] = (0.9 * left_ref[0, 0].astype(F32) + 0.1 * left).astype(left_out.dtype)
    right_out[0, 0] = (0.9 * right_ref[0, 0].astype(F32) + 0.1 * right).astype(right_out.dtype)


def collect_kernel(source_ref, in_ref, out_ref):
    def move(b, _):
        out_ref[b] = in_ref[source_ref[b]]
        return 0

    lax.fori_loop(0, out_ref.shape[0], move, 0, unroll=8)


def per_device(partials, owners, left_stat, right_stat, left_factor, right_factor):
    shards = lax.axis_size("shard")
    classes = lax.axis_size("rep")
    replica = lax.axis_index("rep")
    me = lax.axis_index("shard")
    _, blocks, rows, width = partials.shape
    slots = left_stat.shape[1]
    quarter = width // classes
    lanes = quarter
    panels = width // lanes
    per_class = blocks // classes
    tile = rows * panels

    number = jnp.arange(blocks, dtype=jnp.int32)
    key = owners * blocks + number
    position = jnp.sum((key[None, :] < key[:, None]).astype(jnp.int32), axis=1)
    place = (position % classes) * per_class + position // classes
    order = jnp.sum(jnp.where(place[None, :] == number[:, None], number[None, :], 0), axis=1)
    class_owner = jnp.sum(
        jnp.where(
            position[None, :] == (number[:per_class] * classes + replica)[:, None], owners[None, :], 0
        ),
        axis=1,
    )
    source = (position % classes) * shards + owners
    base = jnp.sum((owners < me).astype(jnp.int32))
    each = jnp.arange(classes, dtype=jnp.int32)
    slot_of_class = (each + 4 * classes - base % classes) % classes
    class_of_slot = (each + base) % classes
    my_slot = (replica + classes - base % classes) % classes

    left_all = lax.all_gather(left_factor[0], "rep", axis=0, tiled=False)

    part_tiles = (
        partials[0].reshape(blocks, rows, panels, lanes).transpose(0, 2, 1, 3).reshape(blocks, tile, lanes)
    )
    factor_tiles = right_factor[0].reshape(slots, width // tile, tile, quarter)
    size = per_class + width // tile
    message = pl.pallas_call(
        pack_kernel,
        out_shape=jax.ShapeDtypeStruct((classes, size, tile, lanes), BF16),
        in_specs=[smem(), smem(), whole(), whole()],
        out_specs=whole(),
        compiler_params=params(),
        name="pack",
    )(order, slot_of_class, part_tiles, factor_tiles)
    received = lax.all_to_all(message, "rep", split_axis=0, concat_axis=0, tiled=True)
    right_panels = received[:, per_class:].reshape(classes, width, lanes)
    outgoing = pl.pallas_call(
        spread_kernel,
        out_shape=jax.ShapeDtypeStruct((shards, tile, lanes), BF16),
        in_specs=[smem(), whole()],
        out_specs=whole(),
        compiler_params=params(),
        name="spread",
    )(class_owner, received)
    incoming = lax.all_to_all(outgoing, "shard", split_axis=0, concat_axis=0, tiled=True)
    grad = (
        incoming.reshape(shards, panels, rows, lanes).transpose(1, 0, 2, 3).reshape(panels, width, lanes)
    )
    grads = lax.all_gather(grad, "rep", axis=0, tiled=False)

    update_panels = pl.pallas_call(
        update_kernel,
        out_shape=jax.ShapeDtypeStruct((panels, width, lanes), BF16),
        grid_spec=pltpu.PrefetchScalarGridSpec(
            num_scalar_prefetch=1,
            grid=(1,),
            in_specs=[
                pl.BlockSpec((classes, 1, quarter, width), lambda i, s: (0, s[0], 0, 0)),
                pl.BlockSpec((panels, width, lanes), lambda i, s: (0, 0, 0)),
                pl.BlockSpec((panels, width, lanes), lambda i, s: (0, 0, 0)),
            ],
            out_specs=pl.BlockSpec((panels, width, lanes), lambda i, s: (0, 0, 0)),
        ),
        compiler_params=params(),
        cost_estimate=pl.CostEstimate(flops=4 * width**3, bytes_accessed=8 * width**2, transcendentals=0),
        name="update",
    )(my_slot[None], left_all, grad, right_panels)
    returned = lax.all_to_all(
        update_panels.reshape(panels * shards, rows, lanes),
        ("rep", "shard"),
        split_axis=0,
        concat_axis=0,
        tiled=True,
    )
    update = pl.pallas_call(
        collect_kernel,
        out_shape=jax.ShapeDtypeStruct((blocks, rows, lanes), BF16),
        in_specs=[smem(), whole()],
        out_specs=whole(),
        compiler_params=params(),
        name="collect",
    )(source, returned)

    stat_spec = pl.BlockSpec((1, 1, quarter, width), lambda k, s: (0, k, 0, 0))
    left_new, right_new = pl.pallas_call(
        stats_kernel,
        out_shape=(
            jax.ShapeDtypeStruct(left_stat.shape, BF16),
            jax.ShapeDtypeStruct(right_stat.shape, BF16),
        ),
        grid_spec=pltpu.PrefetchScalarGridSpec(
            num_scalar_prefetch=1,
            grid=(slots,),
            in_specs=[
                pl.BlockSpec((1, panels, width, lanes), lambda k, s: (s[k], 0, 0, 0)),
                stat_spec,
                stat_spec,
            ],
            out_specs=[stat_spec, stat_spec],
        ),
        compiler_params=params(),
        cost_estimate=pl.CostEstimate(
            flops=4 * slots * quarter * width**2, bytes_accessed=16 * slots * quarter * width, transcendentals=0
        ),
        name="stats",
    )(jnp.concatenate([class_of_slot, replica[None]]), grads, left_stat, right_stat)
    return left_new, right_new, update


def solution(mesh):
    return jax.shard_map(
        per_device,
        mesh=mesh,
        in_specs=(
            P("rep", None, "shard", None),
            P(),
            P("shard", None, "rep", None),
            P("shard", None, "rep", None),
            P("shard", None, "rep", None),
            P("shard", None, None, "rep"),
        ),
        out_specs=(
            P("shard", None, "rep", None),
            P("shard", None, "rep", None),
            P(None, "shard", "rep"),
        ),
        check_vma=False,
    )
```

time: 235 us -> 143 us (0.61)
  waiting for transfers between devices: 110 us -> 35.3 us
  blocking collectives: 67.9 us -> 55.9 us
  Pallas kernels: 0 us -> 9.55 us
  local copies, waits for them, and re-layouts: 16.9 us -> 7.46 us
  matrix products: 8.24 us -> 0 us
    psum x1 -> x0, waiting for transfers between devices: 60.5 us -> none  [per_device(): lax.psum(local_part.astype(jnp.float32).astype(jnp.bfloat16), 'rep')]
    all_gather x1 -> x2, waiting for transfers between devices: 33.6 us -> 0.02 us  [the longest x1 0.02 us: per_device(): left_all = lax.all_gather(left_factor[0], 'rep', axis=0, tiled=False)]
    all_to_all x1 -> x2, waiting for transfers between devices: 15.4 us -> 34.6 us  [the longest x1 21.3 us: per_device(): lax.all_to_all(update_panels.reshape(panels * shards, rows, lanes), ('rep...]
    all_to_all x1, blocking collectives: 67.9 us -> 55.9 us  [per_device(): lax.all_to_all(outgoing, 'shard', split_axis=0, concat_axis=0, tiled=True)]
    pallas_call x0 -> x5, Pallas kernels: none -> 9.55 us  [the longest x1 3.08 us: per_device(): pl.pallas_call(stats_kernel, out_shape=(jax.ShapeDtypeStruct(left_stat.sh...]
    dot_general x4 -> x0, matrix products: 8.24 us -> none  [the longest x1 2.49 us: per_device(): jnp.einsum('kij,kjl->kil', left_product, right_factor[0], preferred_eleme...]
    scatter x1 -> x0, local copies, waits for them, and re-layouts: 7.12 us -> none  [per_device(): outgoing = jnp.zeros((capacity * shard_count, block_rows, width), jnp.bfl...]
    unnamed x8 -> x16, local copies, waits for them, and re-layouts: 0.66 us -> 6.44 us
  transfers between devices with their start and end apart: 3 -> 4, of which waited for: 3 -> 2; matrix products, arithmetic and copies ran while one was open for 2% -> 3% of each run, Pallas kernels for 0% -> 5%
where the time goes in v1:
time: 143 us
  blocking collectives  55.9 us (39%)
  waiting for transfers between devices  35.3 us (25%)
  between operations  16 us (11%)
  starting transfers between devices  15.3 us (11%)
  Pallas kernels  9.55 us (7%)
  local copies, waits for them, and re-layouts  7.46 us (5%)
  other arithmetic  3.22 us (2%)
    all_to_all x1, blocking collectives, per_device(): lax.all_to_all(outgoing, 'shard', split_axis=0, concat_axis=0, tiled=True)  55.9 us
    all_to_all x1, waiting for transfers between devices, per_device(): lax.all_to_all(update_panels.reshape(panels * shards, rows, lanes), ('rep...  21.3 us
    all_to_all x1, waiting for transfers between devices, per_device(): lax.all_to_all(message, 'rep', split_axis=0, concat_axis=0, tiled=True)  13.3 us
    all_to_all x1, starting transfers between devices, per_device(): lax.all_to_all(update_panels.reshape(panels * shards, rows, lanes), ('rep...  10.3 us
    unnamed x16, local copies, waits for them, and re-layouts  6.44 us
    all_to_all x1, starting transfers between devices, per_device(): lax.all_to_all(message, 'rep', split_axis=0, concat_axis=0, tiled=True)  4.97 us
    pallas_call x1, Pallas kernels, per_device(): pl.pallas_call(stats_kernel, out_shape=(jax.ShapeDtypeStruct(left_stat.sh...  3.08 us
  transfers between devices with their start and end apart: 4, of which 2 were waited for; matrix products, arithmetic and copies ran while one was open for 3% of the time, Pallas kernels for 5%

profile of v1, /device:TPU:1, one launch (start us, length us, event | category | flops | bytes accessed | tf_op | source)
XLA Modules:
  0.0 142.8 jit_solution(3292044381708814216)
XLA Ops:
  7.2 0.0 all-gather.5.cloned.1.call-start
  7.2 0.7 all-gather.5.cloned.1.call-update
  7.9 0.7 iota_add_fusion
  8.6 0.2 convert_reduce_fusion
  8.8 1.3 multiply_add_fusion
  12.0 0.1 select_reduce_fusion.order_ref
  12.1 0.0 copy-start.3
  12.1 1.2 copy-done.3
  13.3 0.0 copy-start.4
  13.3 1.0 copy-done.4
  14.3 2.1 %pack.1 = bf16[4,88,16,128]{3,2,1,0:T(8,128)(2,1)} custom-call(s32[224]{0:T(256)S(1)} %select_reduce_fusion.order_ref, s32[4]{0:T(128)S(1)} %and_select_fusion.slot_ref, bf16[224,16,128]{2,1,0:T(8,128)(2,1)S(1)} %bitcast.19, bf16[4,32,16,128]{3,2,1,0:T(8,128)(2,1)S(1)} %bitcast.20), custom_call_target="tpu_custom_call" | custom-call | tf_op jit(solution)/shard_map/pack/pallas_call | solution.py:129
  16.4 0.0 copy-start.7
  16.5 5.0 %all-to-all-start = ((bf16[4,88,16,128]{3,2,1,0:T(8,128)(2,1)}), bf16[4,88,16,128]{3,2,1,0:T(8,128)(2,1)S(1)}, u32[]{:S(2)}, u32[]{:S(2)}) async-start(bf16[4,88,16,128]{3,2,1,0:T(8,128)(2,1)} %pack.1), calls=%async_computation | async-start | bytes 2883584 | tf_op jit(solution)/shard_map/all_to_all | solution.py:137
  21.4 0.0 all-gather.3.cloned.1.call-start
  21.4 0.0 copy-done.7
  21.4 0.2 select_reduce_fusion.1.owner_ref
  21.6 13.3 %all-to-all-done.in_ref = bf16[4,88,16,128]{3,2,1,0:T(8,128)(2,1)S(1)} async-done(((bf16[4,88,16,128]{3,2,1,0:T(8,128)(2,1)}), bf16[4,88,16,128]{3,2,1,0:T(8,128)(2,1)S(1)}, u32[]{:S(2)}, u32[]{:S(2)}) %all-to-all-start) | async-done | bytes 1441824 | tf_op jit(solution)/shard_map/all_to_all | solution.py:137
  34.9 0.8 spread.1
  35.7 55.9 %all_to_all.15 = bf16[128,16,128]{2,1,0:T(8,128)(2,1)S(1)} all-to-all(bf16[128,16,128]{2,1,0:T(8,128)(2,1)S(1)} %spread.1), channel_id=1, replica_groups=mesh['rep'=4,'shard'=128] {'shard'}, dimensions={0} | all-to-all | bytes 1048576 | tf_op jit(solution)/shard_map/all_to_all | solution.py:147
  91.7 1.0 copy.14
  92.6 0.0 all-gather.3.cloned.1.call-update
  92.7 0.0 all-gather.5.cloned.1.call-done.left_ref
  92.8 0.0 copy-start
  92.8 1.0 copy-done
  93.8 0.0 copy-start.1
  93.8 1.6 %copy-done.1 = bf16[4,4,128,512]{3,2,1,0:T(8,128)(2,1)S(1)} copy-done((bf16[4,4,128,512]{3,2,1,0:T(8,128)(2,1)S(1)}, bf16[4,4,128,512]{3,2,1,0:T(8,128)(2,1)}, u32[]{:S(2)}) %copy-start.1) | copy-done | bytes 2097176
  95.4 0.0 copy-start.5
  95.4 0.0 copy-start.6
  95.4 2.0 %update.1 = bf16[4,512,128]{2,1,0:T(8,128)(2,1)} custom-call(s32[1]{0:T(128)} %bitcast.8.slot_ref, bf16[4,4,128,512]{3,2,1,0:T(8,128)(2,1)S(1)} %copy-done.1, bf16[4,512,128]{2,1,0:T(8,128)(2,1)S(1)} %bitcast.17, bf16[4,512,128]{2,1,0:T(8,128)(2,1)S(1)} %bitcast.18), custom_call_target="tpu_custom_call" | custom-call | flops 536870912 | bytes 2097152 | tf_op jit(solution)/shard_map/update/pallas_call | solution.py:153
  97.4 10.3 %all-to-all-start.2 = ((bf16[512,4,128]{2,1,0:T(4,128)(2,1)}), bf16[512,4,128]{2,1,0:T(4,128)(2,1)S(1)}, u32[]{:S(2)}, u32[]{:S(2)}) async-start(bf16[512,4,128]{2,1,0:T(4,128)(2,1)} %bitcast.11), calls=%async_computation.2 | async-start | bytes 1048576 | tf_op jit(solution)/shard_map/all_to_all | solution.py:170
  107.7 0.6 and_select_fusion.3
  108.3 0.1 pad_add_fusion.meta_ref
  108.4 21.3 %all-to-all-done.2.in_ref = bf16[512,4,128]{2,1,0:T(4,128)(2,1)S(1)} async-done(((bf16[512,4,128]{2,1,0:T(4,128)(2,1)}), bf16[512,4,128]{2,1,0:T(4,128)(2,1)S(1)}, u32[]{:S(2)}, u32[]{:S(2)}) %all-to-all-start.2) | async-done | bytes 524320 | tf_op jit(solution)/shard_map/all_to_all | solution.py:170
  129.7 1.6 %collect.1 = bf16[224,4,128]{2,1,0:T(4,128)(2,1)} custom-call(s32[224]{0:T(256)S(1)} %get-tuple-element.7.source_ref, bf16[512,4,128]{2,1,0:T(4,128)(2,1)S(1)} %all-to-all-done.2.in_ref), custom_call_target="tpu_custom_call" | custom-call | tf_op jit(solution)/shard_map/collect/pallas_call | solution.py:177
  131.3 0.0 all-gather.3.cloned.1.call-done.grad_ref
  131.3 0.0 copy-done.5
  131.3 0.0 copy-done.6
  131.3 0.0 copy-start.2
  131.3 1.6 %copy-done.2 = bf16[4,4,512,128]{3,2,1,0:T(8,128)(2,1)S(1)} copy-done((bf16[4,4,512,128]{3,2,1,0:T(8,128)(2,1)S(1)}, bf16[4,4,512,128]{3,2,1,0:T(8,128)(2,1)}, u32[]{:S(2)}) %copy-start.2) | copy-done | bytes 2097176
  132.9 3.1 %stats.1 = (bf16[1,4,128,512]{3,2,1,0:T(8,128)(2,1)}, bf16[1,4,128,512]{3,2,1,0:T(8,128)(2,1)}) custom-call(s32[5]{0:T(128)S(1)} %pad_add_fusion.meta_ref, bf16[4,4,512,128]{3,2,1,0:T(8,128)(2,1)S(1)} %copy-done.2, bf16[1,4,128,512]{3,2,1,0:T(8,128)(2,1)S(1)} %copy-done.5, bf16[1,4,128,512]{3,2,1,0:T(8,128)(2,1)S(1)} %copy-done.6), custom_call_target="tpu_custom_call" | custom-call | flops 536870912 | bytes 4194304 | tf_op jit(solution)/shard_map/stats/pallas_call | solution.py:187
  (4 shorter events, 0.1 us)
Async XLA Ops:
  7.2 85.6 %all-gather.5.cloned.1.call-start = ((), (), s32[]{:S(2)}) async-start(), calls=%async_computation.4 | async-start | bytes 2621440 | tf_op jit(solution)/shard_map/all_gather | solution.py:122
  12.1 1.2 copy-start.3
  13.3 1.0 copy-start.4
  16.4 5.0 %copy-start.7 = (s32[224]{0:T(256)S(1)}, s32[224]{0:T(256)}, u32[]{:S(2)}) copy-start(s32[224]{0:T(256)} %param.7) | copy-start | bytes 2692
  16.5 18.5 %all-to-all-start = ((bf16[4,88,16,128]{3,2,1,0:T(8,128)(2,1)}), bf16[4,88,16,128]{3,2,1,0:T(8,128)(2,1)S(1)}, u32[]{:S(2)}, u32[]{:S(2)}) async-start(bf16[4,88,16,128]{3,2,1,0:T(8,128)(2,1)} %pack.1), calls=%async_computation | async-start | bytes 2883584 | tf_op jit(solution)/shard_map/all_to_all | solution.py:137
  21.4 109.9 %all-gather.3.cloned.1.call-start = ((), (), s32[]{:S(2)}) async-start(), calls=%async_computation.3 | async-start | bytes 2621440 | tf_op jit(solution)/shard_map/all_gather | solution.py:151
  92.8 1.0 copy-start
  93.8 1.6 %copy-start.1 = (bf16[4,4,128,512]{3,2,1,0:T(8,128)(2,1)S(1)}, bf16[4,4,128,512]{3,2,1,0:T(8,128)(2,1)}, u32[]{:S(2)}) copy-start(bf16[4,4,128,512]{3,2,1,0:T(8,128)(2,1)} %all-gather.5.cloned.1.call-done.left_ref) | copy-start | bytes 6291460
  95.4 35.9 %copy-start.5 = (bf16[1,4,128,512]{3,2,1,0:T(8,128)(2,1)S(1)}, bf16[1,4,128,512]{3,2,1,0:T(8,128)(2,1)}, u32[]{:S(2)}) copy-start(bf16[1,4,128,512]{3,2,1,0:T(8,128)(2,1)} %left_ref.1) | copy-start | bytes 1572868
  95.4 35.9 %copy-start.6 = (bf16[1,4,128,512]{3,2,1,0:T(8,128)(2,1)S(1)}, bf16[1,4,128,512]{3,2,1,0:T(8,128)(2,1)}, u32[]{:S(2)}) copy-start(bf16[1,4,128,512]{3,2,1,0:T(8,128)(2,1)} %right_ref.1) | copy-start | bytes 1572868
  97.4 32.3 %all-to-all-start.2 = ((bf16[512,4,128]{2,1,0:T(4,128)(2,1)}), bf16[512,4,128]{2,1,0:T(4,128)(2,1)S(1)}, u32[]{:S(2)}, u32[]{:S(2)}) async-start(bf16[512,4,128]{2,1,0:T(4,128)(2,1)} %bitcast.11), calls=%async_computation.2 | async-start | bytes 1048576 | tf_op jit(solution)/shard_map/all_to_all | solution.py:170
  131.3 1.6 %copy-start.2 = (bf16[4,4,512,128]{3,2,1,0:T(8,128)(2,1)S(1)}, bf16[4,4,512,128]{3,2,1,0:T(8,128)(2,1)}, u32[]{:S(2)}) copy-start(bf16[4,4,512,128]{3,2,1,0:T(8,128)(2,1)} %all-gather.3.cloned.1.call-done.grad_ref) | copy-start | bytes 6291460
Sparse Core Ops, SparseCore 0:
  10.1 48.3 all-gather.4
  92.8 32.5 all-gather.2

commit v2 on v0

v2 whole, which is shorter than its diff:
```python
import jax
import jax.numpy as jnp
from jax import lax
from jax.experimental import pallas as pl
from jax.experimental.pallas import tpu as pltpu
from jax.sharding import PartitionSpec as P

VMEM = pltpu.VMEM
SMEM = pltpu.SMEM
LIMIT = 40 * 1024 * 1024
WIDE = 58 * 1024 * 1024
F32 = jnp.float32
BF16 = jnp.bfloat16
LANES = 128
TILE = 16


def params(limit=LIMIT):
    return pltpu.CompilerParams(vmem_limit_bytes=limit)


def in_vmem():
    return pl.BlockSpec(memory_space=VMEM)


def in_smem():
    return pl.BlockSpec(memory_space=SMEM)


def anywhere():
    return pl.BlockSpec(memory_space=pl.ANY)


def pack_kernel(
    where_ref, owners_ref, lanes_ref, part_ref, left_ref, right_ref,
    out_ref, owner_at_ref, source_ref, base_ref,
    part, left, rank, rank_at, sems,
):
    classes = out_ref.shape[0]
    blocks = part_ref.shape[0]
    count = blocks // classes
    shards = where_ref[2]
    me = where_ref[0]
    panel = right_ref.shape[1]
    side = left_ref.shape[1]
    load_part = pltpu.make_async_copy(part_ref, part, sems.at[0])
    load_left = pltpu.make_async_copy(left_ref, left, sems.at[1])
    load_part.start()
    load_left.start()

    key = lanes_ref[...] * blocks + lax.broadcasted_iota(jnp.int32, lanes_ref.shape, 1)

    def compare(b, carry):
        before, base = carry
        owner = owners_ref[b]
        before = before + jnp.where(key > owner * blocks + b, 1, 0)
        return before, base + jnp.where(owner < me, 1, 0)

    before, base = lax.fori_loop(
        0, blocks, compare, (jnp.zeros_like(key), jnp.int32(0)), unroll=8
    )
    rank[...] = before
    base_ref[0] = base
    place = pltpu.make_async_copy(rank, rank_at, sems.at[2])
    place.start()
    loads = []
    slots = []
    for c in range(classes):
        slot = lax.rem(c + classes - lax.rem(base, classes), classes)
        load = pltpu.make_async_copy(right_ref.at[slot], out_ref.at[c, pl.ds(count, panel)], sems.at[3 + c])
        load.start()
        loads.append(load)
        slots.append(slot)
    load_left.wait()
    for c in range(classes):
        for h in range(left.shape[2] // LANES):
            rows = left[slots[c], :, h * LANES : (h + 1) * LANES]
            out_ref[c, pl.ds(count + panel + h * side // TILE, side // TILE)] = rows.reshape(
                side // TILE, TILE, LANES
            )
    place.wait()
    load_part.wait()

    def move(b, _):
        p = rank_at[0, b]
        c = lax.rem(p, classes)
        j = lax.div(p, classes)
        out_ref[c, j] = part[b]
        owner = owners_ref[b]
        owner_at_ref[c * count + j] = owner
        source_ref[b] = c * shards + owner
        return 0

    lax.fori_loop(0, blocks, move, 0, unroll=8)
    for load in loads:
        load.wait()


def spread_kernel(where_ref, owner_at_ref, in_ref, out_ref):
    out_ref[...] = jnp.zeros_like(out_ref)
    classes = in_ref.shape[0]
    count = owner_at_ref.shape[0] // classes
    first = where_ref[1] * count

    def add(j, _):
        total = in_ref[0, j].astype(F32)
        for r in range(1, classes):
            total = total + in_ref[r, j].astype(F32)
        out_ref[owner_at_ref[first + j]] = total.astype(out_ref.dtype)
        return 0

    lax.fori_loop(0, count, add, 0, unroll=8)


def update_kernel(count, grad_ref, in_ref, out_ref, copy_ref, sem):
    hand_on = pltpu.make_async_copy(grad_ref, copy_ref, sem)
    hand_on.start()
    panels, width, _ = grad_ref.shape
    rows = width // panels
    tall = width // TILE
    wide = rows // TILE
    grad = jnp.concatenate([grad_ref[c] for c in range(panels)], axis=1)
    right = jnp.concatenate(
        [in_ref[c, pl.ds(count, tall)].reshape(width, LANES) for c in range(panels)], axis=1
    )
    for r in range(panels):
        left = jnp.concatenate(
            [
                in_ref[r, pl.ds(count + tall + h * wide, wide)].reshape(rows, LANES)
                for h in range(width // LANES)
            ],
            axis=1,
        )
        product = jnp.dot(left, grad, preferred_element_type=F32).astype(BF16)
        result = jnp.dot(product, right, preferred_element_type=F32).astype(BF16)
        for c in range(panels):
            out_ref[c, pl.ds(r * rows, rows), :] = result[:, c * LANES : (c + 1) * LANES]
    hand_on.wait()


def finish_kernel(
    where_ref, source_ref, base_ref, in_ref, grads_ref, left_ref, right_ref,
    left_out, right_out, update_out,
    grads, lefts, rights, update, in_sems, out_sems,
):
    slots, rows, _ = left_ref.shape
    panels = grads_ref.shape[1]
    replica = where_ref[1]
    base = base_ref[0]
    loads = []
    for k in range(slots):
        c = lax.rem(base + k, slots)
        step = [
            pltpu.make_async_copy(grads_ref.at[c], grads.at[k], in_sems.at[k, 0]),
            pltpu.make_async_copy(left_ref.at[k], lefts.at[k], in_sems.at[k, 1]),
            pltpu.make_async_copy(right_ref.at[k], rights.at[k], in_sems.at[k, 2]),
        ]
        for load in step:
            load.start()
        loads.append(step)

    def move(b, _):
        update[b] = in_ref[source_ref[b]]
        return 0

    lax.fori_loop(0, update.shape[0], move, 0, unroll=8)
    stores = [pltpu.make_async_copy(update, update_out, out_sems.at[2 * slots])]
    stores[0].start()
    start = pl.multiple_of(replica * rows, rows)
    for k in range(slots):
        for load in loads[k]:
            load.wait()
        grad = jnp.concatenate([grads[k, c] for c in range(panels)], axis=1)
        own_rows = jnp.concatenate([grads[k, c, pl.ds(start, rows), :] for c in range(panels)], axis=1)
        own_cols = grads[k, replica]
        left = lax.dot_general(own_rows, grad, (((1,), (1,)), ((), ())), preferred_element_type=F32)
        right = lax.dot_general(own_cols, grad, (((0,), (0,)), ((), ())), preferred_element_type=F32)
        lefts[k] = (0.9 * lefts[k].astype(F32) + 0.1 * left).astype(lefts.dtype)
        rights[k] = (0.9 * rights[k].astype(F32) + 0.1 * right).astype(rights.dtype)
        for n, (new, out) in enumerate(((lefts, left_out), (rights, right_out))):
            store = pltpu.make_async_copy(new.at[k], out.at[k], out_sems.at[2 * k + n])
            store.start()
            stores.append(store)
    for store in stores:
        store.wait()


def per_device(partials, owners, left_stat, right_stat, left_factor, right_factor):
    shards = lax.axis_size("shard")
    classes = lax.axis_size("rep")
    where = jnp.stack([lax.axis_index("shard"), lax.axis_index("rep"), jnp.int32(shards)])
    _, blocks, rows, width = partials.shape
    slots = left_stat.shape[1]
    quarter = width // classes
    panels = width // LANES
    count = blocks // classes
    tall = width // TILE
    size = count + 2 * tall

    part_tiles = (
        partials[0].reshape(blocks, rows, panels, LANES).transpose(0, 2, 1, 3).reshape(blocks, TILE, LANES)
    )
    right_tiles = right_factor[0].reshape(slots, tall, TILE, LANES)
    message, owner_at, source, base = pl.pallas_call(
        pack_kernel,
        out_shape=(
            jax.ShapeDtypeStruct((classes, size, TILE, LANES), BF16),
            jax.ShapeDtypeStruct((blocks,), jnp.int32),
            jax.ShapeDtypeStruct((blocks,), jnp.int32),
            jax.ShapeDtypeStruct((1,), jnp.int32),
        ),
        in_specs=[in_smem(), in_smem(), in_vmem(), anywhere(), anywhere(), anywhere()],
        out_specs=(in_vmem(), in_smem(), in_smem(), in_smem()),
        scratch_shapes=[
            VMEM((blocks, TILE, LANES), BF16),
            VMEM((slots, quarter, width), BF16),
            VMEM((1, blocks), jnp.int32),
            SMEM((1, blocks), jnp.int32),
            pltpu.SemaphoreType.DMA((3 + classes,)),
        ],
        compiler_params=params(WIDE),
        name="pack",
    )(where, owners, owners.reshape(1, blocks), part_tiles, left_factor[0], right_tiles)
    received = lax.all_to_all(message, "rep", split_axis=0, concat_axis=0, tiled=True)
    outgoing = pl.pallas_call(
        spread_kernel,
        out_shape=jax.ShapeDtypeStruct((shards, TILE, LANES), BF16),
        in_specs=[in_smem(), in_smem(), in_vmem()],
        out_specs=in_vmem(),
        compiler_params=params(),
        name="spread",
    )(where, owner_at, received)
    incoming = lax.all_to_all(outgoing, "shard", split_axis=0, concat_axis=0, tiled=True)
    grad = (
        incoming.reshape(shards, panels, rows, LANES).transpose(1, 0, 2, 3).reshape(panels, width, LANES)
    )
    update_panels, grad_copy = pl.pallas_call(
        lambda *refs: update_kernel(count, *refs),
        out_shape=(
            jax.ShapeDtypeStruct((panels, width, LANES), BF16),
            jax.ShapeDtypeStruct((panels, width, LANES), BF16),
        ),
        in_specs=[in_vmem(), in_vmem()],
        out_specs=(in_vmem(), anywhere()),
        scratch_shapes=[pltpu.SemaphoreType.DMA],
        compiler_params=params(),
        cost_estimate=pl.CostEstimate(flops=4 * width**3, bytes_accessed=8 * width**2, transcendentals=0),
        name="update",
    )(grad, received)
    grads = lax.all_gather(grad_copy, "rep", axis=0, tiled=False)
    returned = lax.all_to_all(
        update_panels.reshape(panels * shards, rows, LANES),
        ("rep", "shard"),
        split_axis=0,
        concat_axis=0,
        tiled=True,
    )
    left_new, right_new, update = pl.pallas_call(
        finish_kernel,
        out_shape=(
            jax.ShapeDtypeStruct(left_stat.shape[1:], BF16),
            jax.ShapeDtypeStruct(right_stat.shape[1:], BF16),
            jax.ShapeDtypeStruct((blocks, rows, LANES), BF16),
        ),
        in_specs=[in_smem(), in_smem(), in_smem(), in_vmem(), anywhere(), anywhere(), anywhere()],
        out_specs=(anywhere(), anywhere(), anywhere()),
        scratch_shapes=[
            VMEM((slots, panels, width, LANES), BF16),
            VMEM((slots, quarter, width), BF16),
            VMEM((slots, quarter, width), BF16),
            VMEM((blocks, rows, LANES), BF16),
            pltpu.SemaphoreType.DMA((slots, 3)),
            pltpu.SemaphoreType.DMA((2 * slots + 1,)),
        ],
        compiler_params=params(WIDE),
        cost_estimate=pl.CostEstimate(
            flops=4 * slots * quarter * width**2, bytes_accessed=16 * slots * quarter * width, transcendentals=0
        ),
        name="finish",
    )(where, source, base, returned, grads, left_stat[0], right_stat[0])
    return left_new[None], right_new[None], update


def solution(mesh):
    return jax.shard_map(
        per_device,
        mesh=mesh,
        in_specs=(
            P("rep", None, "shard", None),
            P(),
            P("shard", None, "rep", None),
            P("shard", None, "rep", None),
            P("shard", None, "rep", None),
            P("shard", None, None, "rep"),
        ),
        out_specs=(
            P("shard", None, "rep", None),
            P("shard", None, "rep", None),
            P(None, "shard", "rep"),
        ),
        check_vma=False,
    )
```

time: 235 us -> 128 us (0.54)
  waiting for transfers between devices: 110 us -> 0.45 us
  blocking collectives: 67.9 us -> 100 us
  local copies, waits for them, and re-layouts: 16.9 us -> 0.19 us
  starting transfers between devices: 15.2 us -> 0.04 us
  Pallas kernels: 0 us -> 12.4 us
  matrix products: 8.24 us -> 0 us
    psum x1 -> x0, waiting for transfers between devices: 60.5 us -> none  [per_device(): lax.psum(local_part.astype(jnp.float32).astype(jnp.bfloat16), 'rep')]
    all_gather x1, waiting for transfers between devices: 33.6 us -> 0.44 us  [per_device(): grads = lax.all_gather(grad_copy, 'rep', axis=0, tiled=False)]
    all_to_all x1 -> x3, blocking collectives: 67.9 us -> 100 us  [the longest x1 43 us: per_device(): lax.all_to_all(outgoing, 'shard', split_axis=0, concat_axis=0, tiled=True)]
    all_to_all x1 -> x0, waiting for transfers between devices: 15.4 us -> none  [per_device(): lax.all_to_all(update_cols.reshape(capacity, shard_count, block_rows, qua...]
    all_to_all x1 -> x0, starting transfers between devices: 15.2 us -> none  [per_device(): lax.all_to_all(update_cols.reshape(capacity, shard_count, block_rows, qua...]
    pallas_call x0 -> x4, Pallas kernels: none -> 12.4 us  [the longest x1 5.27 us: per_device(): pl.pallas_call(finish_kernel, out_shape=(jax.ShapeDtypeStruct(left_stat.s...]
    dot_general x4 -> x0, matrix products: 8.24 us -> none  [the longest x1 2.49 us: per_device(): jnp.einsum('kij,kjl->kil', left_product, right_factor[0], preferred_eleme...]
    scatter x1 -> x0, local copies, waits for them, and re-layouts: 7.12 us -> none  [per_device(): outgoing = jnp.zeros((capacity * shard_count, block_rows, width), jnp.bfl...]
  transfers between devices with their start and end apart: 3 -> 1, of which waited for: 3 -> 1; matrix products, arithmetic and copies ran while one was open for 2% -> 0% of each run, Pallas kernels for 0% -> 0%
where the time goes in v2:
time: 128 us
  blocking collectives  100 us (78%)
  between operations  14.1 us (11%)
  Pallas kernels  12.4 us (10%)
    all_to_all x1, blocking collectives, per_device(): lax.all_to_all(outgoing, 'shard', split_axis=0, concat_axis=0, tiled=True)  43 us
    all_to_all x1, blocking collectives, per_device(): lax.all_to_all(update_panels.reshape(panels * shards, rows, LANES), ('rep...  33.3 us
    all_to_all x1, blocking collectives, per_device(): lax.all_to_all(message, 'rep', split_axis=0, concat_axis=0, tiled=True)  23.9 us
    pallas_call x1, Pallas kernels, per_device(): pl.pallas_call(finish_kernel, out_shape=(jax.ShapeDtypeStruct(left_stat.s...  5.27 us
    pallas_call x1, Pallas kernels, per_device(): pl.pallas_call(pack_kernel, out_shape=(jax.ShapeDtypeStruct((classes, siz...  5.17 us
  transfers between devices with their start and end apart: 1, of which 1 were waited for; matrix products, arithmetic and copies ran while one was open for 0% of the time, Pallas kernels for 0%

profile of v2, /device:TPU:1, one launch (start us, length us, event | category | flops | bytes accessed | tf_op | source)
XLA Modules:
  0.0 127.9 jit_solution(9895488425412535)
XLA Ops:
  7.2 0.0 all-gather.3.cloned.1.call-start
  7.2 0.6 pad_add_fusion.where_ref
  7.8 5.2 %pack.1 = (bf16[4,120,16,128]{3,2,1,0:T(8,128)(2,1)}, s32[224]{0:T(256)}, s32[224]{0:T(256)}, s32[1]{0:T(128)}) custom-call(s32[3]{0:T(128)} %pad_add_fusion.where_ref, s32[224]{0:T(256)} %owners_ref.1, s32[1,224]{1,0:T(1,128)} %bitcast.29, bf16[224,16,128]{2,1,0:T(8,128)(2,1)} %bitcast.24, bf16[4,128,512]{2,1,0:T(8,128)(2,1)} %bitcast.25, ...), custom_call_target="tpu_custom_call" | custom-call | tf_op jit(solution)/shard_map/pack/pallas_call | solution.py:204
  13.0 0.0 copy-start
  13.0 0.0 copy-start.1
  13.0 23.9 %all_to_all.15.in_ref.refs_1_ = bf16[4,120,16,128]{3,2,1,0:T(8,128)(2,1)S(1)} all-to-all(bf16[4,120,16,128]{3,2,1,0:T(8,128)(2,1)} %get-tuple-element.15), channel_id=1, replica_groups=mesh['rep'=4,'shard'=128] {'rep'}, dimensions={0} | all-to-all | bytes 3932160 | tf_op jit(solution)/shard_map/all_to_all | solution.py:224
  36.9 0.0 copy-done
  36.9 0.0 copy-done.1
  36.9 0.8 spread.1
  37.7 43.0 %all_to_all.16 = bf16[128,16,128]{2,1,0:T(8,128)(2,1)S(1)} all-to-all(bf16[128,16,128]{2,1,0:T(8,128)(2,1)S(1)} %spread.1), channel_id=1, replica_groups=mesh['rep'=4,'shard'=128] {'shard'}, dimensions={0} | all-to-all | bytes 1048576 | tf_op jit(solution)/shard_map/all_to_all | solution.py:233
  80.7 0.2 copy.12
  80.9 1.2 update.1
  82.1 0.0 all-gather.3.cloned.1.call-update
  82.1 33.3 %all_to_all.17.in_ref = bf16[512,4,128]{2,1,0:T(4,128)(2,1)} all-to-all(bf16[512,4,128]{2,1,0:T(4,128)(2,1)S(1)} %bitcast.21), channel_id=1, replica_groups=mesh['rep'=4,'shard'=128] {'rep','shard'}, dimensions={0} | all-to-all | bytes 1048576 | tf_op jit(solution)/shard_map/all_to_all | solution.py:251
  115.4 0.4 all-gather.3.cloned.1.call-done
  115.8 5.3 %finish.1 = (bf16[4,128,512]{2,1,0:T(8,128)(2,1)}, bf16[4,128,512]{2,1,0:T(8,128)(2,1)}, bf16[224,4,128]{2,1,0:T(4,128)(2,1)}) custom-call(s32[3]{0:T(128)} %pad_add_fusion.where_ref, s32[224]{0:T(256)} %get-tuple-element.12.source_ref, s32[1]{0:T(128)} %get-tuple-element.13.base_ref, bf16[512,4,128]{2,1,0:T(4,128)(2,1)} %all_to_all.17.in_ref, ...), custom_call_target="tpu_custom_call" | custom-call | flops 536870912 | bytes 4194304 | tf_op jit(solution)/shard_map/finish/pallas_call | solution.py:258
Async XLA Ops:
  7.2 108.6 %all-gather.3.cloned.1.call-start = ((), (), s32[]{:S(2)}) async-start(), calls=%async_computation.3 | async-start | bytes 2621440 | tf_op jit(solution)/shard_map/all_gather | solution.py:250
  13.0 23.9 %copy-start = (s32[3]{0:T(128)S(1)}, s32[3]{0:T(128)}, u32[]{:S(2)}) copy-start(s32[3]{0:T(128)} %pad_add_fusion.where_ref) | copy-start | bytes 40
  13.0 23.9 %copy-start.1 = (s32[224]{0:T(256)S(1)}, s32[224]{0:T(256)}, u32[]{:S(2)}) copy-start(s32[224]{0:T(256)} %get-tuple-element.14.owner_at_ref) | copy-start | bytes 2692
Sparse Core Ops, SparseCore 0:
  82.2 33.5 all-gather.2

commit v3 on v2

v3 whole, which is shorter than its diff:
```python
import jax
import jax.numpy as jnp
from jax import lax
from jax.experimental import pallas as pl
from jax.experimental.pallas import tpu as pltpu
from jax.sharding import PartitionSpec as P

VMEM = pltpu.VMEM
SMEM = pltpu.SMEM
LIMIT = 40 * 1024 * 1024
WIDE = 58 * 1024 * 1024
F32 = jnp.float32
BF16 = jnp.bfloat16
LANES = 128
TILE = 16


def params(limit=LIMIT):
    return pltpu.CompilerParams(vmem_limit_bytes=limit)


def in_vmem():
    return pl.BlockSpec(memory_space=VMEM)


def in_smem():
    return pl.BlockSpec(memory_space=SMEM)


def anywhere():
    return pl.BlockSpec(memory_space=pl.ANY)


def pack_kernel(owners_ref, part_ref, left_ref, right_ref, out_ref, plan_ref, source_ref, *rest):
    factor_outs = rest[:-14]
    part, message, left, factors, owners, lanes, place, place_at, plan, source = rest[-14:-4]
    in_sems, right_sems, out_sems, sems = rest[-4:]
    classes, count = out_ref.shape[:2]
    blocks = part_ref.shape[0]
    panels = right_ref.shape[1]
    me, replica = lax.axis_index("shard"), lax.axis_index("rep")
    load_owners = [
        pltpu.make_async_copy(owners_ref, owners, sems.at[0]),
        pltpu.make_async_copy(owners_ref, lanes, sems.at[1]),
    ]
    for load in load_owners:
        load.start()
    load_parts = []
    for c in range(classes):
        chunk = pl.ds(c * count, count)
        load_parts.append(pltpu.make_async_copy(part_ref.at[chunk], part.at[chunk], in_sems.at[c]))
        load_parts[c].start()
    load_left = pltpu.make_async_copy(left_ref, left, in_sems.at[classes])
    load_left.start()
    for load in load_owners:
        load.wait()
    owner = lanes[...]
    key = owner * blocks + lax.broadcasted_iota(jnp.int32, owner.shape, 1)

    def compare(b, carry):
        before, base = carry
        other = owners[0, b]
        before = before + jnp.where(key > other * blocks + b, 1, 0)
        return before, base + jnp.where(other < me, 1, 0)

    rank, base = lax.fori_loop(0, blocks, compare, (jnp.zeros_like(key), jnp.int32(0)), unroll=8)
    base = lax.rem(base, classes)
    plan[0, blocks] = base
    cls = lax.rem(rank, classes)
    place[...] = cls * count + lax.div(rank, classes)
    bring = pltpu.make_async_copy(place, place_at, sems.at[2])
    bring.start()
    slots, load_rights = [], []
    for d in range(classes):
        slots.append(lax.rem(lax.rem(replica + d, classes) + classes - base, classes))
        load_rights.append(
            pltpu.make_async_copy(right_ref.at[slots[d]], factors.at[d, pl.ds(panels, panels)], right_sems.at[d])
        )
        load_rights[d].start()
    source[...] = cls * lax.axis_size("shard") + owner
    stores = [pltpu.make_async_copy(source, source_ref, sems.at[3])]
    stores[0].start()
    load_left.wait()
    for d, factor_out in enumerate(factor_outs):
        for h in range(panels):
            factors[d, h] = left[slots[d], :, h * LANES : (h + 1) * LANES]
        load_rights[d].wait()
        stores.append(pltpu.make_async_copy(factors.at[d], factor_out, out_sems.at[classes + d]))
        stores[-1].start()
    bring.wait()
    for load in load_parts:
        load.wait()

    def move(b, _):
        at = place_at[0, b]
        message[at] = part[b]
        plan[0, at] = owners[0, b]
        return 0

    lax.fori_loop(0, blocks, move, 0, unroll=8)
    stores.append(pltpu.make_async_copy(plan, plan_ref, sems.at[4]))
    stores[-1].start()
    for c in range(classes):
        stores.append(pltpu.make_async_copy(message.at[pl.ds(c * count, count)], out_ref.at[c], out_sems.at[c]))
        stores[-1].start()
    for store in stores:
        store.wait()


def spread_kernel(plan_ref, in_ref, out_ref, spread, plan, sems, sem):
    load = pltpu.make_async_copy(plan_ref, plan, sem)
    load.start()
    spread[...] = jnp.zeros_like(spread)
    classes, count = in_ref.shape[:2]
    first = lax.axis_index("rep") * count
    load.wait()

    def add(j, _):
        total = in_ref[0, j].astype(F32)
        for r in range(1, classes):
            total = total + in_ref[r, j].astype(F32)
        spread[plan[0, first + j]] = total.astype(spread.dtype)
        return 0

    lax.fori_loop(0, count, add, 0, unroll=8)
    parts = sems.shape[0]
    length = spread.shape[0] // parts
    stores = []
    for n in range(parts):
        chunk = pl.ds(n * length, length)
        stores.append(pltpu.make_async_copy(spread.at[chunk], out_ref.at[chunk], sems.at[n]))
        stores[n].start()
    for store in stores:
        store.wait()


def update_kernel(grad_ref, *rest):
    factor_refs = rest[:-4]
    out_ref, product, held, sems = rest[-4:]
    panels, width, _ = grad_ref.shape
    rows = width // panels
    replica = lax.axis_index("rep")
    sources = [lax.rem(replica + panels - d, panels) for d in range(panels)]
    grad = jnp.concatenate([grad_ref[c] for c in range(panels)], axis=1)
    for d, factor_ref in enumerate(factor_refs):
        left = jnp.concatenate([factor_ref[h] for h in range(panels)], axis=1)
        product[d * rows : (d + 1) * rows] = jnp.dot(left, grad, preferred_element_type=F32).astype(BF16)
    stores = []
    for d, factor_ref in enumerate(factor_refs):
        right = jnp.concatenate([factor_ref[panels + h] for h in range(panels)], axis=0)
        result = jnp.dot(product[...], right, preferred_element_type=F32).astype(BF16)
        for e in range(panels):
            held[d, e] = result[e * rows : (e + 1) * rows]
        for e in range(panels):
            to = pl.ds(pl.multiple_of(sources[e] * rows, rows), rows)
            stores.append(pltpu.make_async_copy(held.at[d, e], out_ref.at[sources[d], to], sems.at[d, e]))
            stores[-1].start()
    for store in stores:
        store.wait()


def products_kernel(grad_ref, *out_refs):
    panels, width, _ = grad_ref.shape
    rows = width // panels
    replica = lax.axis_index("rep")
    grad = jnp.concatenate([grad_ref[c] for c in range(panels)], axis=1)
    for d, out_ref in enumerate(out_refs):
        to = lax.rem(replica + d, panels)
        start = pl.multiple_of(to * rows, rows)
        own_rows = jnp.concatenate([grad_ref[c, pl.ds(start, rows), :] for c in range(panels)], axis=1)
        left = lax.dot_general(own_rows, grad, (((1,), (1,)), ((), ())), preferred_element_type=F32)
        right = lax.dot_general(grad_ref[to], grad, (((0,), (0,)), ((), ())), preferred_element_type=F32)
        out_ref[0] = left.astype(out_ref.dtype)
        out_ref[1] = right.astype(out_ref.dtype)


def finish_kernel(plan_ref, source_ref, in_ref, left_ref, right_ref, *rest):
    product_refs = rest[:-10]
    left_out, right_out, update_out, lefts, rights, update, plan, source, sems, in_sems = rest[-10:]
    slots = left_ref.shape[0]
    blocks = update.shape[0]
    replica = lax.axis_index("rep")
    load_plan = pltpu.make_async_copy(plan_ref, plan, in_sems.at[0])
    load_source = pltpu.make_async_copy(source_ref, source, in_sems.at[1])
    load_plan.start()
    load_source.start()
    load_plan.wait()
    load_source.wait()
    base = plan[0, blocks]

    def move(b, _):
        update[b] = in_ref[source[0, b]]
        return 0

    lax.fori_loop(0, blocks, move, 0, unroll=8)
    stores = [pltpu.make_async_copy(update, update_out, sems.at[0])]
    stores[0].start()
    for d, product_ref in enumerate(product_refs):
        k = lax.rem(lax.rem(replica + slots - d, slots) + slots - base, slots)
        for n, (old, new, out) in enumerate(((left_ref, lefts, left_out), (right_ref, rights, right_out))):
            new[d] = (0.9 * old[k].astype(F32) + 0.1 * product_ref[n].astype(F32)).astype(new.dtype)
            stores.append(pltpu.make_async_copy(new.at[d], out.at[k], sems.at[len(stores)]))
            stores[-1].start()
    for store in stores:
        store.wait()


def to_others(messages):
    count = len(messages)
    sent = list(messages)
    for d in sorted(range(1, count), key=lambda d: -min(d, count - d)):
        sent[d] = lax.ppermute(messages[d], "rep", [(s, (s + d) % count) for s in range(count)])
    return sent


def per_device(partials, owners, left_stat, right_stat, left_factor, right_factor):
    shards = lax.axis_size("shard")
    classes = lax.axis_size("rep")
    _, blocks, rows, width = partials.shape
    slots = left_stat.shape[1]
    quarter = width // classes
    panels = width // LANES
    count = blocks // classes
    tall = width // TILE

    part_tiles = (
        partials[0].reshape(blocks, rows, panels, LANES).transpose(0, 2, 1, 3).reshape(blocks, TILE, LANES)
    )
    right_tiles = right_factor[0].reshape(slots, panels, LANES, LANES)
    factor_message = jax.ShapeDtypeStruct((2 * panels, LANES, LANES), BF16)
    message, plan, source, *factors = pl.pallas_call(
        pack_kernel,
        out_shape=(
            jax.ShapeDtypeStruct((classes, count, TILE, LANES), BF16),
            jax.ShapeDtypeStruct((1, 2 * LANES), jnp.int32),
            jax.ShapeDtypeStruct((1, blocks), jnp.int32),
            *[factor_message] * classes,
        ),
        in_specs=[anywhere()] * 4,
        out_specs=[anywhere()] * (3 + classes),
        scratch_shapes=[
            VMEM((blocks, TILE, LANES), BF16),
            VMEM((blocks, TILE, LANES), BF16),
            VMEM((slots, quarter, width), BF16),
            VMEM((classes, 2 * panels, LANES, LANES), BF16),
            SMEM((1, blocks), jnp.int32),
            VMEM((1, blocks), jnp.int32),
            VMEM((1, blocks), jnp.int32),
            SMEM((1, blocks), jnp.int32),
            SMEM((1, 2 * LANES), jnp.int32),
            VMEM((1, blocks), jnp.int32),
            pltpu.SemaphoreType.DMA((classes + 1,)),
            pltpu.SemaphoreType.DMA((classes,)),
            pltpu.SemaphoreType.DMA((2 * classes,)),
            pltpu.SemaphoreType.DMA((5,)),
        ],
        compiler_params=params(WIDE),
        name="pack",
    )(owners.reshape(1, blocks), part_tiles, left_factor[0], right_tiles)
    received = lax.all_to_all(message, "rep", split_axis=0, concat_axis=0, tiled=True)
    factors = to_others(factors)
    outgoing = pl.pallas_call(
        spread_kernel,
        out_shape=jax.ShapeDtypeStruct((shards, TILE, LANES), BF16),
        in_specs=[anywhere(), in_vmem()],
        out_specs=anywhere(),
        scratch_shapes=[
            VMEM((shards, TILE, LANES), BF16),
            SMEM((1, 2 * LANES), jnp.int32),
            pltpu.SemaphoreType.DMA((4,)),
            pltpu.SemaphoreType.DMA,
        ],
        compiler_params=params(),
        name="spread",
    )(plan, received)
    incoming = lax.all_to_all(outgoing, "shard", split_axis=0, concat_axis=0, tiled=True)
    grad = (
        incoming.reshape(shards, panels, rows, LANES).transpose(1, 0, 2, 3).reshape(panels, width, LANES)
    )
    update_panels = pl.pallas_call(
        update_kernel,
        out_shape=jax.ShapeDtypeStruct((panels, width, LANES), BF16),
        in_specs=[in_vmem()] * (1 + classes),
        out_specs=anywhere(),
        scratch_shapes=[
            VMEM((width, width), BF16),
            VMEM((panels, panels, quarter, LANES), BF16),
            pltpu.SemaphoreType.DMA((panels, panels)),
        ],
        compiler_params=params(),
        cost_estimate=pl.CostEstimate(flops=4 * width**3, bytes_accessed=8 * width**2, transcendentals=0),
        name="update",
    )(grad, *factors)
    products = pl.pallas_call(
        products_kernel,
        out_shape=[jax.ShapeDtypeStruct((2, quarter, width), BF16)] * classes,
        in_specs=[in_vmem()],
        out_specs=[in_vmem()] * classes,
        compiler_params=params(),
        cost_estimate=pl.CostEstimate(flops=4 * width**3, bytes_accessed=6 * width**2, transcendentals=0),
        name="products",
    )(grad)
    returned = lax.all_to_all(
        update_panels.reshape(panels * shards, rows, LANES),
        ("rep", "shard"),
        split_axis=0,
        concat_axis=0,
        tiled=True,
    )
    products = to_others(products)
    left_new, right_new, update = pl.pallas_call(
        finish_kernel,
        out_shape=(
            jax.ShapeDtypeStruct(left_stat.shape[1:], BF16),
            jax.ShapeDtypeStruct(right_stat.shape[1:], BF16),
            jax.ShapeDtypeStruct((blocks, rows, LANES), BF16),
        ),
        in_specs=[anywhere()] * 2 + [in_vmem()] * (3 + classes),
        out_specs=(anywhere(), anywhere(), anywhere()),
        scratch_shapes=[
            VMEM((slots, quarter, width), BF16),
            VMEM((slots, quarter, width), BF16),
            VMEM((blocks, rows, LANES), BF16),
            SMEM((1, 2 * LANES), jnp.int32),
            SMEM((1, blocks), jnp.int32),
            pltpu.SemaphoreType.DMA((2 * slots + 1,)),
            pltpu.SemaphoreType.DMA((2,)),
        ],
        compiler_params=params(),
        cost_estimate=pl.CostEstimate(
            flops=8 * slots * quarter * width, bytes_accessed=16 * slots * quarter * width, transcendentals=0
        ),
        name="finish",
    )(plan, source, returned, left_stat[0], right_stat[0], *products)
    return left_new[None], right_new[None], update


def solution(mesh):
    return jax.shard_map(
        per_device,
        mesh=mesh,
        in_specs=(
            P("rep", None, "shard", None),
            P(),
            P("shard", None, "rep", None),
            P("shard", None, "rep", None),
            P("shard", None, "rep", None),
            P("shard", None, None, "rep"),
        ),
        out_specs=(
            P("shard", None, "rep", None),
            P("shard", None, "rep", None),
            P(None, "shard", "rep"),
        ),
        check_vma=False,
    )
```

time: 128 us -> 109 us (0.85)
  blocking collectives: 100 us -> 13.9 us
  starting transfers between devices: 0.04 us -> 58.1 us
  waiting for transfers between devices: 0.45 us -> 22.4 us
  between operations: 14.1 us -> 0.85 us
  local copies, waits for them, and re-layouts: 0.19 us -> 2.26 us
  Pallas kernels: 12.4 us -> 11 us
    all_to_all x2 -> x0, blocking collectives: 76.3 us -> none  [the longest x1 43 us: per_device(): lax.all_to_all(outgoing, 'shard', split_axis=0, concat_axis=0, tiled=True)]
    all_to_all x0 -> x2, starting transfers between devices: none -> 39 us  [the longest x1 22.7 us: per_device(): lax.all_to_all(outgoing, 'shard', split_axis=0, concat_axis=0, tiled=True)]
    ppermute x0 -> x6, starting transfers between devices: none -> 19.1 us  [to_others(): lax.ppermute(messages[d], 'rep', [(s, (s + d) % count) for s in range(cou...]
    ppermute x0 -> x6, waiting for transfers between devices: none -> 11.4 us  [to_others(): lax.ppermute(messages[d], 'rep', [(s, (s + d) % count) for s in range(cou...]
    all_to_all x0 -> x2, waiting for transfers between devices: none -> 11 us  [the longest x1 11 us: per_device(): lax.all_to_all(outgoing, 'shard', split_axis=0, concat_axis=0, tiled=True)]
    all_to_all x1, blocking collectives: 23.9 us -> 13.9 us  [per_device(): lax.all_to_all(message, 'rep', split_axis=0, concat_axis=0, tiled=True)]
    pallas_call x1, Pallas kernels: 5.27 us -> 2.07 us  [per_device(): pl.pallas_call(finish_kernel, out_shape=(jax.ShapeDtypeStruct(left_stat.s...]
    unnamed x4 -> x16, local copies, waits for them, and re-layouts: 0.01 us -> 2.08 us
  transfers between devices with their start and end apart: 1 -> 8, of which waited for: 1 -> 2; matrix products, arithmetic and copies ran while one was open for 0% -> 0% of each run, Pallas kernels for 0% -> 1%
where the time goes in v3:
time: 109 us; the launch traced here: 108 us
  starting transfers between devices  58.1 us (53%)
  waiting for transfers between devices  22.4 us (21%)
  blocking collectives  13.9 us (13%)
  Pallas kernels  11 us (10%)
  local copies, waits for them, and re-layouts  2.26 us (2%)
    all_to_all x1, starting transfers between devices, per_device(): lax.all_to_all(outgoing, 'shard', split_axis=0, concat_axis=0, tiled=True)  22.7 us
    ppermute x6, starting transfers between devices, to_others(): lax.ppermute(messages[d], 'rep', [(s, (s + d) % count) for s in range(cou...  19.1 us
    all_to_all x1, starting transfers between devices, per_device(): lax.all_to_all(update_panels.reshape(panels * shards, rows, LANES), ('rep...  16.3 us
    all_to_all x1, blocking collectives, per_device(): lax.all_to_all(message, 'rep', split_axis=0, concat_axis=0, tiled=True)  13.9 us
    ppermute x6, waiting for transfers between devices, to_others(): lax.ppermute(messages[d], 'rep', [(s, (s + d) % count) for s in range(cou...  11.4 us
    all_to_all x1, waiting for transfers between devices, per_device(): lax.all_to_all(outgoing, 'shard', split_axis=0, concat_axis=0, tiled=True)  11 us
    pallas_call x1, Pallas kernels, per_device(): pl.pallas_call(pack_kernel, out_shape=(jax.ShapeDtypeStruct((classes, cou...  4.43 us
  transfers between devices with their start and end apart: 8, of which 2 were waited for; matrix products, arithmetic and copies ran while one was open for 0% of the time, Pallas kernels for 1%

profile of v3, /device:TPU:1, one launch (start us, length us, event | category | flops | bytes accessed | tf_op | source)
XLA Modules:
  0.0 108.5 jit_solution(15331013458103990519)
XLA Ops:
  0.6 4.4 %pack.1 = (bf16[4,56,16,128]{3,2,1,0:T(8,128)(2,1)}, s32[1,256]{1,0:T(1,128)}, s32[1,224]{1,0:T(1,128)}, bf16[8,128,128]{2,1,0:T(8,128)(2,1)}, bf16[8,128,128]{2...) custom-call(s32[1,224]{1,0:T(1,128)} %bitcast.25, bf16[224,16,128]{2,1,0:T(8,128)(2,1)} %bitcast.22, ...), custom_call_target="tpu_custom_call" | custom-call | tf_op jit(solution)/shard_map/pack/pallas_call | solution.py:231
  5.1 13.9 %all_to_all.15.in_ref = bf16[4,56,16,128]{3,2,1,0:T(8,128)(2,1)S(1)} all-to-all(bf16[4,56,16,128]{3,2,1,0:T(8,128)(2,1)} %get-tuple-element.19), channel_id=1, replica_groups=mesh['rep'=4,'shard'=128] {'rep'}, dimensions={0} | all-to-all | bytes 1835008 | tf_op jit(solution)/shard_map/all_to_all | solution.py:260
  19.0 0.0 copy-start.3
  19.0 0.7 copy-done.3
  19.6 1.5 %spread.1 = bf16[128,16,128]{2,1,0:T(8,128)(2,1)} custom-call(s32[1,256]{1,0:T(1,128)S(1)} %copy-done.3, bf16[4,56,16,128]{3,2,1,0:T(8,128)(2,1)S(1)} %all_to_all.15.in_ref), custom_call_target="tpu_custom_call" | custom-call | tf_op jit(solution)/shard_map/spread/pallas_call | solution.py:262
  21.2 0.0 copy-start.7
  21.2 0.0 copy-start.6
  21.2 0.0 copy-start.5
  21.2 22.7 %all-to-all-start.1 = ((bf16[128,16,128]{2,1,0:T(8,128)(2,1)}), bf16[128,16,128]{2,1,0:T(8,128)(2,1)S(1)}, u32[]{:S(2)}, u32[]{:S(2)}) async-start(bf16[128,16,128]{2,1,0:T(8,128)(2,1)} %spread.1), calls=%async_computation.1 | async-start | bytes 1048576 | tf_op jit(solution)/shard_map/all_to_all | solution.py:276
  43.9 0.0 copy-done.7
  43.9 2.2 %collective-permute-start = (bf16[8,128,128]{2,1,0:T(8,128)(2,1)S(1)}, bf16[8,128,128]{2,1,0:T(8,128)(2,1)S(1)}, u32[]{:S(2)}, u32[]{:S(2)}) collective-permute-start(bf16[8,128,128]{2,1,0:T(8,128)(2,1)S(1)} %copy-done.7), channel_id=1, source_target_pairs={{0,128},{128,256},{256,384},{384,0},{1,129},{129,257},{257,385},{3... | collective-permute-start | bytes 786440 | tf_op jit(solution)/shard_map/ppermute | solution.py:212
  46.1 0.0 copy-done.6
  46.1 3.7 %collective-permute-start.1 = (bf16[8,128,128]{2,1,0:T(8,128)(2,1)S(1)}, bf16[8,128,128]{2,1,0:T(8,128)(2,1)S(1)}, u32[]{:S(2)}, u32[]{:S(2)}) collective-permute-start(bf16[8,128,128]{2,1,0:T(8,128)(2,1)S(1)} %copy-done.6), channel_id=1, source_target_pairs={{0,256},{128,384},{256,0},{384,128},{1,257},{129,385},{257,1},{385... | collective-permute-start | bytes 786440 | tf_op jit(solution)/shard_map/ppermute | solution.py:212
  49.8 0.0 copy-done.5
  49.8 2.5 %collective-permute-start.2 = (bf16[8,128,128]{2,1,0:T(8,128)(2,1)S(1)}, bf16[8,128,128]{2,1,0:T(8,128)(2,1)S(1)}, u32[]{:S(2)}, u32[]{:S(2)}) collective-permute-start(bf16[8,128,128]{2,1,0:T(8,128)(2,1)S(1)} %copy-done.5), channel_id=1, source_target_pairs={{0,384},{128,0},{256,128},{384,256},{1,385},{129,1},{257,129},{385... | collective-permute-start | bytes 786440 | tf_op jit(solution)/shard_map/ppermute | solution.py:212
  52.3 11.0 %all-to-all-done.1 = bf16[128,16,128]{2,1,0:T(8,128)(2,1)S(1)} async-done(((bf16[128,16,128]{2,1,0:T(8,128)(2,1)}), bf16[128,16,128]{2,1,0:T(8,128)(2,1)S(1)}, u32[]{:S(2)}, u32[]{:S(2)}) %all-to-all-start.1) | async-done | bytes 524320 | tf_op jit(solution)/shard_map/all_to_all | solution.py:276
  63.3 0.0 copy-start.2
  63.3 0.2 copy.10
  63.5 0.0 collective-permute-done.rest_1_
  63.5 0.0 collective-permute-done.1.rest_2_
  63.6 0.0 collective-permute-done.2.rest_3_
  63.6 0.7 copy-done.2
  64.3 1.8 %update.1 = bf16[4,512,128]{2,1,0:T(8,128)(2,1)} custom-call(bf16[4,512,128]{2,1,0:T(8,128)(2,1)S(1)} %bitcast.17, bf16[8,128,128]{2,1,0:T(8,128)(2,1)S(1)} %copy-done.2, bf16[8,128,128]{2,1,0:T(8,128)(2,1)S(1)} %collective-permute-done.rest_1_, bf16[8,128,128]{2,1,0:T(8,128)(2,1)S(1)} %collective-permute-done.1.rest_2_, ...), custom_call_target="tpu_custom_call" | custom-call | flops 536870912 | bytes 2097152 | tf_op jit(solution)/shard_map/update/pallas_call | solution.py:280
  66.1 16.3 %all-to-all-start.2 = ((bf16[512,4,128]{2,1,0:T(4,128)(2,1)}), bf16[512,4,128]{2,1,0:T(4,128)(2,1)S(1)}, u32[]{:S(2)}, u32[]{:S(2)}) async-start(bf16[512,4,128]{2,1,0:T(4,128)(2,1)} %bitcast.9), calls=%async_computation.2 | async-start | bytes 1048576 | tf_op jit(solution)/shard_map/all_to_all | solution.py:303
  82.4 0.0 copy-start
  82.5 0.0 copy-start.1
  82.5 1.1 %products.1 = (bf16[2,128,512]{2,1,0:T(8,128)(2,1)S(1)}, bf16[2,128,512]{2,1,0:T(8,128)(2,1)S(1)}, bf16[2,128,512]{2,1,0:T(8,128)(2,1)S(1)}, bf16[2,128,512]{2,1,0:T(8,128)(2,1)S(1)}) custom-call(bf16[4,512,128]{2,1,0:T(8,128)(2,1)S(1)} %bitcast.18), custom_call_target="tpu_custom_call" | custom-call | flops 536870912 | bytes 1572864 | tf_op jit(solution)/shard_map/products/pallas_call | solution.py:294
  83.6 3.3 %collective-permute-start.3 = (bf16[2,128,512]{2,1,0:T(8,128)(2,1)S(1)}, bf16[2,128,512]{2,1,0:T(8,128)(2,1)S(1)}, u32[]{:S(2)}, u32[]{:S(2)}) collective-permute-start(bf16[2,128,512]{2,1,0:T(8,128)(2,1)S(1)} %get-tuple-element.25), channel_id=1, source_target_pairs={{0,128},{128,256},{256,384},{384,0},{1,129},{129,257},{257,385},{3... | collective-permute-start | bytes 786440 | tf_op jit(solution)/shard_map/ppermute | solution.py:212
  86.9 4.3 %collective-permute-start.4 = (bf16[2,128,512]{2,1,0:T(8,128)(2,1)S(1)}, bf16[2,128,512]{2,1,0:T(8,128)(2,1)S(1)}, u32[]{:S(2)}, u32[]{:S(2)}) collective-permute-start(bf16[2,128,512]{2,1,0:T(8,128)(2,1)S(1)} %get-tuple-element.26), channel_id=1, source_target_pairs={{0,256},{128,384},{256,0},{384,128},{1,257},{129,385},{257,1},{385... | collective-permute-start | bytes 786440 | tf_op jit(solution)/shard_map/ppermute | solution.py:212
  91.2 3.1 %collective-permute-start.5 = (bf16[2,128,512]{2,1,0:T(8,128)(2,1)S(1)}, bf16[2,128,512]{2,1,0:T(8,128)(2,1)S(1)}, u32[]{:S(2)}, u32[]{:S(2)}) collective-permute-start(bf16[2,128,512]{2,1,0:T(8,128)(2,1)S(1)} %get-tuple-element.27), channel_id=1, source_target_pairs={{0,384},{128,0},{256,128},{384,256},{1,385},{129,1},{257,129},{385... | collective-permute-start | bytes 786440 | tf_op jit(solution)/shard_map/ppermute | solution.py:212
  94.3 0.0 collective-permute-done.3.rest_1_
  94.3 11.4 %collective-permute-done.4.rest_2_ = bf16[2,128,512]{2,1,0:T(8,128)(2,1)S(1)} collective-permute-done((bf16[2,128,512]{2,1,0:T(8,128)(2,1)S(1)}, bf16[2,128,512]{2,1,0:T(8,128)(2,1)S(1)}, u32[]{:S(2)}, u32[]{:S(2)}) %collective-permute-start.4) | collective-permute-done | bytes 262176 | tf_op jit(solution)/shard_map/ppermute | solution.py:212
  105.7 0.0 collective-permute-done.5.rest_3_
  105.7 0.0 all-to-all-done.2.in_ref
  105.7 0.0 copy-start.4
  105.7 0.0 copy-done
  105.7 0.0 copy-done.1
  105.7 0.6 copy-done.4
  106.4 2.1 %finish.1 = (bf16[4,128,512]{2,1,0:T(8,128)(2,1)}, bf16[4,128,512]{2,1,0:T(8,128)(2,1)}, bf16[224,4,128]{2,1,0:T(4,128)(2,1)}) custom-call(s32[1,256]{1,0:T(1,128)S(1)} %copy-done.3, s32[1,224]{1,0:T(1,128)S(1)} %copy-done.4, bf16[512,4,128]{2,1,0:T(4,128)(2,1)S(1)} %all-to-all-done.2.in_ref, bf16[4,128,512]{2,1,0:T(8,128)(2,1)S(1)} %bitcast.19, ...), custom_call_target="tpu_custom_call" | custom-call | flops 2097152 | bytes 4194304 | tf_op jit(solution)/shard_map/finish/pallas_call | solution.py:311
Async XLA Ops:
  19.0 0.7 copy-start.3
  21.2 22.7 %copy-start.7 = (bf16[8,128,128]{2,1,0:T(8,128)(2,1)S(1)}, bf16[8,128,128]{2,1,0:T(8,128)(2,1)}, u32[]{:S(2)}) copy-start(bf16[8,128,128]{2,1,0:T(8,128)(2,1)} %get-tuple-element.21) | copy-start | bytes 786436
  21.2 24.9 %copy-start.6 = (bf16[8,128,128]{2,1,0:T(8,128)(2,1)S(1)}, bf16[8,128,128]{2,1,0:T(8,128)(2,1)}, u32[]{:S(2)}) copy-start(bf16[8,128,128]{2,1,0:T(8,128)(2,1)} %get-tuple-element.22) | copy-start | bytes 786436
  21.2 28.6 %copy-start.5 = (bf16[8,128,128]{2,1,0:T(8,128)(2,1)S(1)}, bf16[8,128,128]{2,1,0:T(8,128)(2,1)}, u32[]{:S(2)}) copy-start(bf16[8,128,128]{2,1,0:T(8,128)(2,1)} %get-tuple-element.23) | copy-start | bytes 786436
  21.2 42.1 %all-to-all-start.1 = ((bf16[128,16,128]{2,1,0:T(8,128)(2,1)}), bf16[128,16,128]{2,1,0:T(8,128)(2,1)S(1)}, u32[]{:S(2)}, u32[]{:S(2)}) async-start(bf16[128,16,128]{2,1,0:T(8,128)(2,1)} %spread.1), calls=%async_computation.1 | async-start | bytes 1048576 | tf_op jit(solution)/shard_map/all_to_all | solution.py:276
  43.9 19.6 %collective-permute-start = (bf16[8,128,128]{2,1,0:T(8,128)(2,1)S(1)}, bf16[8,128,128]{2,1,0:T(8,128)(2,1)S(1)}, u32[]{:S(2)}, u32[]{:S(2)}) collective-permute-start(bf16[8,128,128]{2,1,0:T(8,128)(2,1)S(1)} %copy-done.7), channel_id=1, source_target_pairs={{0,128},{128,256},{256,384},{384,0},{1,129},{129,257},{257,385},{3... | collective-permute-start | bytes 786440 | tf_op jit(solution)/shard_map/ppermute | solution.py:212
  46.1 17.4 %collective-permute-start.1 = (bf16[8,128,128]{2,1,0:T(8,128)(2,1)S(1)}, bf16[8,128,128]{2,1,0:T(8,128)(2,1)S(1)}, u32[]{:S(2)}, u32[]{:S(2)}) collective-permute-start(bf16[8,128,128]{2,1,0:T(8,128)(2,1)S(1)} %copy-done.6), channel_id=1, source_target_pairs={{0,256},{128,384},{256,0},{384,128},{1,257},{129,385},{257,1},{385... | collective-permute-start | bytes 786440 | tf_op jit(solution)/shard_map/ppermute | solution.py:212
  49.8 13.7 %collective-permute-start.2 = (bf16[8,128,128]{2,1,0:T(8,128)(2,1)S(1)}, bf16[8,128,128]{2,1,0:T(8,128)(2,1)S(1)}, u32[]{:S(2)}, u32[]{:S(2)}) collective-permute-start(bf16[8,128,128]{2,1,0:T(8,128)(2,1)S(1)} %copy-done.5), channel_id=1, source_target_pairs={{0,384},{128,0},{256,128},{384,256},{1,385},{129,1},{257,129},{385... | collective-permute-start | bytes 786440 | tf_op jit(solution)/shard_map/ppermute | solution.py:212
  63.3 1.0 copy-start.2
  66.1 39.6 %all-to-all-start.2 = ((bf16[512,4,128]{2,1,0:T(4,128)(2,1)}), bf16[512,4,128]{2,1,0:T(4,128)(2,1)S(1)}, u32[]{:S(2)}, u32[]{:S(2)}) async-start(bf16[512,4,128]{2,1,0:T(4,128)(2,1)} %bitcast.9), calls=%async_computation.2 | async-start | bytes 1048576 | tf_op jit(solution)/shard_map/all_to_all | solution.py:303
  82.4 23.3 %copy-start = (bf16[1,4,128,512]{3,2,1,0:T(8,128)(2,1)S(1)}, bf16[1,4,128,512]{3,2,1,0:T(8,128)(2,1)}, u32[]{:S(2)}) copy-start(bf16[1,4,128,512]{3,2,1,0:T(8,128)(2,1)} %param.8) | copy-start | bytes 1572868
  82.5 23.3 %copy-start.1 = (bf16[1,4,128,512]{3,2,1,0:T(8,128)(2,1)S(1)}, bf16[1,4,128,512]{3,2,1,0:T(8,128)(2,1)}, u32[]{:S(2)}) copy-start(bf16[1,4,128,512]{3,2,1,0:T(8,128)(2,1)} %param.9) | copy-start | bytes 1572868
  83.6 10.7 %collective-permute-start.3 = (bf16[2,128,512]{2,1,0:T(8,128)(2,1)S(1)}, bf16[2,128,512]{2,1,0:T(8,128)(2,1)S(1)}, u32[]{:S(2)}, u32[]{:S(2)}) collective-permute-start(bf16[2,128,512]{2,1,0:T(8,128)(2,1)S(1)} %get-tuple-element.25), channel_id=1, source_target_pairs={{0,128},{128,256},{256,384},{384,0},{1,129},{129,257},{257,385},{3... | collective-permute-start | bytes 786440 | tf_op jit(solution)/shard_map/ppermute | solution.py:212
  86.9 18.8 %collective-permute-start.4 = (bf16[2,128,512]{2,1,0:T(8,128)(2,1)S(1)}, bf16[2,128,512]{2,1,0:T(8,128)(2,1)S(1)}, u32[]{:S(2)}, u32[]{:S(2)}) collective-permute-start(bf16[2,128,512]{2,1,0:T(8,128)(2,1)S(1)} %get-tuple-element.26), channel_id=1, source_target_pairs={{0,256},{128,384},{256,0},{384,128},{1,257},{129,385},{257,1},{385... | collective-permute-start | bytes 786440 | tf_op jit(solution)/shard_map/ppermute | solution.py:212
  91.2 14.5 %collective-permute-start.5 = (bf16[2,128,512]{2,1,0:T(8,128)(2,1)S(1)}, bf16[2,128,512]{2,1,0:T(8,128)(2,1)S(1)}, u32[]{:S(2)}, u32[]{:S(2)}) collective-permute-start(bf16[2,128,512]{2,1,0:T(8,128)(2,1)S(1)} %get-tuple-element.27), channel_id=1, source_target_pairs={{0,384},{128,0},{256,128},{384,256},{1,385},{129,1},{257,129},{385... | collective-permute-start | bytes 786440 | tf_op jit(solution)/shard_map/ppermute | solution.py:212
  105.7 0.7 copy-start.4

commit v4 on v3

--- a/solution.py
+++ b/solution.py
@@ -13,6 +13,8 @@
 BF16 = jnp.bfloat16
 LANES = 128
 TILE = 16
+PLACES = 256
+OFFSETS = (2, 3, 1, 0)
 
 
 def params(limit=LIMIT):
@@ -31,7 +33,11 @@
     return pl.BlockSpec(memory_space=pl.ANY)
 
 
-def pack_kernel(owners_ref, part_ref, left_ref, right_ref, out_ref, plan_ref, source_ref, *rest):
+def in_hbm():
+    return pl.BlockSpec(memory_space=pltpu.HBM)
+
+
+def pack_kernel(owners_ref, part_ref, left_ref, right_ref, out_ref, plan_ref, *rest):
     factor_outs = rest[:-14]
     part, message, left, factors, owners, lanes, place, place_at, plan, source = rest[-14:-4]
     in_sems, right_sems, out_sems, sems = rest[-4:]
@@ -71,14 +77,14 @@
     bring = pltpu.make_async_copy(place, place_at, sems.at[2])
     bring.start()
     slots, load_rights = [], []
-    for d in range(classes):
+    for n, d in enumerate(OFFSETS):
         slots.append(lax.rem(lax.rem(replica + d, classes) + classes - base, classes))
         load_rights.append(
-            pltpu.make_async_copy(right_ref.at[slots[d]], factors.at[d, pl.ds(panels, panels)], right_sems.at[d])
+            pltpu.make_async_copy(right_ref.at[slots[n]], factors.at[n, pl.ds(panels, panels)], right_sems.at[n])
         )
-        load_rights[d].start()
-    source[...] = cls * lax.axis_size("shard") + owner
-    stores = [pltpu.make_async_copy(source, source_ref, sems.at[3])]
+        load_rights[n].start()
+    source[:, pl.ds(0, blocks)] = cls * lax.axis_size("shard") + owner
+    stores = [pltpu.make_async_copy(source, plan_ref.at[:, pl.ds(PLACES, PLACES)], sems.at[3])]
     stores[0].start()
     load_left.wait()
     for d, factor_out in enumerate(factor_outs):
@@ -98,7 +104,7 @@
         return 0
 
     lax.fori_loop(0, blocks, move, 0, unroll=8)
-    stores.append(pltpu.make_async_copy(plan, plan_ref, sems.at[4]))
+    stores.append(pltpu.make_async_copy(plan, plan_ref.at[:, pl.ds(0, PLACES)], sems.at[4]))
     stores[-1].start()
     for c in range(classes):
         stores.append(pltpu.make_async_copy(message.at[pl.ds(c * count, count)], out_ref.at[c], out_sems.at[c]))
@@ -108,7 +114,7 @@
 
 
 def spread_kernel(plan_ref, in_ref, out_ref, spread, plan, sems, sem):
-    load = pltpu.make_async_copy(plan_ref, plan, sem)
+    load = pltpu.make_async_copy(plan_ref.at[:, pl.ds(0, PLACES)], plan, sem)
     load.start()
     spread[...] = jnp.zeros_like(spread)
     classes, count = in_ref.shape[:2]
@@ -134,13 +140,14 @@
         store.wait()
 
 
-def update_kernel(grad_ref, *rest):
+def update_kernel(grad_ref, after_ref, *rest):
+    del after_ref
     factor_refs = rest[:-4]
     out_ref, product, held, sems = rest[-4:]
     panels, width, _ = grad_ref.shape
     rows = width // panels
     replica = lax.axis_index("rep")
-    sources = [lax.rem(replica + panels - d, panels) for d in range(panels)]
+    sources = [lax.rem(replica + panels - d, panels) for d in OFFSETS]
     grad = jnp.concatenate([grad_ref[c] for c in range(panels)], axis=1)
     for d, factor_ref in enumerate(factor_refs):
         left = jnp.concatenate([factor_ref[h] for h in range(panels)], axis=1)
@@ -164,7 +171,7 @@
     rows = width // panels
     replica = lax.axis_index("rep")
     grad = jnp.concatenate([grad_ref[c] for c in range(panels)], axis=1)
-    for d, out_ref in enumerate(out_refs):
+    for d, out_ref in zip(OFFSETS, out_refs, strict=True):
         to = lax.rem(replica + d, panels)
         start = pl.multiple_of(to * rows, rows)
         own_rows = jnp.concatenate([grad_ref[c, pl.ds(start, rows), :] for c in range(panels)], axis=1)
@@ -174,32 +181,29 @@
         out_ref[1] = right.astype(out_ref.dtype)
 
 
-def finish_kernel(plan_ref, source_ref, in_ref, left_ref, right_ref, *rest):
-    product_refs = rest[:-10]
-    left_out, right_out, update_out, lefts, rights, update, plan, source, sems, in_sems = rest[-10:]
+def finish_kernel(plan_ref, in_ref, left_ref, right_ref, *rest):
+    product_refs = rest[:-9]
+    left_out, right_out, update_out, lefts, rights, update, plan, sems, in_sem = rest[-9:]
     slots = left_ref.shape[0]
     blocks = update.shape[0]
     replica = lax.axis_index("rep")
-    load_plan = pltpu.make_async_copy(plan_ref, plan, in_sems.at[0])
-    load_source = pltpu.make_async_copy(source_ref, source, in_sems.at[1])
-    load_plan.start()
-    load_source.start()
-    load_plan.wait()
-    load_source.wait()
+    load = pltpu.make_async_copy(plan_ref.at[:, pl.ds(0, 2 * PLACES)], plan, in_sem)
+    load.start()
+    load.wait()
     base = plan[0, blocks]
 
     def move(b, _):
-        update[b] = in_ref[source[0, b]]
+        update[b] = in_ref[plan[0, PLACES + b]]
         return 0
 
     lax.fori_loop(0, blocks, move, 0, unroll=8)
     stores = [pltpu.make_async_copy(update, update_out, sems.at[0])]
     stores[0].start()
-    for d, product_ref in enumerate(product_refs):
+    for i, (d, product_ref) in enumerate(zip(OFFSETS, product_refs, strict=True)):
         k = lax.rem(lax.rem(replica + slots - d, slots) + slots - base, slots)
         for n, (old, new, out) in enumerate(((left_ref, lefts, left_out), (right_ref, rights, right_out))):
-            new[d] = (0.9 * old[k].astype(F32) + 0.1 * product_ref[n].astype(F32)).astype(new.dtype)
-            stores.append(pltpu.make_async_copy(new.at[d], out.at[k], sems.at[len(stores)]))
+            new[i] = (0.9 * old[k].astype(F32) + 0.1 * product_ref[n].astype(F32)).astype(new.dtype)
+            stores.append(pltpu.make_async_copy(new.at[i], out.at[k], sems.at[len(stores)]))
             stores[-1].start()
     for store in stores:
         store.wait()
@@ -207,10 +211,10 @@
 
 def to_others(messages):
     count = len(messages)
-    sent = list(messages)
-    for d in sorted(range(1, count), key=lambda d: -min(d, count - d)):
-        sent[d] = lax.ppermute(messages[d], "rep", [(s, (s + d) % count) for s in range(count)])
-    return sent
+    return [
+        lax.ppermute(message, "rep", [(s, (s + d) % count) for s in range(count)]) if d else message
+        for message, d in zip(messages, OFFSETS, strict=True)
+    ]
 
 
 def per_device(partials, owners, left_stat, right_stat, left_factor, right_factor):
@@ -228,16 +232,15 @@
     )
     right_tiles = right_factor[0].reshape(slots, panels, LANES, LANES)
     factor_message = jax.ShapeDtypeStruct((2 * panels, LANES, LANES), BF16)
-    message, plan, source, *factors = pl.pallas_call(
+    message, plan, *factors = pl.pallas_call(
         pack_kernel,
         out_shape=(
             jax.ShapeDtypeStruct((classes, count, TILE, LANES), BF16),
-            jax.ShapeDtypeStruct((1, 2 * LANES), jnp.int32),
-            jax.ShapeDtypeStruct((1, blocks), jnp.int32),
+            jax.ShapeDtypeStruct((1, 2 * PLACES), jnp.int32),
             *[factor_message] * classes,
         ),
         in_specs=[anywhere()] * 4,
-        out_specs=[anywhere()] * (3 + classes),
+        out_specs=[anywhere()] * (2 + classes),
         scratch_shapes=[
             VMEM((blocks, TILE, LANES), BF16),
             VMEM((blocks, TILE, LANES), BF16),
@@ -247,8 +250,8 @@
             VMEM((1, blocks), jnp.int32),
             VMEM((1, blocks), jnp.int32),
             SMEM((1, blocks), jnp.int32),
-            SMEM((1, 2 * LANES), jnp.int32),
-            VMEM((1, blocks), jnp.int32),
+            SMEM((1, PLACES), jnp.int32),
+            VMEM((1, PLACES), jnp.int32),
             pltpu.SemaphoreType.DMA((classes + 1,)),
             pltpu.SemaphoreType.DMA((classes,)),
             pltpu.SemaphoreType.DMA((2 * classes,)),
@@ -262,11 +265,11 @@
     outgoing = pl.pallas_call(
         spread_kernel,
         out_shape=jax.ShapeDtypeStruct((shards, TILE, LANES), BF16),
-        in_specs=[anywhere(), in_vmem()],
+        in_specs=[in_hbm(), in_vmem()],
         out_specs=anywhere(),
         scratch_shapes=[
             VMEM((shards, TILE, LANES), BF16),
-            SMEM((1, 2 * LANES), jnp.int32),
+            SMEM((1, PLACES), jnp.int32),
             pltpu.SemaphoreType.DMA((4,)),
             pltpu.SemaphoreType.DMA,
         ],
@@ -277,10 +280,19 @@
     grad = (
         incoming.reshape(shards, panels, rows, LANES).transpose(1, 0, 2, 3).reshape(panels, width, LANES)
     )
+    products = pl.pallas_call(
+        products_kernel,
+        out_shape=[jax.ShapeDtypeStruct((2, quarter, width), BF16)] * classes,
+        in_specs=[in_vmem()],
+        out_specs=[in_vmem()] * classes,
+        compiler_params=params(),
+        cost_estimate=pl.CostEstimate(flops=4 * width**3, bytes_accessed=6 * width**2, transcendentals=0),
+        name="products",
+    )(grad)
     update_panels = pl.pallas_call(
         update_kernel,
         out_shape=jax.ShapeDtypeStruct((panels, width, LANES), BF16),
-        in_specs=[in_vmem()] * (1 + classes),
+        in_specs=[in_vmem(), anywhere()] + [in_vmem()] * classes,
         out_specs=anywhere(),
         scratch_shapes=[
             VMEM((width, width), BF16),
@@ -290,16 +302,7 @@
         compiler_params=params(),
         cost_estimate=pl.CostEstimate(flops=4 * width**3, bytes_accessed=8 * width**2, transcendentals=0),
         name="update",
-    )(grad, *factors)
-    products = pl.pallas_call(
-        products_kernel,
-        out_shape=[jax.ShapeDtypeStruct((2, quarter, width), BF16)] * classes,
-        in_specs=[in_vmem()],
-        out_specs=[in_vmem()] * classes,
-        compiler_params=params(),
-        cost_estimate=pl.CostEstimate(flops=4 * width**3, bytes_accessed=6 * width**2, transcendentals=0),
-        name="products",
-    )(grad)
+    )(grad, products[-1], *factors)
     returned = lax.all_to_all(
         update_panels.reshape(panels * shards, rows, LANES),
         ("rep", "shard"),
@@ -315,23 +318,22 @@
             jax.ShapeDtypeStruct(right_stat.shape[1:], BF16),
             jax.ShapeDtypeStruct((blocks, rows, LANES), BF16),
         ),
-        in_specs=[anywhere()] * 2 + [in_vmem()] * (3 + classes),
+        in_specs=[in_hbm()] + [in_vmem()] * (3 + classes),
         out_specs=(anywhere(), anywhere(), anywhere()),
         scratch_shapes=[
             VMEM((slots, quarter, width), BF16),
             VMEM((slots, quarter, width), BF16),
             VMEM((blocks, rows, LANES), BF16),
-            SMEM((1, 2 * LANES), jnp.int32),
-            SMEM((1, blocks), jnp.int32),
+            SMEM((1, 2 * PLACES), jnp.int32),
             pltpu.SemaphoreType.DMA((2 * slots + 1,)),
-            pltpu.SemaphoreType.DMA((2,)),
+            pltpu.SemaphoreType.DMA,
         ],
         compiler_params=params(),
         cost_estimate=pl.CostEstimate(
             flops=8 * slots * quarter * width, bytes_accessed=16 * slots * quarter * width, transcendentals=0
         ),
         name="finish",
-    )(plan, source, returned, left_stat[0], right_stat[0], *products)
+    )(plan, returned, left_stat[0], right_stat[0], *products)
     return left_new[None], right_new[None], update
 
 

time: 109 us -> 103 us (0.945)
  starting transfers between devices: 58.1 us -> 53.4 us
  local copies, waits for them, and re-layouts: 2.26 us -> 0.22 us
    all_to_all x1, starting transfers between devices: 16.3 us -> 12.2 us  [per_device(): lax.all_to_all(update_panels.reshape(panels * shards, rows, LANES), ('rep...]
    unnamed x16 -> x14, local copies, waits for them, and re-layouts: 2.08 us -> 0.04 us
  transfers between devices with their start and end apart: 8 -> 8, of which waited for: 2 -> 4; matrix products, arithmetic and copies ran while one was open for 0% -> 0% of each run, Pallas kernels for 1% -> 1%
where the time goes in v4:
time: 103 us
  starting transfers between devices  53.4 us (52%)
  waiting for transfers between devices  23.2 us (23%)
  blocking collectives  13.9 us (13%)
  Pallas kernels  11 us (11%)
    all_to_all x1, starting transfers between devices, per_device(): lax.all_to_all(outgoing, 'shard', split_axis=0, concat_axis=0, tiled=True)  22.7 us
    ppermute x6, starting transfers between devices, to_others(): lax.ppermute(message, 'rep', [(s, (s + d) % count) for s in range(count)])  18.5 us
    all_to_all x1, blocking collectives, per_device(): lax.all_to_all(message, 'rep', split_axis=0, concat_axis=0, tiled=True)  13.9 us
    all_to_all x1, starting transfers between devices, per_device(): lax.all_to_all(update_panels.reshape(panels * shards, rows, LANES), ('rep...  12.2 us
    ppermute x6, waiting for transfers between devices, to_others(): lax.ppermute(message, 'rep', [(s, (s + d) % count) for s in range(count)])  12.2 us
    all_to_all x1, waiting for transfers between devices, per_device(): lax.all_to_all(outgoing, 'shard', split_axis=0, concat_axis=0, tiled=True)  11 us
    pallas_call x1, Pallas kernels, per_device(): pl.pallas_call(pack_kernel, out_shape=(jax.ShapeDtypeStruct((classes, cou...  4.43 us
    pallas_call x1, Pallas kernels, per_device(): pl.pallas_call(finish_kernel, out_shape=(jax.ShapeDtypeStruct(left_stat.s...  2.11 us
  transfers between devices with their start and end apart: 8, of which 4 were waited for; matrix products, arithmetic and copies ran while one was open for 0% of the time, Pallas kernels for 1%

profile of v4, /device:TPU:1, one launch (start us, length us, event | category | flops | bytes accessed | tf_op | source)
XLA Modules:
  0.0 102.6 jit_solution(134707207406175035)
XLA Ops:
  0.6 4.4 %pack.1 = (bf16[4,56,16,128]{3,2,1,0:T(8,128)(2,1)}, s32[1,512]{1,0:T(1,128)}, bf16[8,128,128]{2,1,0:T(8,128)(2,1)}, bf16[8,128,128]{2,1,0:T(8,128)(2,1)}, bf16[...) custom-call(s32[1,224]{1,0:T(1,128)} %bitcast.25, bf16[224,16,128]{2,1,0:T(8,128)(2,1)} %bitcast.22, ...), custom_call_target="tpu_custom_call" | custom-call | tf_op jit(solution)/shard_map/pack/pallas_call | solution.py:235
  5.1 0.0 copy-start.3
  5.1 13.9 %all_to_all.15.in_ref = bf16[4,56,16,128]{3,2,1,0:T(8,128)(2,1)S(1)} all-to-all(bf16[4,56,16,128]{3,2,1,0:T(8,128)(2,1)} %get-tuple-element.17), channel_id=1, replica_groups=mesh['rep'=4,'shard'=128] {'rep'}, dimensions={0} | all-to-all | bytes 1835008 | tf_op jit(solution)/shard_map/all_to_all | solution.py:263
  19.0 0.0 copy-done.3
  19.0 1.5 %spread.1 = bf16[128,16,128]{2,1,0:T(8,128)(2,1)} custom-call(s32[1,512]{1,0:T(1,128)S(1)} %copy-done.3, bf16[4,56,16,128]{3,2,1,0:T(8,128)(2,1)S(1)} %all_to_all.15.in_ref), custom_call_target="tpu_custom_call" | custom-call | tf_op jit(solution)/shard_map/spread/pallas_call | solution.py:265
  20.5 0.0 copy-start.6
  20.5 0.0 copy-start.5
  20.5 0.0 copy-start.4
  20.5 22.7 %all-to-all-start.1 = ((bf16[128,16,128]{2,1,0:T(8,128)(2,1)}), bf16[128,16,128]{2,1,0:T(8,128)(2,1)S(1)}, u32[]{:S(2)}, u32[]{:S(2)}) async-start(bf16[128,16,128]{2,1,0:T(8,128)(2,1)} %spread.1), calls=%async_computation.1 | async-start | bytes 1048576 | tf_op jit(solution)/shard_map/all_to_all | solution.py:279
  43.2 0.0 copy-done.6
  43.2 2.4 %collective-permute-start = (bf16[8,128,128]{2,1,0:T(8,128)(2,1)S(1)}, bf16[8,128,128]{2,1,0:T(8,128)(2,1)S(1)}, u32[]{:S(2)}, u32[]{:S(2)}) collective-permute-start(bf16[8,128,128]{2,1,0:T(8,128)(2,1)S(1)} %copy-done.6), channel_id=1, source_target_pairs={{0,256},{128,384},{256,0},{384,128},{1,257},{129,385},{257,1},{385... | collective-permute-start | bytes 786440 | tf_op jit(solution)/shard_map/ppermute | solution.py:215
  45.7 0.0 copy-done.5
  45.7 4.0 %collective-permute-start.1 = (bf16[8,128,128]{2,1,0:T(8,128)(2,1)S(1)}, bf16[8,128,128]{2,1,0:T(8,128)(2,1)S(1)}, u32[]{:S(2)}, u32[]{:S(2)}) collective-permute-start(bf16[8,128,128]{2,1,0:T(8,128)(2,1)S(1)} %copy-done.5), channel_id=1, source_target_pairs={{0,384},{128,0},{256,128},{384,256},{1,385},{129,1},{257,129},{385... | collective-permute-start | bytes 786440 | tf_op jit(solution)/shard_map/ppermute | solution.py:215
  49.7 0.0 copy-done.4
  49.7 1.9 %collective-permute-start.2 = (bf16[8,128,128]{2,1,0:T(8,128)(2,1)S(1)}, bf16[8,128,128]{2,1,0:T(8,128)(2,1)S(1)}, u32[]{:S(2)}, u32[]{:S(2)}) collective-permute-start(bf16[8,128,128]{2,1,0:T(8,128)(2,1)S(1)} %copy-done.4), channel_id=1, source_target_pairs={{0,128},{128,256},{256,384},{384,0},{1,129},{129,257},{257,385},{3... | collective-permute-start | bytes 786440 | tf_op jit(solution)/shard_map/ppermute | solution.py:215
  51.7 11.0 %all-to-all-done.1 = bf16[128,16,128]{2,1,0:T(8,128)(2,1)S(1)} async-done(((bf16[128,16,128]{2,1,0:T(8,128)(2,1)}), bf16[128,16,128]{2,1,0:T(8,128)(2,1)S(1)}, u32[]{:S(2)}, u32[]{:S(2)}) %all-to-all-start.1) | async-done | bytes 524320 | tf_op jit(solution)/shard_map/all_to_all | solution.py:279
  62.7 0.2 copy.10
  62.9 0.0 copy-start.2
  62.9 1.1 %products.1 = (bf16[2,128,512]{2,1,0:T(8,128)(2,1)S(1)}, bf16[2,128,512]{2,1,0:T(8,128)(2,1)S(1)}, bf16[2,128,512]{2,1,0:T(8,128)(2,1)S(1)}, bf16[2,128,512]{2,1,0:T(8,128)(2,1)S(1)}) custom-call(bf16[4,512,128]{2,1,0:T(8,128)(2,1)S(1)} %bitcast.17), custom_call_target="tpu_custom_call" | custom-call | flops 536870912 | bytes 1572864 | tf_op jit(solution)/shard_map/products/pallas_call | solution.py:283
  64.0 0.0 collective-permute-done.rest_0_
  64.0 0.0 collective-permute-done.1.rest_1_
  64.0 0.0 collective-permute-done.2.rest_2_
  64.0 0.0 copy-done.2
  64.0 1.8 %update.1 = bf16[4,512,128]{2,1,0:T(8,128)(2,1)} custom-call(bf16[4,512,128]{2,1,0:T(8,128)(2,1)S(1)} %bitcast.18, bf16[2,128,512]{2,1,0:T(8,128)(2,1)S(1)} %get-tuple-element.18.after_ref.rest_3_, bf16[8,128,128]{2,1,0:T(8,128)(2,1)S(1)} %collective-permute-done.rest_0_, bf16[8,128,128]{2,1,0:T(8,128)(2,1)S(1)} %collective-permute-done.1.rest_1_, ...), custom_call_target="tpu_custom_call" | custom-call | flops 536870912 | bytes 2097152 | tf_op jit(solution)/shard_map/update/pallas_call | solution.py:292
  65.9 0.0 copy-start
  65.9 0.0 copy-start.1
  65.9 12.2 %all-to-all-start.2 = ((bf16[512,4,128]{2,1,0:T(4,128)(2,1)}), bf16[512,4,128]{2,1,0:T(4,128)(2,1)S(1)}, u32[]{:S(2)}, u32[]{:S(2)}) async-start(bf16[512,4,128]{2,1,0:T(4,128)(2,1)} %bitcast.10), calls=%async_computation.2 | async-start | bytes 1048576 | tf_op jit(solution)/shard_map/all_to_all | solution.py:306
  78.1 4.8 %collective-permute-start.3 = (bf16[2,128,512]{2,1,0:T(8,128)(2,1)S(1)}, bf16[2,128,512]{2,1,0:T(8,128)(2,1)S(1)}, u32[]{:S(2)}, u32[]{:S(2)}) collective-permute-start(bf16[2,128,512]{2,1,0:T(8,128)(2,1)S(1)} %get-tuple-element.23), channel_id=1, source_target_pairs={{0,256},{128,384},{256,0},{384,128},{1,257},{129,385},{257,1},{385... | collective-permute-start | bytes 786440 | tf_op jit(solution)/shard_map/ppermute | solution.py:215
  82.9 2.8 %collective-permute-start.4 = (bf16[2,128,512]{2,1,0:T(8,128)(2,1)S(1)}, bf16[2,128,512]{2,1,0:T(8,128)(2,1)S(1)}, u32[]{:S(2)}, u32[]{:S(2)}) collective-permute-start(bf16[2,128,512]{2,1,0:T(8,128)(2,1)S(1)} %get-tuple-element.24), channel_id=1, source_target_pairs={{0,384},{128,0},{256,128},{384,256},{1,385},{129,1},{257,129},{385... | collective-permute-start | bytes 786440 | tf_op jit(solution)/shard_map/ppermute | solution.py:215
  85.7 2.5 %collective-permute-start.5 = (bf16[2,128,512]{2,1,0:T(8,128)(2,1)S(1)}, bf16[2,128,512]{2,1,0:T(8,128)(2,1)S(1)}, u32[]{:S(2)}, u32[]{:S(2)}) collective-permute-start(bf16[2,128,512]{2,1,0:T(8,128)(2,1)S(1)} %get-tuple-element.25), channel_id=1, source_target_pairs={{0,128},{128,256},{256,384},{384,0},{1,129},{129,257},{257,385},{3... | collective-permute-start | bytes 786440 | tf_op jit(solution)/shard_map/ppermute | solution.py:215
  88.2 2.7 %collective-permute-done.3.rest_0_ = bf16[2,128,512]{2,1,0:T(8,128)(2,1)S(1)} collective-permute-done((bf16[2,128,512]{2,1,0:T(8,128)(2,1)S(1)}, bf16[2,128,512]{2,1,0:T(8,128)(2,1)S(1)}, u32[]{:S(2)}, u32[]{:S(2)}) %collective-permute-start.3) | collective-permute-done | bytes 262176 | tf_op jit(solution)/shard_map/ppermute | solution.py:215
  90.9 8.8 %collective-permute-done.4.rest_1_ = bf16[2,128,512]{2,1,0:T(8,128)(2,1)S(1)} collective-permute-done((bf16[2,128,512]{2,1,0:T(8,128)(2,1)S(1)}, bf16[2,128,512]{2,1,0:T(8,128)(2,1)S(1)}, u32[]{:S(2)}, u32[]{:S(2)}) %collective-permute-start.4) | collective-permute-done | bytes 262176 | tf_op jit(solution)/shard_map/ppermute | solution.py:215
  99.7 0.7 collective-permute-done.5.rest_2_
  100.4 0.0 all-to-all-done.2.in_ref
  100.4 0.0 copy-done
  100.4 0.0 copy-done.1
  100.4 2.1 %finish.1 = (bf16[4,128,512]{2,1,0:T(8,128)(2,1)}, bf16[4,128,512]{2,1,0:T(8,128)(2,1)}, bf16[224,4,128]{2,1,0:T(4,128)(2,1)}) custom-call(s32[1,512]{1,0:T(1,128)S(1)} %copy-done.3, bf16[512,4,128]{2,1,0:T(4,128)(2,1)S(1)} %all-to-all-done.2.in_ref, bf16[4,128,512]{2,1,0:T(8,128)(2,1)S(1)} %bitcast.19, bf16[4,128,512]{2,1,0:T(8,128)(2,1)S(1)} %bitcast.20, ...), custom_call_target="tpu_custom_call" | custom-call | flops 2097152 | bytes 4194304 | tf_op jit(solution)/shard_map/finish/pallas_call | solution.py:314
Async XLA Ops:
  5.1 13.9 %copy-start.3 = (s32[1,512]{1,0:T(1,128)S(1)}, s32[1,512]{1,0:T(1,128)}, u32[]{:S(2)}) copy-start(s32[1,512]{1,0:T(1,128)} %get-tuple-element.16.plan_ref) | copy-start | bytes 6148
  20.5 22.7 %copy-start.6 = (bf16[8,128,128]{2,1,0:T(8,128)(2,1)S(1)}, bf16[8,128,128]{2,1,0:T(8,128)(2,1)}, u32[]{:S(2)}) copy-start(bf16[8,128,128]{2,1,0:T(8,128)(2,1)} %get-tuple-element.19) | copy-start | bytes 786436
  20.5 25.2 %copy-start.5 = (bf16[8,128,128]{2,1,0:T(8,128)(2,1)S(1)}, bf16[8,128,128]{2,1,0:T(8,128)(2,1)}, u32[]{:S(2)}) copy-start(bf16[8,128,128]{2,1,0:T(8,128)(2,1)} %get-tuple-element.20) | copy-start | bytes 786436
  20.5 29.2 %copy-start.4 = (bf16[8,128,128]{2,1,0:T(8,128)(2,1)S(1)}, bf16[8,128,128]{2,1,0:T(8,128)(2,1)}, u32[]{:S(2)}) copy-start(bf16[8,128,128]{2,1,0:T(8,128)(2,1)} %get-tuple-element.21) | copy-start | bytes 786436
  20.5 42.1 %all-to-all-start.1 = ((bf16[128,16,128]{2,1,0:T(8,128)(2,1)}), bf16[128,16,128]{2,1,0:T(8,128)(2,1)S(1)}, u32[]{:S(2)}, u32[]{:S(2)}) async-start(bf16[128,16,128]{2,1,0:T(8,128)(2,1)} %spread.1), calls=%async_computation.1 | async-start | bytes 1048576 | tf_op jit(solution)/shard_map/all_to_all | solution.py:279
  43.2 20.8 %collective-permute-start = (bf16[8,128,128]{2,1,0:T(8,128)(2,1)S(1)}, bf16[8,128,128]{2,1,0:T(8,128)(2,1)S(1)}, u32[]{:S(2)}, u32[]{:S(2)}) collective-permute-start(bf16[8,128,128]{2,1,0:T(8,128)(2,1)S(1)} %copy-done.6), channel_id=1, source_target_pairs={{0,256},{128,384},{256,0},{384,128},{1,257},{129,385},{257,1},{385... | collective-permute-start | bytes 786440 | tf_op jit(solution)/shard_map/ppermute | solution.py:215
  45.7 18.3 %collective-permute-start.1 = (bf16[8,128,128]{2,1,0:T(8,128)(2,1)S(1)}, bf16[8,128,128]{2,1,0:T(8,128)(2,1)S(1)}, u32[]{:S(2)}, u32[]{:S(2)}) collective-permute-start(bf16[8,128,128]{2,1,0:T(8,128)(2,1)S(1)} %copy-done.5), channel_id=1, source_target_pairs={{0,384},{128,0},{256,128},{384,256},{1,385},{129,1},{257,129},{385... | collective-permute-start | bytes 786440 | tf_op jit(solution)/shard_map/ppermute | solution.py:215
  49.7 14.3 %collective-permute-start.2 = (bf16[8,128,128]{2,1,0:T(8,128)(2,1)S(1)}, bf16[8,128,128]{2,1,0:T(8,128)(2,1)S(1)}, u32[]{:S(2)}, u32[]{:S(2)}) collective-permute-start(bf16[8,128,128]{2,1,0:T(8,128)(2,1)S(1)} %copy-done.4), channel_id=1, source_target_pairs={{0,128},{128,256},{256,384},{384,0},{1,129},{129,257},{257,385},{3... | collective-permute-start | bytes 786440 | tf_op jit(solution)/shard_map/ppermute | solution.py:215
  62.9 1.2 %copy-start.2 = (bf16[8,128,128]{2,1,0:T(8,128)(2,1)S(1)}, bf16[8,128,128]{2,1,0:T(8,128)(2,1)}, u32[]{:S(2)}) copy-start(bf16[8,128,128]{2,1,0:T(8,128)(2,1)} %get-tuple-element.22.rest_3_) | copy-start | bytes 786436
  65.9 34.6 %copy-start = (bf16[1,4,128,512]{3,2,1,0:T(8,128)(2,1)S(1)}, bf16[1,4,128,512]{3,2,1,0:T(8,128)(2,1)}, u32[]{:S(2)}) copy-start(bf16[1,4,128,512]{3,2,1,0:T(8,128)(2,1)} %param.8) | copy-start | bytes 1572868
  65.9 34.6 %copy-start.1 = (bf16[1,4,128,512]{3,2,1,0:T(8,128)(2,1)S(1)}, bf16[1,4,128,512]{3,2,1,0:T(8,128)(2,1)}, u32[]{:S(2)}) copy-start(bf16[1,4,128,512]{3,2,1,0:T(8,128)(2,1)} %param.9) | copy-start | bytes 1572868
  65.9 34.5 %all-to-all-start.2 = ((bf16[512,4,128]{2,1,0:T(4,128)(2,1)}), bf16[512,4,128]{2,1,0:T(4,128)(2,1)S(1)}, u32[]{:S(2)}, u32[]{:S(2)}) async-start(bf16[512,4,128]{2,1,0:T(4,128)(2,1)} %bitcast.10), calls=%async_computation.2 | async-start | bytes 1048576 | tf_op jit(solution)/shard_map/all_to_all | solution.py:306
  78.1 12.8 %collective-permute-start.3 = (bf16[2,128,512]{2,1,0:T(8,128)(2,1)S(1)}, bf16[2,128,512]{2,1,0:T(8,128)(2,1)S(1)}, u32[]{:S(2)}, u32[]{:S(2)}) collective-permute-start(bf16[2,128,512]{2,1,0:T(8,128)(2,1)S(1)} %get-tuple-element.23), channel_id=1, source_target_pairs={{0,256},{128,384},{256,0},{384,128},{1,257},{129,385},{257,1},{385... | collective-permute-start | bytes 786440 | tf_op jit(solution)/shard_map/ppermute | solution.py:215
  82.9 16.8 %collective-permute-start.4 = (bf16[2,128,512]{2,1,0:T(8,128)(2,1)S(1)}, bf16[2,128,512]{2,1,0:T(8,128)(2,1)S(1)}, u32[]{:S(2)}, u32[]{:S(2)}) collective-permute-start(bf16[2,128,512]{2,1,0:T(8,128)(2,1)S(1)} %get-tuple-element.24), channel_id=1, source_target_pairs={{0,384},{128,0},{256,128},{384,256},{1,385},{129,1},{257,129},{385... | collective-permute-start | bytes 786440 | tf_op jit(solution)/shard_map/ppermute | solution.py:215
  85.7 14.7 %collective-permute-start.5 = (bf16[2,128,512]{2,1,0:T(8,128)(2,1)S(1)}, bf16[2,128,512]{2,1,0:T(8,128)(2,1)S(1)}, u32[]{:S(2)}, u32[]{:S(2)}) collective-permute-start(bf16[2,128,512]{2,1,0:T(8,128)(2,1)S(1)} %get-tuple-element.25), channel_id=1, source_target_pairs={{0,128},{128,256},{256,384},{384,0},{1,129},{129,257},{257,385},{3... | collective-permute-start | bytes 786440 | tf_op jit(solution)/shard_map/ppermute | solution.py:215

commit v5 on v4

v5 whole, which is shorter than its diff:
```python
import functools

import jax
import jax.numpy as jnp
from jax import lax
from jax.experimental import pallas as pl
from jax.experimental.pallas import tpu as pltpu
from jax.sharding import PartitionSpec as P

VMEM = pltpu.VMEM
SMEM = pltpu.SMEM
LIMIT = 40 * 1024 * 1024
WIDE = 58 * 1024 * 1024
F32 = jnp.float32
BF16 = jnp.bfloat16
LANES = 128
TILE = 16
PLACES = 256
BASE_AT = PLACES - 1
OFFSETS = (2, 3, 1, 0)
HOLD = 1 << 34


def params(limit=LIMIT):
    return pltpu.CompilerParams(vmem_limit_bytes=limit)


def in_vmem():
    return pl.BlockSpec(memory_space=VMEM)


def in_smem():
    return pl.BlockSpec(memory_space=SMEM)


def anywhere():
    return pl.BlockSpec(memory_space=pl.ANY)


def in_hbm():
    return pl.BlockSpec(memory_space=pltpu.HBM)


def pack_kernel(
    owners_ref, part_ref, out_ref, plan_ref,
    part, message, owners, lanes, padded, place, place_at, plan, source, in_sems, out_sems, sems,
):
    classes, count = out_ref.shape[:2]
    blocks = part_ref.shape[0]
    load_owners = [
        pltpu.make_async_copy(owners_ref, owners, sems.at[0]),
        pltpu.make_async_copy(owners_ref, lanes, sems.at[1]),
    ]
    for load in load_owners:
        load.start()
    load_parts = []
    for c in range(classes):
        chunk = pl.ds(c * count, count)
        load_parts.append(pltpu.make_async_copy(part_ref.at[chunk], part.at[chunk], in_sems.at[c]))
        load_parts[c].start()
    for load in load_owners:
        load.wait()
    padded[...] = jnp.full_like(padded, lax.axis_size("shard"))
    padded[:, pl.ds(0, blocks)] = lanes[...]
    owner = padded[...]
    key = owner * PLACES + lax.broadcasted_iota(jnp.int32, owner.shape, 1)
    rank = jnp.zeros_like(key)
    for h in range(PLACES // LANES):
        square = jnp.broadcast_to(key[:, h * LANES : (h + 1) * LANES], (LANES, LANES)).T
        other = jnp.concatenate([square] * (PLACES // LANES), axis=1)
        rank = rank + jnp.sum(jnp.where(other < key, 1, 0), axis=0, keepdims=True)
    cls = lax.rem(rank, classes)
    place[...] = cls * count + lax.div(rank, classes)
    bring = pltpu.make_async_copy(place, place_at, sems.at[2])
    bring.start()
    source[...] = cls * lax.axis_size("shard") + owner
    stores = [pltpu.make_async_copy(source, plan_ref.at[:, pl.ds(PLACES, PLACES)], sems.at[3])]
    stores[0].start()
    base = jnp.sum(jnp.where(owner < lax.axis_index("shard"), 1, 0))
    plan[0, BASE_AT] = lax.rem(base, classes)
    bring.wait()
    for load in load_parts:
        load.wait()

    def move(b, _):
        at = place_at[0, b]
        message[at] = part[b]
        plan[0, at] = owners[0, b]
        return 0

    lax.fori_loop(0, blocks, move, 0, unroll=8)
    stores.append(pltpu.make_async_copy(plan, plan_ref.at[:, pl.ds(0, PLACES)], sems.at[4]))
    stores[-1].start()
    for c in range(classes):
        stores.append(pltpu.make_async_copy(message.at[pl.ds(c * count, count)], out_ref.at[c], out_sems.at[c]))
        stores[-1].start()
    for store in stores:
        store.wait()


def factors_kernel(plan_ref, left_ref, right_ref, *rest):
    factor_outs = rest[:-6]
    left, factors, plan, in_sems, out_sems, sem = rest[-6:]
    classes = len(OFFSETS)
    panels = right_ref.shape[1]
    replica = lax.axis_index("rep")
    load_plan = pltpu.make_async_copy(plan_ref.at[:, pl.ds(0, PLACES)], plan, sem)
    load_plan.start()
    load_left = pltpu.make_async_copy(left_ref, left, in_sems.at[classes])
    load_left.start()
    load_plan.wait()
    slots, loads, stores = [], [], []
    for n, d in enumerate(OFFSETS):
        slots.append(lax.rem(lax.rem(replica + d, classes) + classes - plan[0, BASE_AT], classes))
        loads.append(
            pltpu.make_async_copy(right_ref.at[slots[n]], factors.at[n, pl.ds(panels, panels)], in_sems.at[n])
        )
        loads[n].start()
    load_left.wait()
    for n, factor_out in enumerate(factor_outs):
        for h in range(panels):
            factors[n, h] = left[slots[n], :, h * LANES : (h + 1) * LANES]
        loads[n].wait()
        stores.append(pltpu.make_async_copy(factors.at[n], factor_out, out_sems.at[n]))
        stores[n].start()
    for store in stores:
        store.wait()


def spread_kernel(plan_ref, after_ref, in_ref, out_ref, spread, plan, sems, sem):
    del after_ref
    load = pltpu.make_async_copy(plan_ref.at[:, pl.ds(0, PLACES)], plan, sem)
    load.start()
    spread[...] = jnp.zeros_like(spread)
    classes, count = in_ref.shape[:2]
    first = lax.axis_index("rep") * count
    load.wait()

    def add(j, _):
        total = in_ref[0, j].astype(F32)
        for r in range(1, classes):
            total = total + in_ref[r, j].astype(F32)
        spread[plan[0, first + j]] = total.astype(spread.dtype)
        return 0

    lax.fori_loop(0, count, add, 0, unroll=8)
    parts = sems.shape[0]
    length = spread.shape[0] // parts
    stores = []
    for n in range(parts):
        chunk = pl.ds(n * length, length)
        stores.append(pltpu.make_async_copy(spread.at[chunk], out_ref.at[chunk], sems.at[n]))
        stores[n].start()
    for store in stores:
        store.wait()


def update_kernel(grad_ref, after_ref, *rest):
    del after_ref
    factor_refs = rest[:-3]
    out_ref, held, sems = rest[-3:]
    panels, width, _ = grad_ref.shape
    rows = width // panels
    replica = lax.axis_index("rep")
    sources = [lax.rem(replica + panels - d, panels) for d in OFFSETS]
    grad = jnp.concatenate([grad_ref[c] for c in range(panels)], axis=1)
    right = jnp.concatenate(
        [
            jnp.concatenate([factor_ref[panels + h] for h in range(panels)], axis=0)
            for factor_ref in factor_refs
        ],
        axis=1,
    )
    stores = []
    for i, factor_ref in enumerate(factor_refs):
        left = jnp.concatenate([factor_ref[h] for h in range(panels)], axis=1)
        product = jnp.dot(left, grad, preferred_element_type=F32).astype(BF16)
        result = jnp.dot(product, right, preferred_element_type=F32).astype(BF16)
        to = pl.ds(pl.multiple_of(sources[i] * rows, rows), rows)
        for e in range(panels):
            held[i, e] = result[:, e * LANES : (e + 1) * LANES]
            stores.append(pltpu.make_async_copy(held.at[i, e], out_ref.at[sources[e], to], sems.at[i, e]))
            stores[-1].start()
    for store in stores:
        store.wait()


def products_kernel(offsets, grad_ref, *out_refs):
    panels, width, _ = grad_ref.shape
    rows = width // panels
    replica = lax.axis_index("rep")
    grad = jnp.concatenate([grad_ref[c] for c in range(panels)], axis=1)
    for d, out_ref in zip(offsets, out_refs, strict=True):
        to = lax.rem(replica + d, panels)
        start = pl.multiple_of(to * rows, rows)
        own_rows = jnp.concatenate([grad_ref[c, pl.ds(start, rows), :] for c in range(panels)], axis=1)
        left = lax.dot_general(own_rows, grad, (((1,), (1,)), ((), ())), preferred_element_type=F32)
        right = lax.dot_general(grad_ref[to], grad, (((0,), (0,)), ((), ())), preferred_element_type=F32)
        out_ref[0] = left.astype(out_ref.dtype)
        out_ref[1] = right.astype(out_ref.dtype)


def hold_kernel(in_ref, out_ref):
    out_ref[...] = in_ref[...]


def stats_kernel(plan_ref, left_ref, right_ref, *rest):
    product_refs = rest[:-7]
    left_out, right_out, lefts, rights, plan, sems, in_sem = rest[-7:]
    slots = left_ref.shape[0]
    replica = lax.axis_index("rep")
    load = pltpu.make_async_copy(plan_ref.at[:, pl.ds(0, PLACES)], plan, in_sem)
    load.start()
    load.wait()
    base = plan[0, BASE_AT]
    stores = []
    for i, (d, product_ref) in enumerate(zip(OFFSETS, product_refs, strict=True)):
        k = lax.rem(lax.rem(replica + slots - d, slots) + slots - base, slots)
        for n, (old, new, out) in enumerate(((left_ref, lefts, left_out), (right_ref, rights, right_out))):
            new[i] = (0.9 * old[k].astype(F32) + 0.1 * product_ref[n].astype(F32)).astype(new.dtype)
            stores.append(pltpu.make_async_copy(new.at[i], out.at[k], sems.at[len(stores)]))
            stores[-1].start()
    for store in stores:
        store.wait()


def collect_kernel(plan_ref, in_ref, out_ref, update, plan, sem, in_sem):
    load = pltpu.make_async_copy(plan_ref.at[:, pl.ds(PLACES, PLACES)], plan, in_sem)
    load.start()
    load.wait()

    def move(b, _):
        update[b] = in_ref[plan[0, b]]
        return 0

    lax.fori_loop(0, update.shape[0], move, 0, unroll=8)
    store = pltpu.make_async_copy(update, out_ref, sem)
    store.start()
    store.wait()


def to_others(messages):
    count = len(messages)
    return [
        lax.ppermute(message, "rep", [(s, (s + d) % count) for s in range(count)]) if d else message
        for message, d in zip(messages, OFFSETS, strict=True)
    ]


def per_device(partials, owners, left_stat, right_stat, left_factor, right_factor):
    shards = lax.axis_size("shard")
    classes = lax.axis_size("rep")
    _, blocks, rows, width = partials.shape
    slots = left_stat.shape[1]
    quarter = width // classes
    panels = width // LANES
    count = blocks // classes
    tall = width // TILE

    part_tiles = (
        partials[0].reshape(blocks, rows, panels, LANES).transpose(0, 2, 1, 3).reshape(blocks, TILE, LANES)
    )
    right_tiles = right_factor[0].reshape(slots, panels, LANES, LANES)
    factor_message = jax.ShapeDtypeStruct((2 * panels, LANES, LANES), BF16)
    message, plan = pl.pallas_call(
        pack_kernel,
        out_shape=(
            jax.ShapeDtypeStruct((classes, count, TILE, LANES), BF16),
            jax.ShapeDtypeStruct((1, 2 * PLACES), jnp.int32),
        ),
        in_specs=[anywhere()] * 2,
        out_specs=[anywhere()] * 2,
        scratch_shapes=[
            VMEM((blocks, TILE, LANES), BF16),
            VMEM((blocks, TILE, LANES), BF16),
            SMEM((1, blocks), jnp.int32),
            VMEM((1, blocks), jnp.int32),
            VMEM((1, PLACES), jnp.int32),
            VMEM((1, PLACES), jnp.int32),
            SMEM((1, PLACES), jnp.int32),
            SMEM((1, PLACES), jnp.int32),
            VMEM((1, PLACES), jnp.int32),
            pltpu.SemaphoreType.DMA((classes,)),
            pltpu.SemaphoreType.DMA((classes,)),
            pltpu.SemaphoreType.DMA((5,)),
        ],
        compiler_params=params(WIDE),
        name="pack",
    )(owners.reshape(1, blocks), part_tiles)
    received = lax.all_to_all(message, "rep", split_axis=0, concat_axis=0, tiled=True)
    factors = pl.pallas_call(
        factors_kernel,
        out_shape=[factor_message] * classes,
        in_specs=[in_hbm(), anywhere(), anywhere()],
        out_specs=[anywhere()] * classes,
        scratch_shapes=[
            VMEM((slots, quarter, width), BF16),
            VMEM((classes, 2 * panels, LANES, LANES), BF16),
            SMEM((1, PLACES), jnp.int32),
            pltpu.SemaphoreType.DMA((classes + 1,)),
            pltpu.SemaphoreType.DMA((classes,)),
            pltpu.SemaphoreType.DMA,
        ],
        compiler_params=params(),
        cost_estimate=pl.CostEstimate(flops=0, bytes_accessed=8 * width**2, transcendentals=0),
        name="factors",
    )(plan, left_factor[0], right_tiles)
    packed = factors[-1]
    factors = to_others(factors)
    outgoing = pl.pallas_call(
        spread_kernel,
        out_shape=jax.ShapeDtypeStruct((shards, TILE, LANES), BF16),
        in_specs=[in_hbm(), in_hbm(), in_vmem()],
        out_specs=anywhere(),
        scratch_shapes=[
            VMEM((shards, TILE, LANES), BF16),
            SMEM((1, PLACES), jnp.int32),
            pltpu.SemaphoreType.DMA((4,)),
            pltpu.SemaphoreType.DMA,
        ],
        compiler_params=params(),
        name="spread",
    )(plan, packed, received)
    incoming = lax.all_to_all(outgoing, "shard", split_axis=0, concat_axis=0, tiled=True)
    grad = (
        incoming.reshape(shards, panels, rows, LANES).transpose(1, 0, 2, 3).reshape(panels, width, LANES)
    )
    products = []
    for offsets in (OFFSETS[:1], OFFSETS[1:]):
        products += pl.pallas_call(
            functools.partial(products_kernel, offsets),
            out_shape=[jax.ShapeDtypeStruct((2, quarter, width), BF16)] * len(offsets),
            in_specs=[in_vmem()],
            out_specs=[in_vmem()] * len(offsets),
            compiler_params=params(),
            cost_estimate=pl.CostEstimate(
                flops=len(offsets) * width**3, bytes_accessed=2 * width**2, transcendentals=0
            ),
            name="products",
        )(grad)
    update_panels = pl.pallas_call(
        update_kernel,
        out_shape=jax.ShapeDtypeStruct((panels, width, LANES), BF16),
        in_specs=[in_vmem(), anywhere()] + [in_vmem()] * classes,
        out_specs=anywhere(),
        scratch_shapes=[
            VMEM((panels, panels, quarter, LANES), BF16),
            pltpu.SemaphoreType.DMA((panels, panels)),
        ],
        compiler_params=params(),
        cost_estimate=pl.CostEstimate(flops=4 * width**3, bytes_accessed=8 * width**2, transcendentals=0),
        name="update",
    )(grad, products[0], *factors)
    returned = lax.all_to_all(
        update_panels.reshape(panels * shards, rows, LANES),
        ("rep", "shard"),
        split_axis=0,
        concat_axis=0,
        tiled=True,
    )
    products = to_others(products)
    products[0] = pl.pallas_call(
        hold_kernel,
        out_shape=jax.ShapeDtypeStruct((2, quarter, width), BF16),
        in_specs=[in_vmem()],
        out_specs=in_vmem(),
        compiler_params=params(),
        cost_estimate=pl.CostEstimate(flops=HOLD, bytes_accessed=8 * quarter * width, transcendentals=0),
        name="hold",
    )(products[0])
    left_new, right_new = pl.pallas_call(
        stats_kernel,
        out_shape=(
            jax.ShapeDtypeStruct(left_stat.shape[1:], BF16),
            jax.ShapeDtypeStruct(right_stat.shape[1:], BF16),
        ),
        in_specs=[in_hbm()] + [in_vmem()] * (2 + classes),
        out_specs=(anywhere(), anywhere()),
        scratch_shapes=[
            VMEM((slots, quarter, width), BF16),
            VMEM((slots, quarter, width), BF16),
            SMEM((1, PLACES), jnp.int32),
            pltpu.SemaphoreType.DMA((2 * slots,)),
            pltpu.SemaphoreType.DMA,
        ],
        compiler_params=params(),
        cost_estimate=pl.CostEstimate(
            flops=8 * slots * quarter * width, bytes_accessed=12 * slots * quarter * width, transcendentals=0
        ),
        name="stats",
    )(plan, left_stat[0], right_stat[0], *products)
    update = pl.pallas_call(
        collect_kernel,
        out_shape=jax.ShapeDtypeStruct((blocks, rows, LANES), BF16),
        in_specs=[in_hbm(), in_vmem()],
        out_specs=anywhere(),
        scratch_shapes=[
            VMEM((blocks, rows, LANES), BF16),
            SMEM((1, PLACES), jnp.int32),
            pltpu.SemaphoreType.DMA,
            pltpu.SemaphoreType.DMA,
        ],
        compiler_params=params(),
        cost_estimate=pl.CostEstimate(flops=0, bytes_accessed=4 * blocks * rows * LANES, transcendentals=0),
        name="collect",
    )(plan, returned)
    return left_new[None], right_new[None], update


def solution(mesh):
    return jax.shard_map(
        per_device,
        mesh=mesh,
        in_specs=(
            P("rep", None, "shard", None),
            P(),
            P("shard", None, "rep", None),
            P("shard", None, "rep", None),
            P("shard", None, "rep", None),
            P("shard", None, None, "rep"),
        ),
        out_specs=(
            P("shard", None, "rep", None),
            P("shard", None, "rep", None),
            P(None, "shard", "rep"),
        ),
        check_vma=False,
    )
```

time: 103 us -> 101 us (0.981)
  blocking collectives: 13.9 us -> 0 us
  waiting for transfers between devices: 23.2 us -> 30.5 us
  starting transfers between devices: 53.4 us -> 55.5 us
  Pallas kernels: 11 us -> 12.9 us
    all_to_all x1 -> x0, blocking collectives: 13.9 us -> none  [per_device(): lax.all_to_all(message, 'rep', split_axis=0, concat_axis=0, tiled=True)]
    all_to_all x0 -> x1, waiting for transfers between devices: none -> 6.83 us  [per_device(): lax.all_to_all(message, 'rep', split_axis=0, concat_axis=0, tiled=True)]
    all_to_all x0 -> x1, starting transfers between devices: none -> 4.99 us  [per_device(): lax.all_to_all(message, 'rep', split_axis=0, concat_axis=0, tiled=True)]
    pallas_call x2 -> x6, Pallas kernels: 3.23 us -> 6.1 us  [the longest x1 1.66 us: per_device(): pl.pallas_call(stats_kernel, out_shape=(jax.ShapeDtypeStruct(left_stat.sh...]
    all_to_all x1, waiting for transfers between devices: 0.01 us -> 1.9 us  [per_device(): lax.all_to_all(update_panels.reshape(panels * shards, rows, LANES), ('rep...]
    all_to_all x1, starting transfers between devices: 12.2 us -> 10.8 us  [per_device(): lax.all_to_all(update_panels.reshape(panels * shards, rows, LANES), ('rep...]
    ppermute x6, waiting for transfers between devices: 12.2 us -> 10.8 us  [to_others(): lax.ppermute(message, 'rep', [(s, (s + d) % count) for s in range(count)])]
    ppermute x6, starting transfers between devices: 18.5 us -> 17.2 us  [to_others(): lax.ppermute(message, 'rep', [(s, (s + d) % count) for s in range(count)])]
  transfers between devices with their start and end apart: 8 -> 9, of which waited for: 4 -> 5; matrix products, arithmetic and copies ran while one was open for 0% -> 0% of each run, Pallas kernels for 1% -> 6%
where the time goes in v5:
time: 101 us
  starting transfers between devices  55.5 us (55%)
  waiting for transfers between devices  30.5 us (30%)
  Pallas kernels  12.9 us (13%)
    all_to_all x1, starting transfers between devices, per_device(): lax.all_to_all(outgoing, 'shard', split_axis=0, concat_axis=0, tiled=True)  22.5 us
    ppermute x6, starting transfers between devices, to_others(): lax.ppermute(message, 'rep', [(s, (s + d) % count) for s in range(count)])  17.2 us
    all_to_all x1, waiting for transfers between devices, per_device(): lax.all_to_all(outgoing, 'shard', split_axis=0, concat_axis=0, tiled=True)  11 us
    ppermute x6, waiting for transfers between devices, to_others(): lax.ppermute(message, 'rep', [(s, (s + d) % count) for s in range(count)])  10.8 us
    all_to_all x1, starting transfers between devices, per_device(): lax.all_to_all(update_panels.reshape(panels * shards, rows, LANES), ('rep...  10.8 us
    all_to_all x1, waiting for transfers between devices, per_device(): lax.all_to_all(message, 'rep', split_axis=0, concat_axis=0, tiled=True)  6.83 us
    all_to_all x1, starting transfers between devices, per_device(): lax.all_to_all(message, 'rep', split_axis=0, concat_axis=0, tiled=True)  4.99 us
    pallas_call x1, Pallas kernels, per_device(): pl.pallas_call(pack_kernel, out_shape=(jax.ShapeDtypeStruct((classes, cou...  3.31 us
  transfers between devices with their start and end apart: 9, of which 5 were waited for; matrix products, arithmetic and copies ran while one was open for 0% of the time, Pallas kernels for 6%

profile of v5, /device:TPU:1, one launch (start us, length us, event | category | flops | bytes accessed | tf_op | source)
XLA Modules:
  0.0 100.6 jit_solution(1228671822750097908)
XLA Ops:
  0.6 3.3 %pack.1 = (bf16[4,56,16,128]{3,2,1,0:T(8,128)(2,1)}, s32[1,512]{1,0:T(1,128)}) custom-call(s32[1,224]{1,0:T(1,128)} %bitcast.26, bf16[224,16,128]{2,1,0:T(8,128)(2,1)} %bitcast.25), custom_call_target="tpu_custom_call" | custom-call | tf_op jit(solution)/shard_map/pack/pallas_call | solution.py:265
  3.9 0.0 copy-start.2
  4.0 0.0 copy-start.3
  4.0 5.0 %all-to-all-start = ((bf16[4,56,16,128]{3,2,1,0:T(8,128)(2,1)}), bf16[4,56,16,128]{3,2,1,0:T(8,128)(2,1)S(1)}, u32[]{:S(2)}, u32[]{:S(2)}) async-start(bf16[4,56,16,128]{3,2,1,0:T(8,128)(2,1)} %get-tuple-element.16), calls=%async_computation | async-start | bytes 1835008 | tf_op jit(solution)/shard_map/all_to_all | solution.py:290
  9.0 0.0 copy-start.4
  9.0 0.0 copy-done.2
  9.0 0.0 copy-done.3
  9.0 0.7 copy-done.4
  9.6 1.5 %factors.1 = (bf16[8,128,128]{2,1,0:T(8,128)(2,1)S(1)}, bf16[8,128,128]{2,1,0:T(8,128)(2,1)S(1)}, bf16[8,128,128]{2,1,0:T(8,128)(2,1)S(1)}, bf16[8,128,128]{2,1,0:T(8,128)(2,1)S(1)}) custom-call(s32[1,512]{1,0:T(1,128)S(1)} %copy-done.4, bf16[4,128,512]{2,1,0:T(8,128)(2,1)S(1)} %bitcast.22, bf16[4,4,128,128]{3,2,1,0:T(8,128)(2,1)S(1)} %bitcast.23), custom_call_target="tpu_custom_call" | custom-call | bytes 2097152 | tf_op jit(solution)/shard_map/factors/pallas_call | solution.py:291
  11.2 6.8 %all-to-all-done.in_ref = bf16[4,56,16,128]{3,2,1,0:T(8,128)(2,1)S(1)} async-done(((bf16[4,56,16,128]{3,2,1,0:T(8,128)(2,1)}), bf16[4,56,16,128]{3,2,1,0:T(8,128)(2,1)S(1)}, u32[]{:S(2)}, u32[]{:S(2)}) %all-to-all-start) | async-done | bytes 917536 | tf_op jit(solution)/shard_map/all_to_all | solution.py:290
  18.0 1.5 %spread.1 = bf16[128,16,128]{2,1,0:T(8,128)(2,1)} custom-call(s32[1,512]{1,0:T(1,128)S(1)} %copy-done.4, bf16[8,128,128]{2,1,0:T(8,128)(2,1)S(1)} %get-tuple-element.15.after_ref.rest_3_, bf16[4,56,16,128]{3,2,1,0:T(8,128)(2,1)S(1)} %all-to-all-done.in_ref), custom_call_target="tpu_custom_call" | custom-call | tf_op jit(solution)/shard_map/spread/pallas_call | solution.py:310
  19.5 22.5 %all-to-all-start.1 = ((bf16[128,16,128]{2,1,0:T(8,128)(2,1)}), bf16[128,16,128]{2,1,0:T(8,128)(2,1)S(1)}, u32[]{:S(2)}, u32[]{:S(2)}) async-start(bf16[128,16,128]{2,1,0:T(8,128)(2,1)} %spread.1), calls=%async_computation.1 | async-start | bytes 1048576 | tf_op jit(solution)/shard_map/all_to_all | solution.py:324
  42.1 2.2 %collective-permute-start.3 = (bf16[8,128,128]{2,1,0:T(8,128)(2,1)S(1)}, bf16[8,128,128]{2,1,0:T(8,128)(2,1)S(1)}, u32[]{:S(2)}, u32[]{:S(2)}) collective-permute-start(bf16[8,128,128]{2,1,0:T(8,128)(2,1)S(1)} %get-tuple-element.22), channel_id=1, source_target_pairs={{0,256},{128,384},{256,0},{384,128},{1,257},{129,385},{257,1},{385... | collective-permute-start | bytes 786440 | tf_op jit(solution)/shard_map/ppermute | solution.py:245
  44.3 4.3 %collective-permute-start.4 = (bf16[8,128,128]{2,1,0:T(8,128)(2,1)S(1)}, bf16[8,128,128]{2,1,0:T(8,128)(2,1)S(1)}, u32[]{:S(2)}, u32[]{:S(2)}) collective-permute-start(bf16[8,128,128]{2,1,0:T(8,128)(2,1)S(1)} %get-tuple-element.23), channel_id=1, source_target_pairs={{0,384},{128,0},{256,128},{384,256},{1,385},{129,1},{257,129},{385... | collective-permute-start | bytes 786440 | tf_op jit(solution)/shard_map/ppermute | solution.py:245
  48.6 1.9 %collective-permute-start.5 = (bf16[8,128,128]{2,1,0:T(8,128)(2,1)S(1)}, bf16[8,128,128]{2,1,0:T(8,128)(2,1)S(1)}, u32[]{:S(2)}, u32[]{:S(2)}) collective-permute-start(bf16[8,128,128]{2,1,0:T(8,128)(2,1)S(1)} %get-tuple-element.24), channel_id=1, source_target_pairs={{0,128},{128,256},{256,384},{384,0},{1,129},{129,257},{257,385},{3... | collective-permute-start | bytes 786440 | tf_op jit(solution)/shard_map/ppermute | solution.py:245
  50.5 11.0 %all-to-all-done.1 = bf16[128,16,128]{2,1,0:T(8,128)(2,1)S(1)} async-done(((bf16[128,16,128]{2,1,0:T(8,128)(2,1)}), bf16[128,16,128]{2,1,0:T(8,128)(2,1)S(1)}, u32[]{:S(2)}, u32[]{:S(2)}) %all-to-all-start.1) | async-done | bytes 524320 | tf_op jit(solution)/shard_map/all_to_all | solution.py:324
  61.5 0.2 copy.10
  61.7 0.4 products.2.after_ref
  62.1 2.2 %collective-permute-start = (bf16[2,128,512]{2,1,0:T(8,128)(2,1)S(1)}, bf16[2,128,512]{2,1,0:T(8,128)(2,1)S(1)}, u32[]{:S(2)}, u32[]{:S(2)}) collective-permute-start(bf16[2,128,512]{2,1,0:T(8,128)(2,1)S(1)} %products.2.after_ref), channel_id=1, source_target_pairs={{0,256},{128,384},{256,0},{384,128},{1,257},{129,385},{257,1},{385... | collective-permute-start | bytes 786440 | tf_op jit(solution)/shard_map/ppermute | solution.py:245
  64.3 0.0 collective-permute-done.3.rest_0_
  64.3 0.0 collective-permute-done.4.rest_1_
  64.3 0.0 collective-permute-done.5.rest_2_
  64.3 2.0 %update.1 = bf16[4,512,128]{2,1,0:T(8,128)(2,1)} custom-call(bf16[4,512,128]{2,1,0:T(8,128)(2,1)S(1)} %bitcast.18, bf16[2,128,512]{2,1,0:T(8,128)(2,1)S(1)} %products.2.after_ref, bf16[8,128,128]{2,1,0:T(8,128)(2,1)S(1)} %collective-permute-done.3.rest_0_, bf16[8,128,128]{2,1,0:T(8,128)(2,1)S(1)} %collective-permute-done.4.rest_1_, ...), custom_call_target="tpu_custom_call" | custom-call | flops 536870912 | bytes 2097152 | tf_op jit(solution)/shard_map/update/pallas_call | solution.py:341
  66.3 10.8 %all-to-all-start.2 = ((bf16[512,4,128]{2,1,0:T(4,128)(2,1)}), bf16[512,4,128]{2,1,0:T(4,128)(2,1)S(1)}, u32[]{:S(2)}, u32[]{:S(2)}) async-start(bf16[512,4,128]{2,1,0:T(4,128)(2,1)} %bitcast.14), calls=%async_computation.2 | async-start | bytes 1048576 | tf_op jit(solution)/shard_map/all_to_all | solution.py:354
  77.1 0.9 products.3
  78.0 4.5 %collective-permute-start.1 = (bf16[2,128,512]{2,1,0:T(8,128)(2,1)S(1)}, bf16[2,128,512]{2,1,0:T(8,128)(2,1)S(1)}, u32[]{:S(2)}, u32[]{:S(2)}) collective-permute-start(bf16[2,128,512]{2,1,0:T(8,128)(2,1)S(1)} %get-tuple-element.17), channel_id=1, source_target_pairs={{0,384},{128,0},{256,128},{384,256},{1,385},{129,1},{257,129},{385... | collective-permute-start | bytes 786440 | tf_op jit(solution)/shard_map/ppermute | solution.py:245
  82.5 0.0 copy-start
  82.5 0.0 copy-start.1
  82.5 2.1 %collective-permute-start.2 = (bf16[2,128,512]{2,1,0:T(8,128)(2,1)S(1)}, bf16[2,128,512]{2,1,0:T(8,128)(2,1)S(1)}, u32[]{:S(2)}, u32[]{:S(2)}) collective-permute-start(bf16[2,128,512]{2,1,0:T(8,128)(2,1)S(1)} %get-tuple-element.18), channel_id=1, source_target_pairs={{0,128},{128,256},{256,384},{384,0},{1,129},{129,257},{257,385},{3... | collective-permute-start | bytes 786440 | tf_op jit(solution)/shard_map/ppermute | solution.py:245
  84.6 0.0 collective-permute-done.in_ref
  84.6 5.8 %collective-permute-done.1.rest_1_ = bf16[2,128,512]{2,1,0:T(8,128)(2,1)S(1)} collective-permute-done((bf16[2,128,512]{2,1,0:T(8,128)(2,1)S(1)}, bf16[2,128,512]{2,1,0:T(8,128)(2,1)S(1)}, u32[]{:S(2)}, u32[]{:S(2)}) %collective-permute-start.1) | collective-permute-done | bytes 262176 | tf_op jit(solution)/shard_map/ppermute | solution.py:245
  90.5 4.9 %collective-permute-done.2.rest_2_ = bf16[2,128,512]{2,1,0:T(8,128)(2,1)S(1)} collective-permute-done((bf16[2,128,512]{2,1,0:T(8,128)(2,1)S(1)}, bf16[2,128,512]{2,1,0:T(8,128)(2,1)S(1)}, u32[]{:S(2)}, u32[]{:S(2)}) %collective-permute-start.2) | collective-permute-done | bytes 262176 | tf_op jit(solution)/shard_map/ppermute | solution.py:245
  95.4 0.0 copy-done
  95.4 0.0 copy-done.1
  95.4 1.7 %stats.1 = (bf16[4,128,512]{2,1,0:T(8,128)(2,1)}, bf16[4,128,512]{2,1,0:T(8,128)(2,1)}) custom-call(s32[1,512]{1,0:T(1,128)S(1)} %copy-done.4, bf16[4,128,512]{2,1,0:T(8,128)(2,1)S(1)} %bitcast.20, bf16[4,128,512]{2,1,0:T(8,128)(2,1)S(1)} %bitcast.21, bf16[2,128,512]{2,1,0:T(8,128)(2,1)S(1)} %hold.1.rest_0_, ...), custom_call_target="tpu_custom_call" | custom-call | flops 2097152 | bytes 3145728 | tf_op jit(solution)/shard_map/stats/pallas_call | solution.py:371
  97.1 1.9 %all-to-all-done.2.in_ref = bf16[512,4,128]{2,1,0:T(4,128)(2,1)S(1)} async-done(((bf16[512,4,128]{2,1,0:T(4,128)(2,1)}), bf16[512,4,128]{2,1,0:T(4,128)(2,1)S(1)}, u32[]{:S(2)}, u32[]{:S(2)}) %all-to-all-start.2) | async-done | bytes 524320 | tf_op jit(solution)/shard_map/all_to_all | solution.py:354
  99.0 1.6 %collect.1 = bf16[224,4,128]{2,1,0:T(4,128)(2,1)} custom-call(s32[1,512]{1,0:T(1,128)S(1)} %copy-done.4, bf16[512,4,128]{2,1,0:T(4,128)(2,1)S(1)} %all-to-all-done.2.in_ref), custom_call_target="tpu_custom_call" | custom-call | bytes 458752 | tf_op jit(solution)/shard_map/collect/pallas_call | solution.py:392
  (1 shorter events, 0.0 us)
Async XLA Ops:
  3.9 5.0 %copy-start.2 = (bf16[1,4,128,512]{3,2,1,0:T(8,128)(2,1)S(1)}, bf16[1,4,128,512]{3,2,1,0:T(8,128)(2,1)}, u32[]{:S(2)}) copy-start(bf16[1,4,128,512]{3,2,1,0:T(8,128)(2,1)} %param.10) | copy-start | bytes 1572868
  4.0 5.0 %copy-start.3 = (bf16[1,4,512,128]{3,2,1,0:T(8,128)(2,1)S(1)}, bf16[1,4,512,128]{3,2,1,0:T(8,128)(2,1)}, u32[]{:S(2)}) copy-start(bf16[1,4,512,128]{3,2,1,0:T(8,128)(2,1)} %param.11) | copy-start | bytes 1572868
  4.0 14.0 %all-to-all-start = ((bf16[4,56,16,128]{3,2,1,0:T(8,128)(2,1)}), bf16[4,56,16,128]{3,2,1,0:T(8,128)(2,1)S(1)}, u32[]{:S(2)}, u32[]{:S(2)}) async-start(bf16[4,56,16,128]{3,2,1,0:T(8,128)(2,1)} %get-tuple-element.16), calls=%async_computation | async-start | bytes 1835008 | tf_op jit(solution)/shard_map/all_to_all | solution.py:290
  9.0 0.7 copy-start.4
  19.5 42.0 %all-to-all-start.1 = ((bf16[128,16,128]{2,1,0:T(8,128)(2,1)}), bf16[128,16,128]{2,1,0:T(8,128)(2,1)S(1)}, u32[]{:S(2)}, u32[]{:S(2)}) async-start(bf16[128,16,128]{2,1,0:T(8,128)(2,1)} %spread.1), calls=%async_computation.1 | async-start | bytes 1048576 | tf_op jit(solution)/shard_map/all_to_all | solution.py:324
  42.1 22.3 %collective-permute-start.3 = (bf16[8,128,128]{2,1,0:T(8,128)(2,1)S(1)}, bf16[8,128,128]{2,1,0:T(8,128)(2,1)S(1)}, u32[]{:S(2)}, u32[]{:S(2)}) collective-permute-start(bf16[8,128,128]{2,1,0:T(8,128)(2,1)S(1)} %get-tuple-element.22), channel_id=1, source_target_pairs={{0,256},{128,384},{256,0},{384,128},{1,257},{129,385},{257,1},{385... | collective-permute-start | bytes 786440 | tf_op jit(solution)/shard_map/ppermute | solution.py:245
  44.3 20.1 %collective-permute-start.4 = (bf16[8,128,128]{2,1,0:T(8,128)(2,1)S(1)}, bf16[8,128,128]{2,1,0:T(8,128)(2,1)S(1)}, u32[]{:S(2)}, u32[]{:S(2)}) collective-permute-start(bf16[8,128,128]{2,1,0:T(8,128)(2,1)S(1)} %get-tuple-element.23), channel_id=1, source_target_pairs={{0,384},{128,0},{256,128},{384,256},{1,385},{129,1},{257,129},{385... | collective-permute-start | bytes 786440 | tf_op jit(solution)/shard_map/ppermute | solution.py:245
  48.6 15.8 %collective-permute-start.5 = (bf16[8,128,128]{2,1,0:T(8,128)(2,1)S(1)}, bf16[8,128,128]{2,1,0:T(8,128)(2,1)S(1)}, u32[]{:S(2)}, u32[]{:S(2)}) collective-permute-start(bf16[8,128,128]{2,1,0:T(8,128)(2,1)S(1)} %get-tuple-element.24), channel_id=1, source_target_pairs={{0,128},{128,256},{256,384},{384,0},{1,129},{129,257},{257,385},{3... | collective-permute-start | bytes 786440 | tf_op jit(solution)/shard_map/ppermute | solution.py:245
  62.1 22.5 %collective-permute-start = (bf16[2,128,512]{2,1,0:T(8,128)(2,1)S(1)}, bf16[2,128,512]{2,1,0:T(8,128)(2,1)S(1)}, u32[]{:S(2)}, u32[]{:S(2)}) collective-permute-start(bf16[2,128,512]{2,1,0:T(8,128)(2,1)S(1)} %products.2.after_ref), channel_id=1, source_target_pairs={{0,256},{128,384},{256,0},{384,128},{1,257},{129,385},{257,1},{385... | collective-permute-start | bytes 786440 | tf_op jit(solution)/shard_map/ppermute | solution.py:245
  66.3 32.6 %all-to-all-start.2 = ((bf16[512,4,128]{2,1,0:T(4,128)(2,1)}), bf16[512,4,128]{2,1,0:T(4,128)(2,1)S(1)}, u32[]{:S(2)}, u32[]{:S(2)}) async-start(bf16[512,4,128]{2,1,0:T(4,128)(2,1)} %bitcast.14), calls=%async_computation.2 | async-start | bytes 1048576 | tf_op jit(solution)/shard_map/all_to_all | solution.py:354
  78.0 12.5 %collective-permute-start.1 = (bf16[2,128,512]{2,1,0:T(8,128)(2,1)S(1)}, bf16[2,128,512]{2,1,0:T(8,128)(2,1)S(1)}, u32[]{:S(2)}, u32[]{:S(2)}) collective-permute-start(bf16[2,128,512]{2,1,0:T(8,128)(2,1)S(1)} %get-tuple-element.17), channel_id=1, source_target_pairs={{0,384},{128,0},{256,128},{384,256},{1,385},{129,1},{257,129},{385... | collective-permute-start | bytes 786440 | tf_op jit(solution)/shard_map/ppermute | solution.py:245
  82.5 12.9 %copy-start = (bf16[1,4,128,512]{3,2,1,0:T(8,128)(2,1)S(1)}, bf16[1,4,128,512]{3,2,1,0:T(8,128)(2,1)}, u32[]{:S(2)}) copy-start(bf16[1,4,128,512]{3,2,1,0:T(8,128)(2,1)} %param.8) | copy-start | bytes 1572868
  82.5 12.9 %copy-start.1 = (bf16[1,4,128,512]{3,2,1,0:T(8,128)(2,1)S(1)}, bf16[1,4,128,512]{3,2,1,0:T(8,128)(2,1)}, u32[]{:S(2)}) copy-start(bf16[1,4,128,512]{3,2,1,0:T(8,128)(2,1)} %param.9) | copy-start | bytes 1572868
  82.5 12.9 %collective-permute-start.2 = (bf16[2,128,512]{2,1,0:T(8,128)(2,1)S(1)}, bf16[2,128,512]{2,1,0:T(8,128)(2,1)S(1)}, u32[]{:S(2)}, u32[]{:S(2)}) collective-permute-start(bf16[2,128,512]{2,1,0:T(8,128)(2,1)S(1)} %get-tuple-element.18), channel_id=1, source_target_pairs={{0,128},{128,256},{256,384},{384,0},{1,129},{129,257},{257,385},{3... | collective-permute-start | bytes 786440 | tf_op jit(solution)/shard_map/ppermute | solution.py:245

commit v6 on v5

--- a/solution.py
+++ b/solution.py
@@ -17,7 +17,7 @@
 TILE = 16
 PLACES = 256
 BASE_AT = PLACES - 1
-OFFSETS = (2, 3, 1, 0)
+OFFSETS = (2, 1, 3, 0)
 HOLD = 1 << 34
 
 
@@ -224,8 +224,8 @@
         store.wait()
 
 
-def collect_kernel(plan_ref, in_ref, out_ref, update, plan, sem, in_sem):
-    load = pltpu.make_async_copy(plan_ref.at[:, pl.ds(PLACES, PLACES)], plan, in_sem)
+def collect_kernel(plan_ref, in_ref, out_ref, update, plan, sems, sem):
+    load = pltpu.make_async_copy(plan_ref.at[:, pl.ds(PLACES, PLACES)], plan, sem)
     load.start()
     load.wait()
 
@@ -233,10 +233,16 @@
         update[b] = in_ref[plan[0, b]]
         return 0
 
-    lax.fori_loop(0, update.shape[0], move, 0, unroll=8)
-    store = pltpu.make_async_copy(update, out_ref, sem)
-    store.start()
-    store.wait()
+    parts = sems.shape[0]
+    length = update.shape[0] // parts
+    stores = []
+    for n in range(parts):
+        lax.fori_loop(n * length, (n + 1) * length, move, 0, unroll=8)
+        chunk = pl.ds(n * length, length)
+        stores.append(pltpu.make_async_copy(update.at[chunk], out_ref.at[chunk], sems.at[n]))
+        stores[n].start()
+    for store in stores:
+        store.wait()
 
 
 def to_others(messages):
@@ -397,7 +403,7 @@
         scratch_shapes=[
             VMEM((blocks, rows, LANES), BF16),
             SMEM((1, PLACES), jnp.int32),
-            pltpu.SemaphoreType.DMA,
+            pltpu.SemaphoreType.DMA((classes,)),
             pltpu.SemaphoreType.DMA,
         ],
         compiler_params=params(),

time: 101 us -> 101 us (level)
    ppermute x6, waiting for transfers between devices: 10.8 us -> 7.58 us  [to_others(): lax.ppermute(message, 'rep', [(s, (s + d) % count) for s in range(count)])]
    all_to_all x1, waiting for transfers between devices: 1.9 us -> 5.04 us  [per_device(): lax.all_to_all(update_panels.reshape(panels * shards, rows, LANES), ('rep...]
where the time goes in v6:
time: 101 us
  starting transfers between devices  55.9 us (55%)
  waiting for transfers between devices  30.2 us (30%)
  Pallas kernels  12.8 us (13%)
    all_to_all x1, starting transfers between devices, per_device(): lax.all_to_all(outgoing, 'shard', split_axis=0, concat_axis=0, tiled=True)  22.5 us
    ppermute x6, starting transfers between devices, to_others(): lax.ppermute(message, 'rep', [(s, (s + d) % count) for s in range(count)])  17.5 us
    all_to_all x1, starting transfers between devices, per_device(): lax.all_to_all(update_panels.reshape(panels * shards, rows, LANES), ('rep...  10.8 us
    all_to_all x1, waiting for transfers between devices, per_device(): lax.all_to_all(outgoing, 'shard', split_axis=0, concat_axis=0, tiled=True)  10.8 us
    ppermute x6, waiting for transfers between devices, to_others(): lax.ppermute(message, 'rep', [(s, (s + d) % count) for s in range(count)])  7.58 us
    all_to_all x1, waiting for transfers between devices, per_device(): lax.all_to_all(message, 'rep', split_axis=0, concat_axis=0, tiled=True)  6.83 us
    all_to_all x1, waiting for transfers between devices, per_device(): lax.all_to_all(update_panels.reshape(panels * shards, rows, LANES), ('rep...  5.04 us
    all_to_all x1, starting transfers between devices, per_device(): lax.all_to_all(message, 'rep', split_axis=0, concat_axis=0, tiled=True)  4.99 us
  transfers between devices with their start and end apart: 9, of which 5 were waited for; matrix products, arithmetic and copies ran while one was open for 0% of the time, Pallas kernels for 6%

profile of v6, /device:TPU:1, one launch (start us, length us, event | category | flops | bytes accessed | tf_op | source)
XLA Modules:
  0.0 100.6 jit_solution(5886297457955955574)
XLA Ops:
  0.6 3.3 %pack.1 = (bf16[4,56,16,128]{3,2,1,0:T(8,128)(2,1)}, s32[1,512]{1,0:T(1,128)}) custom-call(s32[1,224]{1,0:T(1,128)} %bitcast.26, bf16[224,16,128]{2,1,0:T(8,128)(2,1)} %bitcast.25), custom_call_target="tpu_custom_call" | custom-call | tf_op jit(solution)/shard_map/pack/pallas_call | solution.py:271
  3.9 0.0 copy-start.2
  4.0 0.0 copy-start.3
  4.0 5.0 %all-to-all-start = ((bf16[4,56,16,128]{3,2,1,0:T(8,128)(2,1)}), bf16[4,56,16,128]{3,2,1,0:T(8,128)(2,1)S(1)}, u32[]{:S(2)}, u32[]{:S(2)}) async-start(bf16[4,56,16,128]{3,2,1,0:T(8,128)(2,1)} %get-tuple-element.16), calls=%async_computation | async-start | bytes 1835008 | tf_op jit(solution)/shard_map/all_to_all | solution.py:296
  9.0 0.0 copy-start.4
  9.0 0.0 copy-done.2
  9.0 0.0 copy-done.3
  9.0 0.7 copy-done.4
  9.6 1.5 %factors.1 = (bf16[8,128,128]{2,1,0:T(8,128)(2,1)S(1)}, bf16[8,128,128]{2,1,0:T(8,128)(2,1)S(1)}, bf16[8,128,128]{2,1,0:T(8,128)(2,1)S(1)}, bf16[8,128,128]{2,1,0:T(8,128)(2,1)S(1)}) custom-call(s32[1,512]{1,0:T(1,128)S(1)} %copy-done.4, bf16[4,128,512]{2,1,0:T(8,128)(2,1)S(1)} %bitcast.22, bf16[4,4,128,128]{3,2,1,0:T(8,128)(2,1)S(1)} %bitcast.23), custom_call_target="tpu_custom_call" | custom-call | bytes 2097152 | tf_op jit(solution)/shard_map/factors/pallas_call | solution.py:297
  11.2 6.8 %all-to-all-done.in_ref = bf16[4,56,16,128]{3,2,1,0:T(8,128)(2,1)S(1)} async-done(((bf16[4,56,16,128]{3,2,1,0:T(8,128)(2,1)}), bf16[4,56,16,128]{3,2,1,0:T(8,128)(2,1)S(1)}, u32[]{:S(2)}, u32[]{:S(2)}) %all-to-all-start) | async-done | bytes 917536 | tf_op jit(solution)/shard_map/all_to_all | solution.py:296
  18.0 1.5 %spread.1 = bf16[128,16,128]{2,1,0:T(8,128)(2,1)} custom-call(s32[1,512]{1,0:T(1,128)S(1)} %copy-done.4, bf16[8,128,128]{2,1,0:T(8,128)(2,1)S(1)} %get-tuple-element.15.after_ref.rest_3_, bf16[4,56,16,128]{3,2,1,0:T(8,128)(2,1)S(1)} %all-to-all-done.in_ref), custom_call_target="tpu_custom_call" | custom-call | tf_op jit(solution)/shard_map/spread/pallas_call | solution.py:316
  19.5 22.5 %all-to-all-start.1 = ((bf16[128,16,128]{2,1,0:T(8,128)(2,1)}), bf16[128,16,128]{2,1,0:T(8,128)(2,1)S(1)}, u32[]{:S(2)}, u32[]{:S(2)}) async-start(bf16[128,16,128]{2,1,0:T(8,128)(2,1)} %spread.1), calls=%async_computation.1 | async-start | bytes 1048576 | tf_op jit(solution)/shard_map/all_to_all | solution.py:330
  42.1 2.2 %collective-permute-start.3 = (bf16[8,128,128]{2,1,0:T(8,128)(2,1)S(1)}, bf16[8,128,128]{2,1,0:T(8,128)(2,1)S(1)}, u32[]{:S(2)}, u32[]{:S(2)}) collective-permute-start(bf16[8,128,128]{2,1,0:T(8,128)(2,1)S(1)} %get-tuple-element.22), channel_id=1, source_target_pairs={{0,256},{128,384},{256,0},{384,128},{1,257},{129,385},{257,1},{385... | collective-permute-start | bytes 786440 | tf_op jit(solution)/shard_map/ppermute | solution.py:251
  44.3 3.1 %collective-permute-start.4 = (bf16[8,128,128]{2,1,0:T(8,128)(2,1)S(1)}, bf16[8,128,128]{2,1,0:T(8,128)(2,1)S(1)}, u32[]{:S(2)}, u32[]{:S(2)}) collective-permute-start(bf16[8,128,128]{2,1,0:T(8,128)(2,1)S(1)} %get-tuple-element.23), channel_id=1, source_target_pairs={{0,128},{128,256},{256,384},{384,0},{1,129},{129,257},{257,385},{3... | collective-permute-start | bytes 786440 | tf_op jit(solution)/shard_map/ppermute | solution.py:251
  47.4 3.4 %collective-permute-start.5 = (bf16[8,128,128]{2,1,0:T(8,128)(2,1)S(1)}, bf16[8,128,128]{2,1,0:T(8,128)(2,1)S(1)}, u32[]{:S(2)}, u32[]{:S(2)}) collective-permute-start(bf16[8,128,128]{2,1,0:T(8,128)(2,1)S(1)} %get-tuple-element.24), channel_id=1, source_target_pairs={{0,384},{128,0},{256,128},{384,256},{1,385},{129,1},{257,129},{385... | collective-permute-start | bytes 786440 | tf_op jit(solution)/shard_map/ppermute | solution.py:251
  50.8 10.8 %all-to-all-done.1 = bf16[128,16,128]{2,1,0:T(8,128)(2,1)S(1)} async-done(((bf16[128,16,128]{2,1,0:T(8,128)(2,1)}), bf16[128,16,128]{2,1,0:T(8,128)(2,1)S(1)}, u32[]{:S(2)}, u32[]{:S(2)}) %all-to-all-start.1) | async-done | bytes 524320 | tf_op jit(solution)/shard_map/all_to_all | solution.py:330
  61.5 0.2 copy.10
  61.7 0.4 products.2.after_ref
  62.1 2.2 %collective-permute-start = (bf16[2,128,512]{2,1,0:T(8,128)(2,1)S(1)}, bf16[2,128,512]{2,1,0:T(8,128)(2,1)S(1)}, u32[]{:S(2)}, u32[]{:S(2)}) collective-permute-start(bf16[2,128,512]{2,1,0:T(8,128)(2,1)S(1)} %products.2.after_ref), channel_id=1, source_target_pairs={{0,256},{128,384},{256,0},{384,128},{1,257},{129,385},{257,1},{385... | collective-permute-start | bytes 786440 | tf_op jit(solution)/shard_map/ppermute | solution.py:251
  64.3 0.0 collective-permute-done.3.rest_0_
  64.3 0.0 collective-permute-done.4.rest_1_
  64.3 0.0 collective-permute-done.5.rest_2_
  64.3 2.0 %update.1 = bf16[4,512,128]{2,1,0:T(8,128)(2,1)} custom-call(bf16[4,512,128]{2,1,0:T(8,128)(2,1)S(1)} %bitcast.18, bf16[2,128,512]{2,1,0:T(8,128)(2,1)S(1)} %products.2.after_ref, bf16[8,128,128]{2,1,0:T(8,128)(2,1)S(1)} %collective-permute-done.3.rest_0_, bf16[8,128,128]{2,1,0:T(8,128)(2,1)S(1)} %collective-permute-done.4.rest_1_, ...), custom_call_target="tpu_custom_call" | custom-call | flops 536870912 | bytes 2097152 | tf_op jit(solution)/shard_map/update/pallas_call | solution.py:347
  66.3 10.8 %all-to-all-start.2 = ((bf16[512,4,128]{2,1,0:T(4,128)(2,1)}), bf16[512,4,128]{2,1,0:T(4,128)(2,1)S(1)}, u32[]{:S(2)}, u32[]{:S(2)}) async-start(bf16[512,4,128]{2,1,0:T(4,128)(2,1)} %bitcast.14), calls=%async_computation.2 | async-start | bytes 1048576 | tf_op jit(solution)/shard_map/all_to_all | solution.py:360
  77.2 0.9 products.3
  78.1 3.3 %collective-permute-start.1 = (bf16[2,128,512]{2,1,0:T(8,128)(2,1)S(1)}, bf16[2,128,512]{2,1,0:T(8,128)(2,1)S(1)}, u32[]{:S(2)}, u32[]{:S(2)}) collective-permute-start(bf16[2,128,512]{2,1,0:T(8,128)(2,1)S(1)} %get-tuple-element.17), channel_id=1, source_target_pairs={{0,128},{128,256},{256,384},{384,0},{1,129},{129,257},{257,385},{3... | collective-permute-start | bytes 786440 | tf_op jit(solution)/shard_map/ppermute | solution.py:251
  81.4 0.0 copy-start
  81.4 0.0 copy-start.1
  81.4 3.3 %collective-permute-start.2 = (bf16[2,128,512]{2,1,0:T(8,128)(2,1)S(1)}, bf16[2,128,512]{2,1,0:T(8,128)(2,1)S(1)}, u32[]{:S(2)}, u32[]{:S(2)}) collective-permute-start(bf16[2,128,512]{2,1,0:T(8,128)(2,1)S(1)} %get-tuple-element.18), channel_id=1, source_target_pairs={{0,384},{128,0},{256,128},{384,256},{1,385},{129,1},{257,129},{385... | collective-permute-start | bytes 786440 | tf_op jit(solution)/shard_map/ppermute | solution.py:251
  84.7 0.0 collective-permute-done.in_ref
  84.8 3.5 %collective-permute-done.1.rest_1_ = bf16[2,128,512]{2,1,0:T(8,128)(2,1)S(1)} collective-permute-done((bf16[2,128,512]{2,1,0:T(8,128)(2,1)S(1)}, bf16[2,128,512]{2,1,0:T(8,128)(2,1)S(1)}, u32[]{:S(2)}, u32[]{:S(2)}) %collective-permute-start.1) | collective-permute-done | bytes 262176 | tf_op jit(solution)/shard_map/ppermute | solution.py:251
  88.3 4.0 %collective-permute-done.2.rest_2_ = bf16[2,128,512]{2,1,0:T(8,128)(2,1)S(1)} collective-permute-done((bf16[2,128,512]{2,1,0:T(8,128)(2,1)S(1)}, bf16[2,128,512]{2,1,0:T(8,128)(2,1)S(1)}, u32[]{:S(2)}, u32[]{:S(2)}) %collective-permute-start.2) | collective-permute-done | bytes 262176 | tf_op jit(solution)/shard_map/ppermute | solution.py:251
  92.3 0.0 copy-done
  92.3 0.0 copy-done.1
  92.3 1.7 %stats.1 = (bf16[4,128,512]{2,1,0:T(8,128)(2,1)}, bf16[4,128,512]{2,1,0:T(8,128)(2,1)}) custom-call(s32[1,512]{1,0:T(1,128)S(1)} %copy-done.4, bf16[4,128,512]{2,1,0:T(8,128)(2,1)S(1)} %bitcast.20, bf16[4,128,512]{2,1,0:T(8,128)(2,1)S(1)} %bitcast.21, bf16[2,128,512]{2,1,0:T(8,128)(2,1)S(1)} %hold.1.rest_0_, ...), custom_call_target="tpu_custom_call" | custom-call | flops 2097152 | bytes 3145728 | tf_op jit(solution)/shard_map/stats/pallas_call | solution.py:377
  94.0 5.0 %all-to-all-done.2.in_ref = bf16[512,4,128]{2,1,0:T(4,128)(2,1)S(1)} async-done(((bf16[512,4,128]{2,1,0:T(4,128)(2,1)}), bf16[512,4,128]{2,1,0:T(4,128)(2,1)S(1)}, u32[]{:S(2)}, u32[]{:S(2)}) %all-to-all-start.2) | async-done | bytes 524320 | tf_op jit(solution)/shard_map/all_to_all | solution.py:360
  99.0 1.6 %collect.1 = bf16[224,4,128]{2,1,0:T(4,128)(2,1)} custom-call(s32[1,512]{1,0:T(1,128)S(1)} %copy-done.4, bf16[512,4,128]{2,1,0:T(4,128)(2,1)S(1)} %all-to-all-done.2.in_ref), custom_call_target="tpu_custom_call" | custom-call | bytes 458752 | tf_op jit(solution)/shard_map/collect/pallas_call | solution.py:398
  (1 shorter events, 0.0 us)
Async XLA Ops:
  3.9 5.0 %copy-start.2 = (bf16[1,4,128,512]{3,2,1,0:T(8,128)(2,1)S(1)}, bf16[1,4,128,512]{3,2,1,0:T(8,128)(2,1)}, u32[]{:S(2)}) copy-start(bf16[1,4,128,512]{3,2,1,0:T(8,128)(2,1)} %param.10) | copy-start | bytes 1572868
  4.0 5.0 %copy-start.3 = (bf16[1,4,512,128]{3,2,1,0:T(8,128)(2,1)S(1)}, bf16[1,4,512,128]{3,2,1,0:T(8,128)(2,1)}, u32[]{:S(2)}) copy-start(bf16[1,4,512,128]{3,2,1,0:T(8,128)(2,1)} %param.11) | copy-start | bytes 1572868
  4.0 14.0 %all-to-all-start = ((bf16[4,56,16,128]{3,2,1,0:T(8,128)(2,1)}), bf16[4,56,16,128]{3,2,1,0:T(8,128)(2,1)S(1)}, u32[]{:S(2)}, u32[]{:S(2)}) async-start(bf16[4,56,16,128]{3,2,1,0:T(8,128)(2,1)} %get-tuple-element.16), calls=%async_computation | async-start | bytes 1835008 | tf_op jit(solution)/shard_map/all_to_all | solution.py:296
  9.0 0.7 copy-start.4
  19.5 42.0 %all-to-all-start.1 = ((bf16[128,16,128]{2,1,0:T(8,128)(2,1)}), bf16[128,16,128]{2,1,0:T(8,128)(2,1)S(1)}, u32[]{:S(2)}, u32[]{:S(2)}) async-start(bf16[128,16,128]{2,1,0:T(8,128)(2,1)} %spread.1), calls=%async_computation.1 | async-start | bytes 1048576 | tf_op jit(solution)/shard_map/all_to_all | solution.py:330
  42.1 22.3 %collective-permute-start.3 = (bf16[8,128,128]{2,1,0:T(8,128)(2,1)S(1)}, bf16[8,128,128]{2,1,0:T(8,128)(2,1)S(1)}, u32[]{:S(2)}, u32[]{:S(2)}) collective-permute-start(bf16[8,128,128]{2,1,0:T(8,128)(2,1)S(1)} %get-tuple-element.22), channel_id=1, source_target_pairs={{0,256},{128,384},{256,0},{384,128},{1,257},{129,385},{257,1},{385... | collective-permute-start | bytes 786440 | tf_op jit(solution)/shard_map/ppermute | solution.py:251
  44.3 20.1 %collective-permute-start.4 = (bf16[8,128,128]{2,1,0:T(8,128)(2,1)S(1)}, bf16[8,128,128]{2,1,0:T(8,128)(2,1)S(1)}, u32[]{:S(2)}, u32[]{:S(2)}) collective-permute-start(bf16[8,128,128]{2,1,0:T(8,128)(2,1)S(1)} %get-tuple-element.23), channel_id=1, source_target_pairs={{0,128},{128,256},{256,384},{384,0},{1,129},{129,257},{257,385},{3... | collective-permute-start | bytes 786440 | tf_op jit(solution)/shard_map/ppermute | solution.py:251
  47.4 17.0 %collective-permute-start.5 = (bf16[8,128,128]{2,1,0:T(8,128)(2,1)S(1)}, bf16[8,128,128]{2,1,0:T(8,128)(2,1)S(1)}, u32[]{:S(2)}, u32[]{:S(2)}) collective-permute-start(bf16[8,128,128]{2,1,0:T(8,128)(2,1)S(1)} %get-tuple-element.24), channel_id=1, source_target_pairs={{0,384},{128,0},{256,128},{384,256},{1,385},{129,1},{257,129},{385... | collective-permute-start | bytes 786440 | tf_op jit(solution)/shard_map/ppermute | solution.py:251
  62.1 22.6 %collective-permute-start = (bf16[2,128,512]{2,1,0:T(8,128)(2,1)S(1)}, bf16[2,128,512]{2,1,0:T(8,128)(2,1)S(1)}, u32[]{:S(2)}, u32[]{:S(2)}) collective-permute-start(bf16[2,128,512]{2,1,0:T(8,128)(2,1)S(1)} %products.2.after_ref), channel_id=1, source_target_pairs={{0,256},{128,384},{256,0},{384,128},{1,257},{129,385},{257,1},{385... | collective-permute-start | bytes 786440 | tf_op jit(solution)/shard_map/ppermute | solution.py:251
  66.3 32.7 %all-to-all-start.2 = ((bf16[512,4,128]{2,1,0:T(4,128)(2,1)}), bf16[512,4,128]{2,1,0:T(4,128)(2,1)S(1)}, u32[]{:S(2)}, u32[]{:S(2)}) async-start(bf16[512,4,128]{2,1,0:T(4,128)(2,1)} %bitcast.14), calls=%async_computation.2 | async-start | bytes 1048576 | tf_op jit(solution)/shard_map/all_to_all | solution.py:360
  78.1 10.2 %collective-permute-start.1 = (bf16[2,128,512]{2,1,0:T(8,128)(2,1)S(1)}, bf16[2,128,512]{2,1,0:T(8,128)(2,1)S(1)}, u32[]{:S(2)}, u32[]{:S(2)}) collective-permute-start(bf16[2,128,512]{2,1,0:T(8,128)(2,1)S(1)} %get-tuple-element.17), channel_id=1, source_target_pairs={{0,128},{128,256},{256,384},{384,0},{1,129},{129,257},{257,385},{3... | collective-permute-start | bytes 786440 | tf_op jit(solution)/shard_map/ppermute | solution.py:251
  81.4 11.0 %copy-start = (bf16[1,4,128,512]{3,2,1,0:T(8,128)(2,1)S(1)}, bf16[1,4,128,512]{3,2,1,0:T(8,128)(2,1)}, u32[]{:S(2)}) copy-start(bf16[1,4,128,512]{3,2,1,0:T(8,128)(2,1)} %param.8) | copy-start | bytes 1572868
  81.4 11.0 %copy-start.1 = (bf16[1,4,128,512]{3,2,1,0:T(8,128)(2,1)S(1)}, bf16[1,4,128,512]{3,2,1,0:T(8,128)(2,1)}, u32[]{:S(2)}) copy-start(bf16[1,4,128,512]{3,2,1,0:T(8,128)(2,1)} %param.9) | copy-start | bytes 1572868
  81.4 10.9 %collective-permute-start.2 = (bf16[2,128,512]{2,1,0:T(8,128)(2,1)S(1)}, bf16[2,128,512]{2,1,0:T(8,128)(2,1)S(1)}, u32[]{:S(2)}, u32[]{:S(2)}) collective-permute-start(bf16[2,128,512]{2,1,0:T(8,128)(2,1)S(1)} %get-tuple-element.18), channel_id=1, source_target_pairs={{0,384},{128,0},{256,128},{384,256},{1,385},{129,1},{257,129},{385... | collective-permute-start | bytes 786440 | tf_op jit(solution)/shard_map/ppermute | solution.py:251

commit v7 on v5

--- a/solution.py
+++ b/solution.py
@@ -127,23 +127,29 @@
         store.wait()
 
 
-def spread_kernel(plan_ref, after_ref, in_ref, out_ref, spread, plan, sems, sem):
+def spread_kernel(plan_ref, after_ref, in_ref, out_ref, spread, sums, plan, sems, sem):
     del after_ref
     load = pltpu.make_async_copy(plan_ref.at[:, pl.ds(0, PLACES)], plan, sem)
     load.start()
     spread[...] = jnp.zeros_like(spread)
     classes, count = in_ref.shape[:2]
     first = lax.axis_index("rep") * count
-    load.wait()
 
     def add(j, _):
         total = in_ref[0, j].astype(F32)
         for r in range(1, classes):
             total = total + in_ref[r, j].astype(F32)
-        spread[plan[0, first + j]] = total.astype(spread.dtype)
+        sums[j] = total.astype(sums.dtype)
         return 0
 
     lax.fori_loop(0, count, add, 0, unroll=8)
+    load.wait()
+
+    def place(j, _):
+        spread[plan[0, first + j]] = sums[j]
+        return 0
+
+    lax.fori_loop(0, count, place, 0, unroll=8)
     parts = sems.shape[0]
     length = spread.shape[0] // parts
     stores = []
@@ -157,29 +163,25 @@
 
 def update_kernel(grad_ref, after_ref, *rest):
     del after_ref
-    factor_refs = rest[:-3]
-    out_ref, held, sems = rest[-3:]
+    factor_refs = rest[:-4]
+    out_ref, product, held, sems = rest[-4:]
     panels, width, _ = grad_ref.shape
     rows = width // panels
     replica = lax.axis_index("rep")
     sources = [lax.rem(replica + panels - d, panels) for d in OFFSETS]
     grad = jnp.concatenate([grad_ref[c] for c in range(panels)], axis=1)
-    right = jnp.concatenate(
-        [
-            jnp.concatenate([factor_ref[panels + h] for h in range(panels)], axis=0)
-            for factor_ref in factor_refs
-        ],
-        axis=1,
-    )
+    for d, factor_ref in enumerate(factor_refs):
+        left = jnp.concatenate([factor_ref[h] for h in range(panels)], axis=1)
+        product[d * rows : (d + 1) * rows] = jnp.dot(left, grad, preferred_element_type=F32).astype(BF16)
     stores = []
-    for i, factor_ref in enumerate(factor_refs):
-        left = jnp.concatenate([factor_ref[h] for h in range(panels)], axis=1)
-        product = jnp.dot(left, grad, preferred_element_type=F32).astype(BF16)
-        result = jnp.dot(product, right, preferred_element_type=F32).astype(BF16)
-        to = pl.ds(pl.multiple_of(sources[i] * rows, rows), rows)
+    for d, factor_ref in enumerate(factor_refs):
+        right = jnp.concatenate([factor_ref[panels + h] for h in range(panels)], axis=0)
+        result = jnp.dot(product[...], right, preferred_element_type=F32).astype(BF16)
         for e in range(panels):
-            held[i, e] = result[:, e * LANES : (e + 1) * LANES]
-            stores.append(pltpu.make_async_copy(held.at[i, e], out_ref.at[sources[e], to], sems.at[i, e]))
+            held[d, e] = result[e * rows : (e + 1) * rows]
+        for e in range(panels):
+            to = pl.ds(pl.multiple_of(sources[e] * rows, rows), rows)
+            stores.append(pltpu.make_async_copy(held.at[d, e], out_ref.at[sources[d], to], sems.at[d, e]))
             stores[-1].start()
     for store in stores:
         store.wait()
@@ -314,6 +316,7 @@
         out_specs=anywhere(),
         scratch_shapes=[
             VMEM((shards, TILE, LANES), BF16),
+            VMEM((count, TILE, LANES), BF16),
             SMEM((1, PLACES), jnp.int32),
             pltpu.SemaphoreType.DMA((4,)),
             pltpu.SemaphoreType.DMA,
@@ -344,6 +347,7 @@
         in_specs=[in_vmem(), anywhere()] + [in_vmem()] * classes,
         out_specs=anywhere(),
         scratch_shapes=[
+            VMEM((width, width), BF16),
             VMEM((panels, panels, quarter, LANES), BF16),
             pltpu.SemaphoreType.DMA((panels, panels)),
         ],

time: 101 us -> 101 us (level)
  no operation moved by 1% of the time
where the time goes in v7:
time: 101 us; the launch traced here: 100 us
  starting transfers between devices  55.5 us (55%)
  waiting for transfers between devices  30.5 us (30%)
  Pallas kernels  12.7 us (13%)
    all_to_all x1, starting transfers between devices, per_device(): lax.all_to_all(outgoing, 'shard', split_axis=0, concat_axis=0, tiled=True)  22.5 us
    ppermute x6, starting transfers between devices, to_others(): lax.ppermute(message, 'rep', [(s, (s + d) % count) for s in range(count)])  17.2 us
    all_to_all x1, waiting for transfers between devices, per_device(): lax.all_to_all(outgoing, 'shard', split_axis=0, concat_axis=0, tiled=True)  11 us
    all_to_all x1, starting transfers between devices, per_device(): lax.all_to_all(update_panels.reshape(panels * shards, rows, LANES), ('rep...  10.8 us
    ppermute x6, waiting for transfers between devices, to_others(): lax.ppermute(message, 'rep', [(s, (s + d) % count) for s in range(count)])  10.8 us
    all_to_all x1, waiting for transfers between devices, per_device(): lax.all_to_all(message, 'rep', split_axis=0, concat_axis=0, tiled=True)  6.83 us
    all_to_all x1, starting transfers between devices, per_device(): lax.all_to_all(message, 'rep', split_axis=0, concat_axis=0, tiled=True)  4.99 us
    pallas_call x1, Pallas kernels, per_device(): pl.pallas_call(pack_kernel, out_shape=(jax.ShapeDtypeStruct((classes, cou...  3.31 us
  transfers between devices with their start and end apart: 9, of which 5 were waited for; matrix products, arithmetic and copies ran while one was open for 0% of the time, Pallas kernels for 6%

profile of v7, /device:TPU:1, one launch (start us, length us, event | category | flops | bytes accessed | tf_op | source)
XLA Modules:
  0.0 100.4 jit_solution(2678737185150233952)
XLA Ops:
  0.6 3.3 %pack.1 = (bf16[4,56,16,128]{3,2,1,0:T(8,128)(2,1)}, s32[1,512]{1,0:T(1,128)}) custom-call(s32[1,224]{1,0:T(1,128)} %bitcast.26, bf16[224,16,128]{2,1,0:T(8,128)(2,1)} %bitcast.25), custom_call_target="tpu_custom_call" | custom-call | tf_op jit(solution)/shard_map/pack/pallas_call | solution.py:267
  3.9 0.0 copy-start.2
  4.0 0.0 copy-start.3
  4.0 5.0 %all-to-all-start = ((bf16[4,56,16,128]{3,2,1,0:T(8,128)(2,1)}), bf16[4,56,16,128]{3,2,1,0:T(8,128)(2,1)S(1)}, u32[]{:S(2)}, u32[]{:S(2)}) async-start(bf16[4,56,16,128]{3,2,1,0:T(8,128)(2,1)} %get-tuple-element.16), calls=%async_computation | async-start | bytes 1835008 | tf_op jit(solution)/shard_map/all_to_all | solution.py:292
  9.0 0.0 copy-start.4
  9.0 0.0 copy-done.2
  9.0 0.0 copy-done.3
  9.0 0.7 copy-done.4
  9.6 1.5 %factors.1 = (bf16[8,128,128]{2,1,0:T(8,128)(2,1)S(1)}, bf16[8,128,128]{2,1,0:T(8,128)(2,1)S(1)}, bf16[8,128,128]{2,1,0:T(8,128)(2,1)S(1)}, bf16[8,128,128]{2,1,0:T(8,128)(2,1)S(1)}) custom-call(s32[1,512]{1,0:T(1,128)S(1)} %copy-done.4, bf16[4,128,512]{2,1,0:T(8,128)(2,1)S(1)} %bitcast.22, bf16[4,4,128,128]{3,2,1,0:T(8,128)(2,1)S(1)} %bitcast.23), custom_call_target="tpu_custom_call" | custom-call | bytes 2097152 | tf_op jit(solution)/shard_map/factors/pallas_call | solution.py:293
  11.2 6.8 %all-to-all-done.in_ref = bf16[4,56,16,128]{3,2,1,0:T(8,128)(2,1)S(1)} async-done(((bf16[4,56,16,128]{3,2,1,0:T(8,128)(2,1)}), bf16[4,56,16,128]{3,2,1,0:T(8,128)(2,1)S(1)}, u32[]{:S(2)}, u32[]{:S(2)}) %all-to-all-start) | async-done | bytes 917536 | tf_op jit(solution)/shard_map/all_to_all | solution.py:292
  18.0 1.5 %spread.1 = bf16[128,16,128]{2,1,0:T(8,128)(2,1)} custom-call(s32[1,512]{1,0:T(1,128)S(1)} %copy-done.4, bf16[8,128,128]{2,1,0:T(8,128)(2,1)S(1)} %get-tuple-element.15.after_ref.rest_3_, bf16[4,56,16,128]{3,2,1,0:T(8,128)(2,1)S(1)} %all-to-all-done.in_ref), custom_call_target="tpu_custom_call" | custom-call | tf_op jit(solution)/shard_map/spread/pallas_call | solution.py:312
  19.5 22.5 %all-to-all-start.1 = ((bf16[128,16,128]{2,1,0:T(8,128)(2,1)}), bf16[128,16,128]{2,1,0:T(8,128)(2,1)S(1)}, u32[]{:S(2)}, u32[]{:S(2)}) async-start(bf16[128,16,128]{2,1,0:T(8,128)(2,1)} %spread.1), calls=%async_computation.1 | async-start | bytes 1048576 | tf_op jit(solution)/shard_map/all_to_all | solution.py:327
  42.0 2.2 %collective-permute-start.3 = (bf16[8,128,128]{2,1,0:T(8,128)(2,1)S(1)}, bf16[8,128,128]{2,1,0:T(8,128)(2,1)S(1)}, u32[]{:S(2)}, u32[]{:S(2)}) collective-permute-start(bf16[8,128,128]{2,1,0:T(8,128)(2,1)S(1)} %get-tuple-element.22), channel_id=1, source_target_pairs={{0,256},{128,384},{256,0},{384,128},{1,257},{129,385},{257,1},{385... | collective-permute-start | bytes 786440 | tf_op jit(solution)/shard_map/ppermute | solution.py:247
  44.2 4.3 %collective-permute-start.4 = (bf16[8,128,128]{2,1,0:T(8,128)(2,1)S(1)}, bf16[8,128,128]{2,1,0:T(8,128)(2,1)S(1)}, u32[]{:S(2)}, u32[]{:S(2)}) collective-permute-start(bf16[8,128,128]{2,1,0:T(8,128)(2,1)S(1)} %get-tuple-element.23), channel_id=1, source_target_pairs={{0,384},{128,0},{256,128},{384,256},{1,385},{129,1},{257,129},{385... | collective-permute-start | bytes 786440 | tf_op jit(solution)/shard_map/ppermute | solution.py:247
  48.5 1.9 %collective-permute-start.5 = (bf16[8,128,128]{2,1,0:T(8,128)(2,1)S(1)}, bf16[8,128,128]{2,1,0:T(8,128)(2,1)S(1)}, u32[]{:S(2)}, u32[]{:S(2)}) collective-permute-start(bf16[8,128,128]{2,1,0:T(8,128)(2,1)S(1)} %get-tuple-element.24), channel_id=1, source_target_pairs={{0,128},{128,256},{256,384},{384,0},{1,129},{129,257},{257,385},{3... | collective-permute-start | bytes 786440 | tf_op jit(solution)/shard_map/ppermute | solution.py:247
  50.5 11.0 %all-to-all-done.1 = bf16[128,16,128]{2,1,0:T(8,128)(2,1)S(1)} async-done(((bf16[128,16,128]{2,1,0:T(8,128)(2,1)}), bf16[128,16,128]{2,1,0:T(8,128)(2,1)S(1)}, u32[]{:S(2)}, u32[]{:S(2)}) %all-to-all-start.1) | async-done | bytes 524320 | tf_op jit(solution)/shard_map/all_to_all | solution.py:327
  61.5 0.2 copy.10
  61.7 0.4 products.2.after_ref
  62.1 2.2 %collective-permute-start = (bf16[2,128,512]{2,1,0:T(8,128)(2,1)S(1)}, bf16[2,128,512]{2,1,0:T(8,128)(2,1)S(1)}, u32[]{:S(2)}, u32[]{:S(2)}) collective-permute-start(bf16[2,128,512]{2,1,0:T(8,128)(2,1)S(1)} %products.2.after_ref), channel_id=1, source_target_pairs={{0,256},{128,384},{256,0},{384,128},{1,257},{129,385},{257,1},{385... | collective-permute-start | bytes 786440 | tf_op jit(solution)/shard_map/ppermute | solution.py:247
  64.3 0.0 collective-permute-done.3.rest_0_
  64.3 0.0 collective-permute-done.4.rest_1_
  64.3 0.0 collective-permute-done.5.rest_2_
  64.3 1.8 %update.1 = bf16[4,512,128]{2,1,0:T(8,128)(2,1)} custom-call(bf16[4,512,128]{2,1,0:T(8,128)(2,1)S(1)} %bitcast.18, bf16[2,128,512]{2,1,0:T(8,128)(2,1)S(1)} %products.2.after_ref, bf16[8,128,128]{2,1,0:T(8,128)(2,1)S(1)} %collective-permute-done.3.rest_0_, bf16[8,128,128]{2,1,0:T(8,128)(2,1)S(1)} %collective-permute-done.4.rest_1_, ...), custom_call_target="tpu_custom_call" | custom-call | flops 536870912 | bytes 2097152 | tf_op jit(solution)/shard_map/update/pallas_call | solution.py:344
  66.1 10.8 %all-to-all-start.2 = ((bf16[512,4,128]{2,1,0:T(4,128)(2,1)}), bf16[512,4,128]{2,1,0:T(4,128)(2,1)S(1)}, u32[]{:S(2)}, u32[]{:S(2)}) async-start(bf16[512,4,128]{2,1,0:T(4,128)(2,1)} %bitcast.14), calls=%async_computation.2 | async-start | bytes 1048576 | tf_op jit(solution)/shard_map/all_to_all | solution.py:358
  76.9 0.9 products.3
  77.8 4.5 %collective-permute-start.1 = (bf16[2,128,512]{2,1,0:T(8,128)(2,1)S(1)}, bf16[2,128,512]{2,1,0:T(8,128)(2,1)S(1)}, u32[]{:S(2)}, u32[]{:S(2)}) collective-permute-start(bf16[2,128,512]{2,1,0:T(8,128)(2,1)S(1)} %get-tuple-element.17), channel_id=1, source_target_pairs={{0,384},{128,0},{256,128},{384,256},{1,385},{129,1},{257,129},{385... | collective-permute-start | bytes 786440 | tf_op jit(solution)/shard_map/ppermute | solution.py:247
  82.3 0.0 copy-start
  82.4 0.0 copy-start.1
  82.4 2.1 %collective-permute-start.2 = (bf16[2,128,512]{2,1,0:T(8,128)(2,1)S(1)}, bf16[2,128,512]{2,1,0:T(8,128)(2,1)S(1)}, u32[]{:S(2)}, u32[]{:S(2)}) collective-permute-start(bf16[2,128,512]{2,1,0:T(8,128)(2,1)S(1)} %get-tuple-element.18), channel_id=1, source_target_pairs={{0,128},{128,256},{256,384},{384,0},{1,129},{129,257},{257,385},{3... | collective-permute-start | bytes 786440 | tf_op jit(solution)/shard_map/ppermute | solution.py:247
  84.4 0.0 collective-permute-done.in_ref
  84.5 5.8 %collective-permute-done.1.rest_1_ = bf16[2,128,512]{2,1,0:T(8,128)(2,1)S(1)} collective-permute-done((bf16[2,128,512]{2,1,0:T(8,128)(2,1)S(1)}, bf16[2,128,512]{2,1,0:T(8,128)(2,1)S(1)}, u32[]{:S(2)}, u32[]{:S(2)}) %collective-permute-start.1) | collective-permute-done | bytes 262176 | tf_op jit(solution)/shard_map/ppermute | solution.py:247
  90.3 4.9 %collective-permute-done.2.rest_2_ = bf16[2,128,512]{2,1,0:T(8,128)(2,1)S(1)} collective-permute-done((bf16[2,128,512]{2,1,0:T(8,128)(2,1)S(1)}, bf16[2,128,512]{2,1,0:T(8,128)(2,1)S(1)}, u32[]{:S(2)}, u32[]{:S(2)}) %collective-permute-start.2) | collective-permute-done | bytes 262176 | tf_op jit(solution)/shard_map/ppermute | solution.py:247
  95.2 0.0 copy-done
  95.2 0.0 copy-done.1
  95.2 1.7 %stats.1 = (bf16[4,128,512]{2,1,0:T(8,128)(2,1)}, bf16[4,128,512]{2,1,0:T(8,128)(2,1)}) custom-call(s32[1,512]{1,0:T(1,128)S(1)} %copy-done.4, bf16[4,128,512]{2,1,0:T(8,128)(2,1)S(1)} %bitcast.20, bf16[4,128,512]{2,1,0:T(8,128)(2,1)S(1)} %bitcast.21, bf16[2,128,512]{2,1,0:T(8,128)(2,1)S(1)} %hold.1.rest_0_, ...), custom_call_target="tpu_custom_call" | custom-call | flops 2097152 | bytes 3145728 | tf_op jit(solution)/shard_map/stats/pallas_call | solution.py:375
  96.9 1.9 %all-to-all-done.2.in_ref = bf16[512,4,128]{2,1,0:T(4,128)(2,1)S(1)} async-done(((bf16[512,4,128]{2,1,0:T(4,128)(2,1)}), bf16[512,4,128]{2,1,0:T(4,128)(2,1)S(1)}, u32[]{:S(2)}, u32[]{:S(2)}) %all-to-all-start.2) | async-done | bytes 524320 | tf_op jit(solution)/shard_map/all_to_all | solution.py:358
  98.8 1.6 %collect.1 = bf16[224,4,128]{2,1,0:T(4,128)(2,1)} custom-call(s32[1,512]{1,0:T(1,128)S(1)} %copy-done.4, bf16[512,4,128]{2,1,0:T(4,128)(2,1)S(1)} %all-to-all-done.2.in_ref), custom_call_target="tpu_custom_call" | custom-call | bytes 458752 | tf_op jit(solution)/shard_map/collect/pallas_call | solution.py:396
  (1 shorter events, 0.0 us)
Async XLA Ops:
  3.9 5.0 %copy-start.2 = (bf16[1,4,128,512]{3,2,1,0:T(8,128)(2,1)S(1)}, bf16[1,4,128,512]{3,2,1,0:T(8,128)(2,1)}, u32[]{:S(2)}) copy-start(bf16[1,4,128,512]{3,2,1,0:T(8,128)(2,1)} %param.10) | copy-start | bytes 1572868
  4.0 5.0 %copy-start.3 = (bf16[1,4,512,128]{3,2,1,0:T(8,128)(2,1)S(1)}, bf16[1,4,512,128]{3,2,1,0:T(8,128)(2,1)}, u32[]{:S(2)}) copy-start(bf16[1,4,512,128]{3,2,1,0:T(8,128)(2,1)} %param.11) | copy-start | bytes 1572868
  4.0 14.0 %all-to-all-start = ((bf16[4,56,16,128]{3,2,1,0:T(8,128)(2,1)}), bf16[4,56,16,128]{3,2,1,0:T(8,128)(2,1)S(1)}, u32[]{:S(2)}, u32[]{:S(2)}) async-start(bf16[4,56,16,128]{3,2,1,0:T(8,128)(2,1)} %get-tuple-element.16), calls=%async_computation | async-start | bytes 1835008 | tf_op jit(solution)/shard_map/all_to_all | solution.py:292
  9.0 0.7 copy-start.4
  19.5 42.0 %all-to-all-start.1 = ((bf16[128,16,128]{2,1,0:T(8,128)(2,1)}), bf16[128,16,128]{2,1,0:T(8,128)(2,1)S(1)}, u32[]{:S(2)}, u32[]{:S(2)}) async-start(bf16[128,16,128]{2,1,0:T(8,128)(2,1)} %spread.1), calls=%async_computation.1 | async-start | bytes 1048576 | tf_op jit(solution)/shard_map/all_to_all | solution.py:327
  42.0 22.2 %collective-permute-start.3 = (bf16[8,128,128]{2,1,0:T(8,128)(2,1)S(1)}, bf16[8,128,128]{2,1,0:T(8,128)(2,1)S(1)}, u32[]{:S(2)}, u32[]{:S(2)}) collective-permute-start(bf16[8,128,128]{2,1,0:T(8,128)(2,1)S(1)} %get-tuple-element.22), channel_id=1, source_target_pairs={{0,256},{128,384},{256,0},{384,128},{1,257},{129,385},{257,1},{385... | collective-permute-start | bytes 786440 | tf_op jit(solution)/shard_map/ppermute | solution.py:247
  44.2 20.1 %collective-permute-start.4 = (bf16[8,128,128]{2,1,0:T(8,128)(2,1)S(1)}, bf16[8,128,128]{2,1,0:T(8,128)(2,1)S(1)}, u32[]{:S(2)}, u32[]{:S(2)}) collective-permute-start(bf16[8,128,128]{2,1,0:T(8,128)(2,1)S(1)} %get-tuple-element.23), channel_id=1, source_target_pairs={{0,384},{128,0},{256,128},{384,256},{1,385},{129,1},{257,129},{385... | collective-permute-start | bytes 786440 | tf_op jit(solution)/shard_map/ppermute | solution.py:247
  48.5 15.8 %collective-permute-start.5 = (bf16[8,128,128]{2,1,0:T(8,128)(2,1)S(1)}, bf16[8,128,128]{2,1,0:T(8,128)(2,1)S(1)}, u32[]{:S(2)}, u32[]{:S(2)}) collective-permute-start(bf16[8,128,128]{2,1,0:T(8,128)(2,1)S(1)} %get-tuple-element.24), channel_id=1, source_target_pairs={{0,128},{128,256},{256,384},{384,0},{1,129},{129,257},{257,385},{3... | collective-permute-start | bytes 786440 | tf_op jit(solution)/shard_map/ppermute | solution.py:247
  62.1 22.4 %collective-permute-start = (bf16[2,128,512]{2,1,0:T(8,128)(2,1)S(1)}, bf16[2,128,512]{2,1,0:T(8,128)(2,1)S(1)}, u32[]{:S(2)}, u32[]{:S(2)}) collective-permute-start(bf16[2,128,512]{2,1,0:T(8,128)(2,1)S(1)} %products.2.after_ref), channel_id=1, source_target_pairs={{0,256},{128,384},{256,0},{384,128},{1,257},{129,385},{257,1},{385... | collective-permute-start | bytes 786440 | tf_op jit(solution)/shard_map/ppermute | solution.py:247
  66.1 32.7 %all-to-all-start.2 = ((bf16[512,4,128]{2,1,0:T(4,128)(2,1)}), bf16[512,4,128]{2,1,0:T(4,128)(2,1)S(1)}, u32[]{:S(2)}, u32[]{:S(2)}) async-start(bf16[512,4,128]{2,1,0:T(4,128)(2,1)} %bitcast.14), calls=%async_computation.2 | async-start | bytes 1048576 | tf_op jit(solution)/shard_map/all_to_all | solution.py:358
  77.8 12.5 %collective-permute-start.1 = (bf16[2,128,512]{2,1,0:T(8,128)(2,1)S(1)}, bf16[2,128,512]{2,1,0:T(8,128)(2,1)S(1)}, u32[]{:S(2)}, u32[]{:S(2)}) collective-permute-start(bf16[2,128,512]{2,1,0:T(8,128)(2,1)S(1)} %get-tuple-element.17), channel_id=1, source_target_pairs={{0,384},{128,0},{256,128},{384,256},{1,385},{129,1},{257,129},{385... | collective-permute-start | bytes 786440 | tf_op jit(solution)/shard_map/ppermute | solution.py:247
  82.3 12.9 %copy-start = (bf16[1,4,128,512]{3,2,1,0:T(8,128)(2,1)S(1)}, bf16[1,4,128,512]{3,2,1,0:T(8,128)(2,1)}, u32[]{:S(2)}) copy-start(bf16[1,4,128,512]{3,2,1,0:T(8,128)(2,1)} %param.8) | copy-start | bytes 1572868
  82.4 12.9 %copy-start.1 = (bf16[1,4,128,512]{3,2,1,0:T(8,128)(2,1)S(1)}, bf16[1,4,128,512]{3,2,1,0:T(8,128)(2,1)}, u32[]{:S(2)}) copy-start(bf16[1,4,128,512]{3,2,1,0:T(8,128)(2,1)} %param.9) | copy-start | bytes 1572868
  82.4 12.9 %collective-permute-start.2 = (bf16[2,128,512]{2,1,0:T(8,128)(2,1)S(1)}, bf16[2,128,512]{2,1,0:T(8,128)(2,1)S(1)}, u32[]{:S(2)}, u32[]{:S(2)}) collective-permute-start(bf16[2,128,512]{2,1,0:T(8,128)(2,1)S(1)} %get-tuple-element.18), channel_id=1, source_target_pairs={{0,128},{128,256},{256,384},{384,0},{1,129},{129,257},{257,385},{3... | collective-permute-start | bytes 786440 | tf_op jit(solution)/shard_map/ppermute | solution.py:247
